TPU v7x, 32 devices: a whole 2x2x4 slice. The times are simulated.
32 devices in a mesh: clip: 8 (over z, x), band: 4 (over y, core).
Axes of the slice: x: 2, y: 2, z: 4, core: 2. Of those that a mesh axis runs over, the one named last changes fastest.
Arguments:
- tokens: bfloat16 [8, 3072, 1024], P('clip', 'band'), may hold values from -6 to 6
- cotangent: bfloat16 [8, 3072, 1024], P('clip', 'band'), may hold values from -6 to 6
- frame_counts: int32 [8], P('clip'), may hold values from 6 to 12, as said below
- noise_levels: int32 [8, 12], P('clip'), may hold values from 0 to 999
- qkv_master: float32 [1024, 3072], P(('clip', 'band')), may hold values from -0.25 to 0.25
- out_master: float32 [1024, 1024], P(('clip', 'band')), may hold values from -0.375 to 0.375
- up_master: float32 [1024, 4096], P(('clip', 'band')), may hold values from -0.1875 to 0.1875
- down_master: float32 [4096, 1024], P(('clip', 'band')), may hold values from -0.09375 to 0.09375
- ada_master: float32 [1024, 6144], P(('clip', 'band')), may hold values from -0.1875 to 0.1875
- qkv_first: float32 [1024, 3072], P(('clip', 'band')), may hold values from -0.00036621094 to 0.00036621094
- out_first: float32 [1024, 1024], P(('clip', 'band')), may hold values from -0.00036621094 to 0.00036621094
- up_first: float32 [1024, 4096], P(('clip', 'band')), may hold values from -0.00036621094 to 0.00036621094
- down_first: float32 [4096, 1024], P(('clip', 'band')), may hold values from -0.00036621094 to 0.00036621094
- ada_first: float32 [1024, 6144], P(('clip', 'band')), may hold values from -0.00036621094 to 0.00036621094
- qkv_second: float32 [1024, 3072], P(('clip', 'band')), may hold values from 5.3511723e-10 to 2.140469e-09
- out_second: float32 [1024, 1024], P(('clip', 'band')), may hold values from 5.3511723e-10 to 2.140469e-09
- up_second: float32 [1024, 4096], P(('clip', 'band')), may hold values from 5.3511723e-10 to 2.140469e-09
- down_second: float32 [4096, 1024], P(('clip', 'band')), may hold values from 5.3511723e-10 to 2.140469e-09
- ada_second: float32 [1024, 6144], P(('clip', 'band')), may hold values from 5.3511723e-10 to 2.140469e-09
Outputs:
- activations: bfloat16 [8, 3072, 1024], P('clip', 'band')
- input_grad: float32 [8, 3072, 1024], P('clip', 'band')
- grad_norm: float32 [], replicated
- qkv_updated: float32 [1024, 3072], P(('clip', 'band'))
- qkv_first_new: float32 [1024, 3072], P(('clip', 'band'))
- qkv_second_new: float32 [1024, 3072], P(('clip', 'band'))
- out_updated: float32 [1024, 1024], P(('clip', 'band'))
- out_first_new: float32 [1024, 1024], P(('clip', 'band'))
- out_second_new: float32 [1024, 1024], P(('clip', 'band'))
- up_updated: float32 [1024, 4096], P(('clip', 'band'))
- up_first_new: float32 [1024, 4096], P(('clip', 'band'))
- up_second_new: float32 [1024, 4096], P(('clip', 'band'))
- down_updated: float32 [4096, 1024], P(('clip', 'band'))
- down_first_new: float32 [4096, 1024], P(('clip', 'band'))
- down_second_new: float32 [4096, 1024], P(('clip', 'band'))
- ada_updated: float32 [1024, 6144], P(('clip', 'band'))
- ada_first_new: float32 [1024, 6144], P(('clip', 'band'))
- ada_second_new: float32 [1024, 6144], P(('clip', 'band'))
Inputs may be any that keep to these rules, and one draw needn't show every extreme that they name: `frame_counts`: frames at or after a clip's count are padding and are never attended to as keys; some clip holds 12 frames and some other clip 12 // 2.
All inputs are finite; a program needn't handle non-finite values.
Results may differ from a plain program's by a relative error of at most 0.014.
The roundings to bfloat16 on the way count: a program that leaves them out, or rounds other values in their place, can miss the bound.
Values may be sent and summed in bfloat16 or wider, within the bound.
No kernel may reach another device: no remote copies, remote signals or barrier semaphores. Data moves between devices by JAX's collectives and lax.ppermute only.
A program may use at most 256 MiB of HBM per device.

v0:
```python
import math

import jax
import jax.numpy as jnp
from jax import lax
from jax.sharding import PartitionSpec as P

D = 1024
HEADS = 16
HEAD_DIM = 64
FRAMES = 12
STEP = 10


beta_first = 0.9
beta_second = 0.99
learn_rate = 0.03
weight_decay = 0.01
adam_epsilon = 1e-08
clip_limit = 1.0
norm_epsilon = 1e-06
masked_score = -1000000000.0


def contract_rows(left, right, precision=None):
    return lax.dot_general(
        left,
        right,
        (((0,), (0,)), ((), ())),
        precision=precision,
        preferred_element_type=jnp.float32,
    )


def contract_cols(left, right):
    return lax.dot_general(
        left, right, (((1,), (1,)), ((), ())), preferred_element_type=jnp.float32
    )


def normalize(values):
    average = jnp.mean(values, axis=-1, keepdims=True)
    centred = values - average
    variance = jnp.mean(centred * centred, axis=-1, keepdims=True)
    return centred * lax.rsqrt(variance + norm_epsilon)


def modulate(residual, shift, scale):
    return normalize(residual) * (1.0 + scale[:, None, :]) + shift[:, None, :]


def embed_levels(levels):
    halfway = D // 2
    spacing = jnp.exp(-math.log(10000.0) * jnp.arange(halfway, dtype=jnp.float32) / halfway)
    angles = levels.astype(jnp.float32)[..., None] * spacing
    return jax.nn.silu(jnp.concatenate([jnp.cos(angles), jnp.sin(angles)], axis=-1))


def attend(query_array, key_array, value_array, key_valid):
    row_count, head_count, head_size = query_array.shape
    blocks = row_count // row_count
    query_split = query_array.transpose(1, 0, 2).reshape(head_count, blocks, row_count, head_size)

    def one_head(pieces):
        query_head, key_head, value_head = pieces

        def one_block(query_part):
            scores = jnp.where(
                key_valid[None, :], contract_cols(query_part, key_head) * 0.125, masked_score
            )
            maxima = jnp.max(scores, axis=1, keepdims=True)
            exponent = jnp.exp(scores - maxima)
            totals = jnp.sum(exponent, axis=1, keepdims=True)
            probability = (exponent / totals).astype(jnp.bfloat16)
            outcome = jnp.dot(probability, value_head, preferred_element_type=jnp.float32)
            return (outcome.astype(jnp.bfloat16), (maxima + jnp.log(totals))[:, 0])

        return lax.map(one_block, query_head)

    outcome, log_totals = lax.map(
        one_head, (query_split, key_array.transpose(1, 0, 2), value_array.transpose(1, 0, 2))
    )
    outcome = outcome.reshape(head_count, row_count, head_size).transpose(1, 0, 2)
    return (outcome, log_totals)


def attend_back(query_array, key_array, value_array, log_totals, grad_attended, key_valid):
    row_count, head_count, head_size = query_array.shape
    blocks = row_count // row_count

    def to_blocks(tensor):
        return tensor.transpose(1, 0, 2).reshape(head_count, blocks, row_count, head_size)

    def one_head(pieces):
        query_head, key_head, value_head, logsum_head, grad_head = pieces

        def one_block(running, inputs):
            key_sum, value_sum = running
            query_part, logsum_part, grad_part = inputs
            scores = jnp.where(
                key_valid[None, :], contract_cols(query_part, key_head) * 0.125, masked_score
            )
            probability = jnp.exp(scores - logsum_part[:, None])
            grad_prob = contract_cols(grad_part, value_head)
            row_delta = jnp.sum(probability * grad_prob, axis=1, keepdims=True)
            grad_scores = (probability * (grad_prob - row_delta)).astype(jnp.bfloat16)
            grad_query = jnp.dot(grad_scores, key_head, preferred_element_type=jnp.float32) * 0.125
            key_sum = key_sum + contract_rows(grad_scores, query_part) * 0.125
            value_sum = value_sum + contract_rows(probability.astype(jnp.bfloat16), grad_part)
            return ((key_sum, value_sum), grad_query)

        zero_keys = jnp.zeros(key_head.shape, jnp.float32)
        (key_sum, value_sum), grad_query = lax.scan(
            one_block, (zero_keys, zero_keys), (query_head, logsum_head, grad_head)
        )
        return (grad_query, key_sum, value_sum)

    grad_query, grad_key, grad_value = lax.map(
        one_head,
        (
            to_blocks(query_array),
            key_array.transpose(1, 0, 2),
            value_array.transpose(1, 0, 2),
            log_totals,
            to_blocks(grad_attended),
        ),
    )
    grad_query = grad_query.reshape(head_count, row_count, head_size).transpose(1, 0, 2)
    return (grad_query, grad_key.transpose(1, 0, 2), grad_value.transpose(1, 0, 2))


def adam_step(master, clipped, first, second):
    first_new = beta_first * first + (1.0 - beta_first) * clipped
    second_new = beta_second * second + (1.0 - beta_second) * clipped * clipped
    first_hat = first_new / (1.0 - beta_first**STEP)
    second_hat = second_new / (1.0 - beta_second**STEP)
    updated = master - learn_rate * (
        first_hat / (jnp.sqrt(second_hat) + adam_epsilon) + weight_decay * master
    )
    return (updated, first_new, second_new)


def per_device(
    tokens,
    cotangent,
    frame_counts,
    noise_levels,
    qkv_master,
    out_master,
    up_master,
    down_master,
    ada_master,
    qkv_first,
    out_first,
    up_first,
    down_first,
    ada_first,
    qkv_second,
    out_second,
    up_second,
    down_second,
    ada_second,
):
    band_count = lax.axis_size("band")
    masters = (qkv_master, out_master, up_master, down_master, ada_master)
    firsts = (qkv_first, out_first, up_first, down_first, ada_first)
    seconds = (qkv_second, out_second, up_second, down_second, ada_second)
    w_qkv, w_out, w_up, w_down, w_ada = (
        lax.all_gather(qkv_master.astype(jnp.bfloat16), ("clip", "band"), axis=0, tiled=True),
        lax.all_gather(out_master.astype(jnp.bfloat16), ("clip", "band"), axis=0, tiled=True),
        lax.all_gather(up_master.astype(jnp.bfloat16), ("clip", "band"), axis=0, tiled=True),
        lax.all_gather(down_master.astype(jnp.bfloat16), ("clip", "band"), axis=0, tiled=True),
        lax.all_gather(ada_master.astype(jnp.bfloat16), ("clip", "band"), axis=0, tiled=True),
    )
    local_rows = tokens.shape[1]
    frame_rows = local_rows // FRAMES
    condition = embed_levels(noise_levels[0]).astype(jnp.bfloat16)
    modulation = jnp.dot(condition, w_ada, preferred_element_type=jnp.float32)
    shift_one, scale_one, gate_one, shift_two, scale_two, gate_two = jnp.split(
        modulation, 6, axis=1
    )
    residual = tokens[0].astype(jnp.float32).reshape(FRAMES, frame_rows, D)
    first_in = modulate(residual, shift_one, scale_one).astype(jnp.bfloat16).reshape(local_rows, D)
    projected = jnp.dot(first_in, w_qkv, preferred_element_type=jnp.float32).astype(jnp.bfloat16)
    query_array = projected[:, :D].reshape(local_rows, HEADS, HEAD_DIM)
    key_array = projected[:, D : 2 * D].reshape(local_rows, HEADS, HEAD_DIM)
    value_array = projected[:, 2 * D :].reshape(local_rows, HEADS, HEAD_DIM)
    local_valid = jnp.arange(local_rows, dtype=jnp.int32) // frame_rows < frame_counts[0]
    key_valid = jnp.tile(local_valid, band_count)
    all_keys, all_values = (
        lax.all_gather(key_array, "band", axis=0, tiled=True),
        lax.all_gather(value_array, "band", axis=0, tiled=True),
    )
    attended, row_logsum = attend(query_array, all_keys, all_values, key_valid)
    attended = attended.reshape(local_rows, D)
    branch_one = jnp.dot(attended, w_out, preferred_element_type=jnp.float32).reshape(
        FRAMES, frame_rows, D
    )
    middle = residual + gate_one[:, None, :] * branch_one
    second_in = modulate(middle, shift_two, scale_two).astype(jnp.bfloat16).reshape(local_rows, D)
    pre_act = jnp.dot(second_in, w_up, preferred_element_type=jnp.float32)
    hidden = jax.nn.gelu(pre_act, approximate=True).astype(jnp.bfloat16)
    branch_two = jnp.dot(hidden, w_down, preferred_element_type=jnp.float32).reshape(
        FRAMES, frame_rows, D
    )
    activations = (
        (middle + gate_two[:, None, :] * branch_two).astype(jnp.bfloat16).reshape(1, local_rows, D)
    )
    upstream = cotangent[0].astype(jnp.float32).reshape(FRAMES, frame_rows, D)
    grad_branch_two = (gate_two[:, None, :] * upstream).astype(jnp.bfloat16).reshape(local_rows, D)
    grad_gate_two = jnp.sum(upstream * branch_two, axis=1)
    grad_down = contract_rows(hidden, grad_branch_two)
    grad_hidden = contract_cols(grad_branch_two, w_down)
    _, gelu_pullback = jax.vjp(lambda inner: jax.nn.gelu(inner, approximate=True), pre_act)
    grad_pre = gelu_pullback(grad_hidden)[0].astype(jnp.bfloat16)
    grad_up = contract_rows(second_in, grad_pre)
    grad_second = contract_cols(grad_pre, w_up).reshape(FRAMES, frame_rows, D)
    _, second_pullback = jax.vjp(modulate, middle, shift_two, scale_two)
    middle_part, grad_shift_two, grad_scale_two = second_pullback(grad_second)
    grad_middle = upstream + middle_part
    grad_branch_one = (
        (gate_one[:, None, :] * grad_middle).astype(jnp.bfloat16).reshape(local_rows, D)
    )
    grad_gate_one = jnp.sum(grad_middle * branch_one, axis=1)
    grad_out = contract_rows(attended, grad_branch_one)
    grad_attended = (
        contract_cols(grad_branch_one, w_out)
        .astype(jnp.bfloat16)
        .reshape(local_rows, HEADS, HEAD_DIM)
    )
    query_grad, key_part, value_part = attend_back(
        query_array, all_keys, all_values, row_logsum, grad_attended, key_valid
    )
    key_grad, value_grad = (
        lax.psum_scatter(
            key_part.astype(jnp.bfloat16), "band", scatter_dimension=0, tiled=True
        ).astype(jnp.float32),
        lax.psum_scatter(
            value_part.astype(jnp.bfloat16), "band", scatter_dimension=0, tiled=True
        ).astype(jnp.float32),
    )
    grad_query = query_grad.astype(jnp.bfloat16)
    grad_key = key_grad.astype(jnp.bfloat16)
    grad_value = value_grad.astype(jnp.bfloat16)
    grad_projected = jnp.concatenate(
        [
            grad_query.reshape(local_rows, D),
            grad_key.reshape(local_rows, D),
            grad_value.reshape(local_rows, D),
        ],
        axis=1,
    )
    grad_qkv = contract_rows(first_in, grad_projected)
    grad_first = contract_cols(grad_projected, w_qkv).reshape(FRAMES, frame_rows, D)
    _, first_pullback = jax.vjp(modulate, residual, shift_one, scale_one)
    residual_part, grad_shift_one, grad_scale_one = first_pullback(grad_first)
    input_grad = (grad_middle + residual_part).reshape(1, local_rows, D)
    grad_modulation = jnp.concatenate(
        [
            grad_shift_one,
            grad_scale_one,
            grad_gate_one,
            grad_shift_two,
            grad_scale_two,
            grad_gate_two,
        ],
        axis=1,
    )
    grad_ada = contract_rows(
        condition.astype(jnp.float32), grad_modulation, precision=lax.Precision.HIGHEST
    )
    reduced = (
        lax.psum_scatter(grad_qkv, ("clip", "band"), scatter_dimension=0, tiled=True),
        lax.psum_scatter(grad_out, ("clip", "band"), scatter_dimension=0, tiled=True),
        lax.psum_scatter(grad_up, ("clip", "band"), scatter_dimension=0, tiled=True),
        lax.psum_scatter(grad_down, ("clip", "band"), scatter_dimension=0, tiled=True),
        lax.psum_scatter(grad_ada, ("clip", "band"), scatter_dimension=0, tiled=True),
    )
    local_squares = sum((jnp.sum(piece * piece) for piece in reduced))
    grad_norm = jnp.sqrt(lax.psum(local_squares, ("clip", "band")))
    factor = jnp.minimum(1.0, clip_limit / (grad_norm + 1e-06))
    results = []
    for master, gradient, first, second in zip(masters, reduced, firsts, seconds):
        results.extend(adam_step(master, gradient * factor, first, second))
    return (activations, input_grad, grad_norm, *results)


def solution(mesh):
    placed = (
        P("clip", "band", None),
        P("clip", "band", None),
        P("clip"),
        P("clip", None),
        P(("clip", "band"), None),
        P(("clip", "band"), None),
        P(("clip", "band"), None),
        P(("clip", "band"), None),
        P(("clip", "band"), None),
        P(("clip", "band"), None),
        P(("clip", "band"), None),
        P(("clip", "band"), None),
        P(("clip", "band"), None),
        P(("clip", "band"), None),
        P(("clip", "band"), None),
        P(("clip", "band"), None),
        P(("clip", "band"), None),
        P(("clip", "band"), None),
        P(("clip", "band"), None),
    )
    return jax.shard_map(
        per_device,
        mesh=mesh,
        in_specs=placed,
        out_specs=(
            P("clip", "band", None),
            P("clip", "band", None),
            P(),
            P(("clip", "band"), None),
            P(("clip", "band"), None),
            P(("clip", "band"), None),
            P(("clip", "band"), None),
            P(("clip", "band"), None),
            P(("clip", "band"), None),
            P(("clip", "band"), None),
            P(("clip", "band"), None),
            P(("clip", "band"), None),
            P(("clip", "band"), None),
            P(("clip", "band"), None),
            P(("clip", "band"), None),
            P(("clip", "band"), None),
            P(("clip", "band"), None),
            P(("clip", "band"), None),
        ),
        check_vma=False,
    )
```

profile of v0, /device:TPU:0, one launch (start us, length us, event | category | flops | bytes accessed | tf_op | source)
XLA Modules:
  0.0 2345.4 jit_solution(11601421993152868409)
XLA Ops:
  15.3 94.9 %all-gather.8.cloned.1.call-done = bf16[1024,6144]{1,0:T(8,128)(2,1)} async-done(((bf16[32,6144]{1,0:T(8,128)(2,1)}), bf16[1024,6144]{1,0:T(8,128)(2,1)}) %all-gather.8.cloned.1.call-update) | async-done | bytes 12582928 | tf_op jit(solution)/shard_map/all_gather | solution.py:173
  117.9 63.6 %all-gather.10.cloned.1.call-done = bf16[1024,3072]{1,0:T(8,128)(2,1)} async-done(((bf16[32,3072]{1,0:T(8,128)(2,1)}), bf16[1024,3072]{1,0:T(8,128)(2,1)}) %all-gather.10.cloned.1.call-update) | async-done | bytes 6291472 | tf_op jit(solution)/shard_map/all_gather | solution.py:169
  206.7 54.4 %all-gather.20.cloned.1.call-done = bf16[4096,1024]{1,0:T(8,128)(2,1)} async-done(((bf16[128,1024]{1,0:T(8,128)(2,1)}), bf16[4096,1024]{1,0:T(8,128)(2,1)}) %all-gather.20.cloned.1.call-update) | async-done | bytes 8388624 | tf_op jit(solution)/shard_map/all_gather | solution.py:172
  261.1 12.6 fusion.98
  273.7 34.4 %all-gather.12.cloned.1.call-done = bf16[3072,16,64]{0,2,1:T(8,128)(2,1)} async-done(((bf16[768,16,64]{0,2,1:T(8,128)(2,1)}), bf16[3072,16,64]{0,2,1:T(8,128)(2,1)}) %all-gather.12.cloned.1.call-update) | async-done | bytes 6291472 | tf_op jit(solution)/shard_map/all_gather | solution.py:191
  308.1 12.3 copy.46
  320.4 35.6 %all-gather.14.cloned.1.call-done = bf16[3072,16,64]{0,2,1:T(8,128)(2,1)} async-done(((bf16[768,16,64]{0,2,1:T(8,128)(2,1)}), bf16[3072,16,64]{0,2,1:T(8,128)(2,1)}) %all-gather.14.cloned.1.call-update) | async-done | bytes 6291472 | tf_op jit(solution)/shard_map/all_gather | solution.py:192
  355.9 12.0 copy.47
  367.9 146.7 %while.28 = (s32[]{:T(128)}, bf16[16,1,768,64]{2,3,1,0:T(8,128)(2,1)}, f32[16,1,768]{2,1,0:T(1,128)S(1)}, bf16[16,1,768,64]{3,2,1,0:T(8,128)(2,1)S(1)}, bf16[16,...) while((s32[]{:T(128)}, ...), condition=%wide.region_5.6_spmd.clone, body=%wide.region_2.5_spmd.clone.sunk | while | flops 632339712 | bytes 30232408 | solution.py:80
  533.6 20.6 fusion.59
  554.2 11.8 fusion.99
  570.6 11.1 fusion.88
  592.9 645.8 %while.29 = (s32[]{:T(128)}, bf16[16,1,768,64]{2,3,1,0:T(8,128)(2,1)}, bf16[16,3072,64]{1,2,0:T(8,128)(2,1)}, bf16[16,3072,64]{1,2,0:T(8,128)(2,1)}, bf16[16,1,7...) while((s32[]{:T(128)}, ...), condition=%wide.region_12.13_spmd.clone, body=%wide.region_10.12_spmd.clone.sunk | while | flops 1531428096 | bytes 89686944 | solution.py:118
  609.5 11.0 multiply_convert_fusion.9
  649.8 11.0 multiply_convert_fusion.9
  690.1 11.0 multiply_convert_fusion.9
  730.5 11.0 multiply_convert_fusion.9
  760.7 10.1 multiply_reduce_fusion.14
  770.8 11.0 multiply_convert_fusion.9
  811.2 11.0 multiply_convert_fusion.9
  841.4 10.1 multiply_reduce_fusion.14
  851.5 11.0 multiply_convert_fusion.9
  881.7 10.1 multiply_reduce_fusion.14
  891.8 11.0 multiply_convert_fusion.9
  932.2 11.0 multiply_convert_fusion.9
  962.4 10.1 multiply_reduce_fusion.14
  972.5 11.0 multiply_convert_fusion.9
  1012.9 11.0 multiply_convert_fusion.9
  1053.3 11.0 multiply_convert_fusion.9
  1083.6 10.1 multiply_reduce_fusion.14
  1093.7 11.0 multiply_convert_fusion.9
  1134.0 11.0 multiply_convert_fusion.9
  1164.3 10.1 multiply_reduce_fusion.14
  1174.4 11.0 multiply_convert_fusion.9
  1214.7 11.0 multiply_convert_fusion.9
  1246.1 51.3 %reduce-scatter.8.cloned.1.call-done = bf16[768,16,64]{0,2,1:T(8,128)(2,1)} async-done(((bf16[3072,16,64]{0,2,1:T(8,128)(2,1)}), bf16[768,16,64]{0,2,1:T(8,128)(2,1)}) %reduce-scatter.8.cloned.1.call-update) | async-done | bytes 1572880 | tf_op jit(solution)/shard_map/reduce_scatter | solution.py:235
  1297.5 61.1 %reduce-scatter.10.cloned.1.call-done = bf16[768,16,64]{0,2,1:T(8,128)(2,1)} async-done(((bf16[3072,16,64]{0,2,1:T(8,128)(2,1)}), bf16[768,16,64]{0,2,1:T(8,128)(2,1)}) %reduce-scatter.10.cloned.1.call-update) | async-done | bytes 1572880 | tf_op jit(solution)/shard_map/reduce_scatter | solution.py:238
  1358.6 11.5 fusion.69
  1371.5 13.1 fusion.101
  1385.9 14.7 fusion.87
  1401.5 10.6 bitcast_multiply_fusion
  1423.5 13.5 fusion.85
  1437.1 65.0 %reduce-scatter.14.cloned.1.call-done = f32[32,1024]{1,0:T(8,128)} async-done(((f32[1024,1024]{1,0:T(8,128)}), f32[32,1024]{1,0:T(8,128)}) %reduce-scatter.14.cloned.1.call-update) | async-done | bytes 131088 | tf_op jit(solution)/shard_map/reduce_scatter | solution.py:274
  1503.6 155.8 %reduce-scatter.12.cloned.1.call-done = f32[32,3072]{1,0:T(8,128)} async-done(((f32[1024,3072]{1,0:T(8,128)}), f32[32,3072]{1,0:T(8,128)}) %reduce-scatter.12.cloned.1.call-update) | async-done | bytes 393232 | tf_op jit(solution)/shard_map/reduce_scatter | solution.py:273
  1662.4 181.4 %reduce-scatter.16.cloned.1.call-done = f32[32,4096]{1,0:T(8,128)} async-done(((f32[1024,4096]{1,0:T(8,128)}), f32[32,4096]{1,0:T(8,128)}) %reduce-scatter.16.cloned.1.call-update) | async-done | bytes 524304 | tf_op jit(solution)/shard_map/reduce_scatter | solution.py:275
  1846.2 184.6 %reduce-scatter.18.cloned.1.call-done = f32[128,1024]{1,0:T(8,128)} async-done(((f32[4096,1024]{1,0:T(8,128)}), f32[128,1024]{1,0:T(8,128)}) %reduce-scatter.18.cloned.1.call-update) | async-done | bytes 524304 | tf_op jit(solution)/shard_map/reduce_scatter | solution.py:276
  2033.2 251.9 %reduce-scatter.20.cloned.1.call-done = f32[32,6144]{1,0:T(8,128)} async-done(((f32[1024,6144]{1,0:T(8,128)}), f32[32,6144]{1,0:T(8,128)}) %reduce-scatter.20.cloned.1.call-update) | async-done | bytes 786448 | tf_op jit(solution)/shard_map/reduce_scatter | solution.py:277
  2287.8 40.4 %psum.7 = f32[]{:T(128)} all-reduce(f32[]{:T(128)S(6)} %add.242), channel_id=1, replica_groups=mesh['clip'=8,'band'=4] {'clip','band'}, use_global_device_ids=true, to_apply=%region_33.34 | all-reduce | flops 1 | bytes 8 | tf_op jit(solution)/shard_map/psum | solution.py:280
  (533 shorter events, 668.9 us)
Async XLA Ops:
  7.2 103.0 %all-gather.8.cloned.1.call-start = ((), (), s32[]{:S(2)}) async-start(), calls=%async_computation.7 | async-start | bytes 12976128 | tf_op jit(solution)/shard_map/all_gather | solution.py:173
  9.3 172.3 %all-gather.10.cloned.1.call-start = ((), (), s32[]{:S(2)}) async-start(), calls=%async_computation.8 | async-start | bytes 6488064 | tf_op jit(solution)/shard_map/all_gather | solution.py:169
  11.1 250.0 %all-gather.20.cloned.1.call-start = ((), (), s32[]{:S(2)}) async-start(), calls=%async_computation.13 | async-start | bytes 8650752 | tf_op jit(solution)/shard_map/all_gather | solution.py:172
  12.9 295.2 %all-gather.12.cloned.1.call-start = ((), (), s32[]{:S(2)}) async-start(), calls=%async_computation.9 | async-start | bytes 7864320 | tf_op jit(solution)/shard_map/all_gather | solution.py:191
  13.3 103.9 %copy-start.47 = (f32[768]{0:T(1024)}, f32[768]{0:T(1024)S(1)}, u32[]{:S(2)}) copy-start(f32[768]{0:T(1024)S(1)} %broadcast_multiply_fusion.1) | copy-start | bytes 9220
  15.1 102.2 %copy-start.51 = (f32[768]{0:T(1024)}, f32[768]{0:T(1024)S(1)}, u32[]{:S(2)}) copy-start(f32[768]{0:T(1024)S(1)} %get-tuple-element.302) | copy-start | bytes 9220
  15.3 101.3 %copy-start.38 = (f32[12,512]{1,0:T(8,128)}, f32[12,512]{1,0:T(8,128)S(1)}, u32[]{:S(2)}) copy-start(f32[12,512]{1,0:T(8,128)S(1)} %get-tuple-element.303) | copy-start | bytes 73732
  15.3 101.3 %copy-start.40 = (f32[12,512]{1,0:T(8,128)}, f32[12,512]{1,0:T(8,128)S(1)}, u32[]{:S(2)}) copy-start(f32[12,512]{1,0:T(8,128)S(1)} %get-tuple-element.304) | copy-start | bytes 73732
  117.3 72.3 %copy-start.25 = (f32[12,1024]{1,0:T(8,128)}, f32[12,1024]{1,0:T(8,128)S(1)}, u32[]{:S(2)}) copy-start(f32[12,1024]{1,0:T(8,128)S(1)} %get-tuple-element.297) | copy-start | bytes 147460
  117.3 86.4 %copy-start.27 = (f32[12,1024]{1,0:T(8,128)}, f32[12,1024]{1,0:T(8,128)S(1)}, u32[]{:S(2)}) copy-start(f32[12,1024]{1,0:T(8,128)S(1)} %get-tuple-element.293) | copy-start | bytes 147460
  117.9 63.6 %copy-start.16 = (bf16[768,1024]{1,0:T(8,128)(2,1)}, bf16[768,1024]{1,0:T(8,128)(2,1)S(1)}, u32[]{:S(2)}) copy-start(bf16[768,1024]{1,0:T(8,128)(2,1)S(1)} %fusion.64) | copy-start | bytes 4718596
  193.9 162.0 %all-gather.14.cloned.1.call-start = ((), (), s32[]{:S(2)}) async-start(), calls=%async_computation.10 | async-start | bytes 7864320 | tf_op jit(solution)/shard_map/all_gather | solution.py:192
  195.5 328.2 %all-gather.16.cloned.1.call-start = ((), (), s32[]{:S(2)}) async-start(), calls=%async_computation.11 | async-start | bytes 2162688 | tf_op jit(solution)/shard_map/all_gather | solution.py:170
  196.3 337.3 %all-gather.18.cloned.1.call-start = ((), (), s32[]{:S(2)}) async-start(), calls=%async_computation.12 | async-start | bytes 8650752 | tf_op jit(solution)/shard_map/all_gather | solution.py:171
  198.1 1099.4 %reduce-scatter.8.cloned.1.call-start = ((), (), s32[]{:S(2)}) async-start(), calls=%async_computation.14 | async-start | bytes 7864320 | tf_op jit(solution)/shard_map/reduce_scatter | solution.py:235
  554.2 11.8 copy-start.7
  570.6 11.1 copy-start.8
  620.5 9.6 slice-start
  660.8 9.6 slice-start
  701.1 9.7 slice-start
  741.5 9.6 slice-start
  781.8 9.7 slice-start
  822.2 9.7 slice-start
  862.6 9.6 slice-start
  902.9 9.7 slice-start
  943.2 9.7 slice-start
  983.6 9.7 slice-start
  1024.0 9.7 slice-start
  1064.3 9.7 slice-start
  1104.7 9.7 slice-start
  1145.0 9.7 slice-start
  1185.4 9.6 slice-start
  1225.7 9.7 slice-start
  1238.8 119.8 %reduce-scatter.10.cloned.1.call-start = ((), (), s32[]{:S(2)}) async-start(), calls=%async_computation.15 | async-start | bytes 7864320 | tf_op jit(solution)/shard_map/reduce_scatter | solution.py:238
  1239.5 262.5 %reduce-scatter.14.cloned.1.call-start = ((), (), s32[]{:S(2)}) async-start(), calls=%async_computation.17 | async-start | bytes 4325376 | tf_op jit(solution)/shard_map/reduce_scatter | solution.py:274
  1245.8 112.7 %copy-start.17 = (bf16[768,1024]{1,0:T(8,128)(2,1)S(1)}, bf16[768,1024]{1,0:T(8,128)(2,1)}, u32[]{:S(2)}) copy-start(bf16[768,1024]{1,0:T(8,128)(2,1)} %copy-done.16) | copy-start | bytes 4718596
  1245.8 112.7 %copy-start.56 = (bf16[16,1,768,64]{2,3,1,0:T(8,128)(2,1)S(1)}, bf16[16,1,768,64]{2,3,1,0:T(8,128)(2,1)}, u32[]{:S(2)}) copy-start(bf16[16,1,768,64]{2,3,1,0:T(8,128)(2,1)} %get-tuple-element.163) | copy-start | bytes 4718596
  1245.9 413.5 %reduce-scatter.12.cloned.1.call-start = ((), (), s32[]{:S(2)}) async-start(), calls=%async_computation.16 | async-start | bytes 12976128 | tf_op jit(solution)/shard_map/reduce_scatter | solution.py:273
  1370.1 473.7 %reduce-scatter.16.cloned.1.call-start = ((), (), s32[]{:S(2)}) async-start(), calls=%async_computation.18 | async-start | bytes 17301504 | tf_op jit(solution)/shard_map/reduce_scatter | solution.py:275
  1384.5 646.2 %reduce-scatter.18.cloned.1.call-start = ((), (), s32[]{:S(2)}) async-start(), calls=%async_computation.19 | async-start | bytes 17301504 | tf_op jit(solution)/shard_map/reduce_scatter | solution.py:276
  1400.7 884.5 %reduce-scatter.20.cloned.1.call-start = ((), (), s32[]{:S(2)}) async-start(), calls=%async_computation.20 | async-start | bytes 25952256 | tf_op jit(solution)/shard_map/reduce_scatter | solution.py:277
  1401.5 12.3 copy-start.1
  1417.4 6.1 copy-start.39
  1437.0 891.8 %copy-start.9 = (f32[32,6144]{1,0:T(8,128)S(1)}, f32[32,6144]{1,0:T(8,128)}, u32[]{:S(2)}) copy-start(f32[32,6144]{1,0:T(8,128)} %param.31) | copy-start | bytes 2359300
  1437.0 891.8 %copy-start.23 = (f32[32,6144]{1,0:T(8,128)S(1)}, f32[32,6144]{1,0:T(8,128)}, u32[]{:S(2)}) copy-start(f32[32,6144]{1,0:T(8,128)} %param.36) | copy-start | bytes 2359300
  1437.0 891.8 %copy-start.24 = (f32[32,6144]{1,0:T(8,128)S(1)}, f32[32,6144]{1,0:T(8,128)}, u32[]{:S(2)}) copy-start(f32[32,6144]{1,0:T(8,128)} %param.41) | copy-start | bytes 2359300
  2033.2 298.7 %copy-start.11 = (f32[128,1024]{1,0:T(8,128)S(1)}, f32[128,1024]{1,0:T(8,128)}, u32[]{:S(2)}) copy-start(f32[128,1024]{1,0:T(8,128)} %param.30) | copy-start | bytes 1572868
  2033.2 298.7 %copy-start.14 = (f32[128,1024]{1,0:T(8,128)S(1)}, f32[128,1024]{1,0:T(8,128)}, u32[]{:S(2)}) copy-start(f32[128,1024]{1,0:T(8,128)} %reduce-scatter.18.cloned.1.call-done) | copy-start | bytes 1572868
  (57 other events, 198.6 us)
Sparse Core Ops, SparseCore 0:
  11.5 98.6 all-gather.7
  113.7 67.8 all-gather.9
  185.0 76.0 all-gather.19
  263.1 44.9 all-gather.11
  309.5 46.3 all-gather.13
  359.2 56.3 all-gather.15
  419.1 76.5 all-gather.17
  1238.9 58.5 reduce-scatter.7
  1300.2 58.3 reduce-scatter.9
  1360.7 141.2 reduce-scatter.13
  1508.1 151.2 reduce-scatter.11
  1661.7 182.0 reduce-scatter.15
  1846.2 184.5 reduce-scatter.17
  2038.2 246.9 reduce-scatter.19
where the time goes:
time: 2360 us; the launch traced here: 2350 us
  waiting for transfers between devices  1230 us (52%)
  matrix products  729 us (31%)
  other arithmetic  260 us (11%)
  local copies, waits for them, and re-layouts  58.5 us (2%)
  blocking collectives  40.4 us (2%)
    dot_general x52, matrix products, contract_cols(): lax.dot_general(left, right, (((1,), (1,)), ((), ())), preferred_element_...  341 us
    reduce_scatter x1, waiting for transfers between devices, per_device(): lax.psum_scatter(grad_ada, ('clip', 'band'), scatter_dimension=0, tiled=T...  252 us
    dot_general x37, matrix products, contract_rows(): lax.dot_general(left, right, (((0,), (0,)), ((), ())), precision=precisio...  213 us
    reduce_scatter x1, waiting for transfers between devices, per_device(): lax.psum_scatter(grad_down, ('clip', 'band'), scatter_dimension=0, tiled=...  185 us
    reduce_scatter x1, waiting for transfers between devices, per_device(): lax.psum_scatter(grad_up, ('clip', 'band'), scatter_dimension=0, tiled=True)  181 us
    convert_element_type x16, other arithmetic, one_block(): grad_scores = (probability * (grad_prob - row_delta)).astype(jnp.bfloat16)  177 us
    reduce_scatter x1, waiting for transfers between devices, per_device(): lax.psum_scatter(grad_qkv, ('clip', 'band'), scatter_dimension=0, tiled=T...  156 us
    all_gather x1, waiting for transfers between devices, per_device(): lax.all_gather(ada_master.astype(jnp.bfloat16), ('clip', 'band'), axis=0,...  94.9 us
  transfers between devices with their start and end apart: 14, of which 12 were waited for; matrix products, arithmetic and copies ran while one was open for 14% of the time, Pallas kernels for 0%

commit v1 on v0

v1 whole, which is shorter than its diff:
```python
import math

import jax
import jax.numpy as jnp
from jax import lax
from jax.sharding import Mesh, PartitionSpec as P

D = 1024
HEADS = 16
HEAD_DIM = 64
FF = 4096
FRAMES = 12
STEP = 10
BANDS = 4
OWN_COLS = D // BANDS
LANES = 128

beta_first = 0.9
beta_second = 0.99
learn_rate = 0.03
weight_decay = 0.01
adam_epsilon = 1e-08
clip_limit = 1.0
norm_epsilon = 1e-06
masked_score = -1000000000.0


def contract_rows(left, right, precision=None):
    return lax.dot_general(
        left,
        right,
        (((0,), (0,)), ((), ())),
        precision=precision,
        preferred_element_type=jnp.float32,
    )


def contract_cols(left, right):
    return lax.dot_general(
        left, right, (((1,), (1,)), ((), ())), preferred_element_type=jnp.float32
    )


def normalize(values):
    average = jnp.mean(values, axis=-1, keepdims=True)
    centred = values - average
    variance = jnp.mean(centred * centred, axis=-1, keepdims=True)
    return centred * lax.rsqrt(variance + norm_epsilon)


def modulate(residual, shift, scale):
    return normalize(residual) * (1.0 + scale[:, None, :]) + shift[:, None, :]


def to_half(tensor):
    return lax.ppermute(tensor, "half", [(0, 1), (1, 0)])


def to_pair(tensor):
    return lax.ppermute(tensor, "pair", [(0, 1), (1, 0)])


def to_both(tensor):
    return lax.ppermute(tensor, ("pair", "half"), [(0, 3), (1, 2), (2, 1), (3, 0)])


def band_sum(tensor):
    tensor = tensor + to_half(tensor)
    return tensor + to_pair(tensor)


def relative_order(blocks, pair, half):
    rest = blocks.shape[1:]
    blocks = blocks.reshape((2, 2) + rest)
    blocks = jnp.where(half == 1, blocks[:, ::-1], blocks)
    blocks = jnp.where(pair == 1, blocks[::-1], blocks)
    return blocks.reshape((BANDS,) + rest)


def heads_of(blocks):
    count, rows, _ = blocks.shape
    return blocks.reshape(count, rows, 2, HEAD_DIM).transpose(0, 2, 1, 3).reshape(-1, rows, HEAD_DIM)


def blocks_of(heads):
    count, rows, _ = heads.shape
    return heads.reshape(-1, 2, rows, HEAD_DIM).transpose(0, 2, 1, 3).reshape(-1, rows, LANES)


def valid_keys(count, rows, local_rows):
    return jnp.arange(rows, dtype=jnp.int32) % local_rows // (local_rows // FRAMES) < count[0]


def attend(count, projected, local_rows):
    rows = projected.shape[1]
    key_valid = valid_keys(count, rows, local_rows)
    heads = heads_of(projected).reshape(3, BANDS, rows, HEAD_DIM)

    def one_head(pieces):
        query, key, value = pieces

        def one_block(query_part):
            scores = jnp.where(
                key_valid[None, :], contract_cols(query_part, key) * 0.125, masked_score
            )
            maxima = jnp.max(scores, axis=1, keepdims=True)
            exponent = jnp.exp(scores - maxima)
            totals = jnp.sum(exponent, axis=1, keepdims=True)
            outcome = jnp.dot(
                exponent.astype(jnp.bfloat16), value, preferred_element_type=jnp.float32
            )
            return outcome / totals, (maxima + jnp.log(totals))[:, 0]

        outcome, logs = lax.map(one_block, query.reshape(BANDS, local_rows, HEAD_DIM))
        return outcome.reshape(rows, HEAD_DIM), logs

    outcome, logs = lax.map(one_head, (heads[0], heads[1], heads[2]))
    return blocks_of(outcome.astype(jnp.bfloat16)), (outcome, logs)


def attend_back(count, projected, grad_attended, raw, local_rows):
    rows = projected.shape[1]
    key_valid = valid_keys(count, rows, local_rows)
    heads = heads_of(projected).reshape(3, BANDS, rows, HEAD_DIM)
    outcome, logs = raw
    grads = heads_of(grad_attended)
    deltas = jnp.sum(outcome * grads.astype(jnp.float32), axis=-1).reshape(logs.shape)

    def one_head(pieces):
        query, key, value, log_head, delta_head, grad = pieces

        def one_block(running, inputs):
            key_sum, value_sum = running
            query_part, log_part, delta_part, grad_part = inputs
            scores = jnp.where(
                key_valid[None, :], contract_cols(query_part, key) * 0.125, masked_score
            )
            probability = jnp.exp(scores - log_part[:, None])
            grad_prob = contract_cols(grad_part, value)
            grad_scores = (probability * (grad_prob - delta_part[:, None])).astype(jnp.bfloat16)
            grad_query = jnp.dot(grad_scores, key, preferred_element_type=jnp.float32) * 0.125
            key_sum = key_sum + contract_rows(grad_scores, query_part) * 0.125
            value_sum = value_sum + contract_rows(probability.astype(jnp.bfloat16), grad_part)
            return (key_sum, value_sum), grad_query.astype(jnp.bfloat16)

        zero = jnp.zeros((rows, HEAD_DIM), jnp.float32)
        split = (BANDS, local_rows, HEAD_DIM)
        (key_sum, value_sum), grad_query = lax.scan(
            one_block, (zero, zero), (query.reshape(split), log_head, delta_head, grad.reshape(split))
        )
        return (
            grad_query.reshape(rows, HEAD_DIM),
            key_sum.astype(jnp.bfloat16),
            value_sum.astype(jnp.bfloat16),
        )

    results = lax.map(one_head, (*heads, logs, deltas, grads))
    return tuple(blocks_of(result) for result in results)


def to_columns(blocks):
    return blocks.transpose(1, 0, 2).reshape(blocks.shape[1], -1)


def to_blocks(tensor):
    return tensor.reshape(tensor.shape[0], -1, LANES).transpose(1, 0, 2)


def adam_step(master, clipped, first, second):
    first_new = beta_first * first + (1.0 - beta_first) * clipped
    second_new = beta_second * second + (1.0 - beta_second) * clipped * clipped
    first_hat = first_new / (1.0 - beta_first**STEP)
    second_hat = second_new / (1.0 - beta_second**STEP)
    updated = master - learn_rate * (
        first_hat / (jnp.sqrt(second_hat) + adam_epsilon) + weight_decay * master
    )
    return (updated, first_new, second_new)


def per_device(
    tokens,
    cotangent,
    frame_counts,
    noise_levels,
    qkv_master,
    out_master,
    up_master,
    down_master,
    ada_master,
    qkv_first,
    out_first,
    up_first,
    down_first,
    ada_first,
    qkv_second,
    out_second,
    up_second,
    down_second,
    ada_second,
):
    clips = lax.axis_size("clip")
    clip, pair, half = lax.axis_index("clip"), lax.axis_index("pair"), lax.axis_index("half")
    everywhere = ("clip", "pair", "half")
    masters = (qkv_master, out_master, up_master, down_master, ada_master)
    firsts = (qkv_first, out_first, up_first, down_first, ada_first)
    seconds = (qkv_second, out_second, up_second, down_second, ada_second)
    local_rows = tokens.shape[1]
    frame_rows = local_rows // FRAMES
    own_rows = qkv_master.shape[0]
    up_groups = FF // (2 * LANES)

    own_tokens = tokens[0]
    half_tokens = to_half(own_tokens)
    pair_tokens = to_pair(own_tokens)
    clip_tokens = jnp.stack([own_tokens, half_tokens, pair_tokens, to_half(pair_tokens)])

    condition = embed_levels(noise_levels[0]).astype(jnp.bfloat16)
    conditions = lax.all_gather(condition.reshape(-1, LANES), "clip", tiled=True)
    device = (clip * 2 + pair) * 2 + half
    condition = lax.dynamic_slice_in_dim(
        conditions.reshape(clips * FRAMES, D), device * own_rows, own_rows, axis=1
    )
    part = jnp.dot(condition, ada_master.astype(jnp.bfloat16), preferred_element_type=jnp.float32)
    part = part.reshape(clips, FRAMES, 6, D).transpose(0, 2, 1, 3)
    modulation = lax.psum_scatter(
        part.reshape(clips * 6 * FRAMES, D), "clip", scatter_dimension=0, tiled=True
    )
    modulation = band_sum(modulation)
    shift_one, scale_one, gate_one, shift_two, scale_two, gate_two = modulation.reshape(
        6, FRAMES, D
    )

    w_qkv = qkv_master.astype(jnp.bfloat16).reshape(own_rows, 3, BANDS, OWN_COLS)
    w_qkv = lax.all_to_all(w_qkv.transpose(2, 0, 1, 3), ("pair", "half"), 0, 0)
    w_qkv = lax.all_gather(w_qkv.reshape(BANDS * own_rows, 3 * OWN_COLS), "clip", tiled=True)

    up_low = up_master.astype(jnp.bfloat16).reshape(own_rows, up_groups, 2, LANES)
    mine = jnp.where(half == 0, up_low[:, :, 0], up_low[:, :, 1])
    other = to_half(jnp.where(half == 0, up_low[:, :, 1], up_low[:, :, 0]))
    up_low = jnp.where(half == 0, jnp.stack([mine, other]), jnp.stack([other, mine]))
    up_low = up_low.reshape(2 * own_rows, FF // 2)
    w_up = lax.all_gather(up_low, ("clip", "pair"), tiled=True)
    w_down = lax.all_gather(down_master.astype(jnp.bfloat16), ("clip", "pair"), tiled=True)
    w_out = lax.all_gather(out_master.astype(jnp.bfloat16), everywhere, tiled=True)
    w_out = relative_order(w_out.reshape(BANDS, OWN_COLS, D), pair, half).reshape(D, D)

    wide = clip_tokens.astype(jnp.float32).reshape(BANDS, FRAMES, frame_rows, D)
    normed = normalize(wide)
    first_in = normed * (1.0 + scale_one[None, :, None, :]) + shift_one[None, :, None, :]
    first_in = first_in.astype(jnp.bfloat16).reshape(BANDS * local_rows, D)
    projected = jnp.dot(first_in, w_qkv, preferred_element_type=jnp.float32).astype(jnp.bfloat16)
    projected = to_blocks(projected)
    attended, raw = attend(frame_counts, projected, local_rows)
    attended = attended.reshape(-1, BANDS, local_rows, LANES)
    attended = [attended[:, place] for place in range(BANDS)]
    attended = to_columns(
        jnp.concatenate(
            [attended[0], to_half(attended[1]), to_pair(attended[2]), to_both(attended[3])]
        )
    )

    residual = own_tokens.astype(jnp.float32).reshape(FRAMES, frame_rows, D)
    branch_one = jnp.dot(attended, w_out, preferred_element_type=jnp.float32).reshape(
        FRAMES, frame_rows, D
    )
    middle = residual + gate_one[:, None, :] * branch_one
    second_in = modulate(middle, shift_two, scale_two).astype(jnp.bfloat16).reshape(local_rows, D)
    upstream = cotangent[0].astype(jnp.float32).reshape(FRAMES, frame_rows, D)
    grad_branch_two = (gate_two[:, None, :] * upstream).astype(jnp.bfloat16).reshape(local_rows, D)
    second_both = jnp.concatenate([second_in, to_half(second_in)])
    grad_branch_both = jnp.concatenate([grad_branch_two, to_half(grad_branch_two)])

    pre_act = jnp.dot(second_both, w_up, preferred_element_type=jnp.float32)
    hidden, gelu_pullback = jax.vjp(lambda inner: jax.nn.gelu(inner, approximate=True), pre_act)
    hidden = hidden.astype(jnp.bfloat16)
    grad_hidden = contract_cols(grad_branch_both, w_down)
    grad_pre = gelu_pullback(grad_hidden)[0].astype(jnp.bfloat16)
    grad_second = contract_cols(grad_pre, w_up)
    grad_second = grad_second[:local_rows] + to_half(
        grad_second[local_rows:].astype(jnp.bfloat16)
    ).astype(jnp.float32)
    grad_second = grad_second.reshape(FRAMES, frame_rows, D)
    _, second_pullback = jax.vjp(modulate, middle, shift_two, scale_two)
    middle_part, grad_shift_two, grad_scale_two = second_pullback(grad_second)
    grad_middle = upstream + middle_part
    grad_branch_one = (
        (gate_one[:, None, :] * grad_middle).astype(jnp.bfloat16).reshape(local_rows, D)
    )
    grad_gate_one = jnp.sum(grad_middle * branch_one, axis=1)
    grad_attended = contract_cols(grad_branch_one, w_out).astype(jnp.bfloat16)
    pieces = to_blocks(grad_attended).reshape(BANDS, -1, local_rows, LANES)
    grad_attended = jnp.concatenate(
        [pieces[0], to_half(pieces[1]), to_pair(pieces[2]), to_both(pieces[3])], axis=1
    )

    branch_two = jnp.dot(hidden, w_down, preferred_element_type=jnp.float32)
    branch_two = branch_two[:local_rows] + to_half(
        branch_two[local_rows:].astype(jnp.bfloat16)
    ).astype(jnp.float32)
    branch_two = branch_two.reshape(FRAMES, frame_rows, D)
    activations = (
        (middle + gate_two[:, None, :] * branch_two).astype(jnp.bfloat16).reshape(1, local_rows, D)
    )
    grad_gate_two = jnp.sum(upstream * branch_two, axis=1)
    grad_down = contract_rows(hidden, grad_branch_both).astype(jnp.bfloat16)
    grad_down = lax.psum_scatter(grad_down, ("clip", "pair"), scatter_dimension=0, tiled=True)
    grad_up = contract_rows(second_both, grad_pre).astype(jnp.bfloat16)
    grad_up = lax.psum_scatter(grad_up, ("clip", "pair"), scatter_dimension=0, tiled=True)
    grad_out = contract_rows(attended, grad_branch_one).astype(jnp.bfloat16)
    grad_out = relative_order(grad_out.reshape(BANDS, OWN_COLS, D), pair, half).reshape(D, D)
    grad_out = lax.psum_scatter(grad_out, everywhere, scatter_dimension=0, tiled=True)
    early = jnp.concatenate([grad_gate_one, grad_shift_two, grad_scale_two, grad_gate_two])
    early = lax.all_gather(band_sum(early), "clip")

    grad_query, grad_key, grad_value = attend_back(
        frame_counts, projected, grad_attended, raw, local_rows
    )
    grad_projected = to_columns(jnp.concatenate([grad_query, grad_key, grad_value]))
    grad_qkv = contract_rows(first_in, grad_projected).astype(jnp.bfloat16)
    grad_qkv = lax.psum_scatter(grad_qkv, "clip", scatter_dimension=0, tiled=True)
    grad_first = contract_cols(grad_projected, w_qkv)
    grad_first = grad_first.reshape(BANDS, FRAMES, frame_rows, D)
    late = jnp.concatenate(
        [jnp.sum(grad_first, axis=(0, 2)), jnp.sum(grad_first * normed, axis=(0, 2))]
    )
    late = lax.all_gather(band_sum(late), "clip")
    low = grad_first.astype(jnp.bfloat16)
    own_part = grad_first[0] + to_half(low[1]).astype(jnp.float32)
    far_part = grad_first[2] + to_half(low[3]).astype(jnp.float32)
    grad_first = own_part + to_pair(far_part.astype(jnp.bfloat16)).astype(jnp.float32)
    _, first_pullback = jax.vjp(lambda inner: modulate(inner, shift_one, scale_one), residual)
    input_grad = (grad_middle + first_pullback(grad_first)[0]).reshape(1, local_rows, D)

    grad_qkv = grad_qkv.reshape(BANDS, own_rows, 3 * OWN_COLS)
    grad_qkv = lax.all_to_all(grad_qkv, ("pair", "half"), 0, 0)
    grad_qkv = grad_qkv.reshape(BANDS, own_rows, 3, OWN_COLS).transpose(1, 2, 0, 3)
    grad_qkv = grad_qkv.reshape(own_rows, 3 * D).astype(jnp.float32)
    grad_up = grad_up.reshape(2, own_rows, up_groups, LANES)
    mine = jnp.where(half == 0, grad_up[0], grad_up[1])
    other = to_half(jnp.where(half == 0, grad_up[1], grad_up[0]))
    grad_up = jnp.where(
        half == 0, jnp.stack([mine, other], axis=2), jnp.stack([other, mine], axis=2)
    )
    grad_up = grad_up.reshape(own_rows, FF).astype(jnp.float32)
    grad_modulation = jnp.concatenate([late, early], axis=1).reshape(clips, 6, FRAMES, D)
    grad_modulation = grad_modulation.transpose(0, 2, 1, 3).reshape(clips * FRAMES, 6 * D)
    grad_ada = contract_rows(
        condition.astype(jnp.float32), grad_modulation, precision=lax.Precision.HIGHEST
    )
    reduced = (
        grad_qkv,
        grad_out.astype(jnp.float32),
        grad_up,
        grad_down.astype(jnp.float32),
        grad_ada,
    )
    local_squares = sum((jnp.sum(piece * piece) for piece in reduced))
    grad_norm = jnp.sqrt(lax.psum(local_squares, everywhere))
    factor = jnp.minimum(1.0, clip_limit / (grad_norm + 1e-06))
    results = []
    for master, gradient, first, second in zip(masters, reduced, firsts, seconds):
        results.extend(adam_step(master, gradient * factor, first, second))
    return (activations, input_grad, grad_norm, *results)


def embed_levels(levels):
    halfway = D // 2
    spacing = jnp.exp(-math.log(10000.0) * jnp.arange(halfway, dtype=jnp.float32) / halfway)
    angles = levels.astype(jnp.float32)[..., None] * spacing
    return jax.nn.silu(jnp.concatenate([jnp.cos(angles), jnp.sin(angles)], axis=-1))


def solution(mesh):
    clips, bands = mesh.devices.shape
    split = Mesh(mesh.devices.reshape(clips, bands // 2, 2), ("clip", "pair", "half"))
    rows = P(("clip", "pair", "half"), None)
    activation = P("clip", ("pair", "half"), None)
    return jax.shard_map(
        per_device,
        mesh=split,
        in_specs=(activation, activation, P("clip"), P("clip", None)) + (rows,) * 15,
        out_specs=(activation, activation, P()) + (rows,) * 15,
        check_vma=False,
    )
```

time: 2360 us -> 1250 us (0.53)
  waiting for transfers between devices: 1230 us -> 422 us
  matrix products: 729 us -> 324 us
  local copies, waits for them, and re-layouts: 58.5 us -> 142 us
  blocking collectives: 40.4 us -> 110 us
  other arithmetic: 260 us -> 206 us
    reduce_scatter x7 -> x5, waiting for transfers between devices: 951 us -> 233 us  [the longest x1 90.6 us: per_device(): lax.psum_scatter(grad_down, ('clip', 'pair'), scatter_dimension=0, tiled=...]
    all_gather x7 -> x5, waiting for transfers between devices: 283 us -> 65 us  [the longest x1 40.7 us: per_device(): early = lax.all_gather(band_sum(early), 'clip')]
    dot_general x52, matrix products: 341 us -> 130 us  [contract_cols(): lax.dot_general(left, right, (((1,), (1,)), ((), ())), preferred_element_...]
    convert_element_type x20 -> x7, other arithmetic: 183 us -> 22.4 us  [the longest x1 9.12 us: per_device(): first_in = first_in.astype(jnp.bfloat16).reshape(BANDS * local_rows, D)]
    ppermute x0 -> x24, waiting for transfers between devices: none -> 123 us  [the longest x7 98.5 us: to_pair(): return lax.ppermute(tensor, 'pair', [(0, 1), (1, 0)])]
    dot_general x37, matrix products: 213 us -> 90.4 us  [contract_rows(): lax.dot_general(left, right, (((0,), (0,)), ((), ())), precision=precisio...]
    dot_general x35, matrix products: 160 us -> 87.2 us  [the longest x16 35.2 us: one_block(): jnp.dot(exponent.astype(jnp.bfloat16), value, preferred_element_type=jnp....]
    all_gather x0 -> x2, blocking collectives: none -> 64.7 us  [the longest x1 32.4 us: per_device(): lax.all_gather(condition.reshape(-1, LANES), 'clip', tiled=True)]
  transfers between devices with their start and end apart: 14 -> 35, of which waited for: 12 -> 21; matrix products, arithmetic and copies ran while one was open for 14% -> 25% of each run, Pallas kernels for 0% -> 0%
where the time goes in v1:
time: 1250 us
  waiting for transfers between devices  422 us (34%)
  matrix products  324 us (26%)
  other arithmetic  206 us (16%)
  local copies, waits for them, and re-layouts  142 us (11%)
  blocking collectives  110 us (9%)
  between operations  20.7 us (2%)
  starting transfers between devices  18.2 us (1%)
    dot_general x52, matrix products, contract_cols(): lax.dot_general(left, right, (((1,), (1,)), ((), ())), preferred_element_...  130 us
    ppermute x7, waiting for transfers between devices, to_pair(): return lax.ppermute(tensor, 'pair', [(0, 1), (1, 0)])  98.5 us
    reduce_scatter x1, waiting for transfers between devices, per_device(): lax.psum_scatter(grad_down, ('clip', 'pair'), scatter_dimension=0, tiled=...  90.6 us
    dot_general x37, matrix products, contract_rows(): lax.dot_general(left, right, (((0,), (0,)), ((), ())), precision=precisio...  90.4 us
    reduce_scatter x1, waiting for transfers between devices, per_device(): lax.psum_scatter(grad_up, ('clip', 'pair'), scatter_dimension=0, tiled=True)  88.9 us
    all_gather x1, waiting for transfers between devices, per_device(): early = lax.all_gather(band_sum(early), 'clip')  40.7 us
    psum x1, blocking collectives, per_device(): grad_norm = jnp.sqrt(lax.psum(local_squares, everywhere))  37.6 us
    reduce_scatter x1, waiting for transfers between devices, per_device(): lax.psum_scatter(grad_out, everywhere, scatter_dimension=0, tiled=True)  35.7 us
  transfers between devices with their start and end apart: 35, of which 21 were waited for; matrix products, arithmetic and copies ran while one was open for 25% of the time, Pallas kernels for 0%

profile of v1, /device:TPU:0, one launch (start us, length us, event | category | flops | bytes accessed | tf_op | source)
XLA Modules:
  0.0 1245.9 jit_solution(13772167854099692563)
XLA Ops:
  8.2 32.4 %all_gather.27 = bf16[768,128]{1,0:T(8,128)(2,1)S(1)} all-gather(bf16[96,128]{1,0:T(8,128)(2,1)S(1)} %multiply_convert_fusion.3), channel_id=1, replica_groups=mesh['clip'=8,'pair'=2,'half'=2] {'clip'}, dimensions={0}, use_global_device_ids=true | all-gather | bytes 221184 | tf_op jit(solution)/shard_map/all_gather | solution.py:218
  54.5 8.1 all_to_all.10
  67.8 36.1 %collective-permute-done.3 = bf16[768,1024]{1,0:T(8,128)(2,1)S(1)} collective-permute-done((bf16[768,1024]{1,0:T(8,128)(2,1)S(1)}, bf16[768,1024]{1,0:T(8,128)(2,1)S(1)}, u32[]{:S(2)}, u32[]{:S(2)}) %collective-permute-start.3) | collective-permute-done | bytes 1572896 | tf_op jit(solution)/shard_map/ppermute | solution.py:60
  106.5 17.9 %reduce-scatter.6.cloned.1.call-done = f32[72,1024]{1,0:T(8,128)} async-done(((f32[576,1024]{1,0:T(8,128)}), f32[72,1024]{1,0:T(8,128)}) %reduce-scatter.6.cloned.1.call-update) | async-done | bytes 294928 | tf_op jit(solution)/shard_map/reduce_scatter | solution.py:225
  133.1 4.1 collective-permute-done.1
  139.5 9.1 fusion.72
  148.6 21.7 %all-gather.8.cloned.1.call-done = bf16[1024,768]{1,0:T(8,128)(2,1)} async-done(((bf16[128,768]{1,0:T(8,128)(2,1)}), bf16[1024,768]{1,0:T(8,128)(2,1)}) %all-gather.8.cloned.1.call-update) | async-done | bytes 1572880 | tf_op jit(solution)/shard_map/all_gather | solution.py:235
  170.3 9.2 convolution_convert_fusion
  179.5 9.6 copy.190
  189.1 6.7 fusion.117
  195.8 116.6 %while.58 = (s32[]{:T(128)}, f32[4,3072,64]{2,1,0:T(8,128)}, f32[4,4,768]{2,1,0:T(4,128)}, bf16[4,3072,64]{2,1,0:T(8,128)(2,1)}, bf16[4,3072,64]{2,1,0:T(8,128)(...) while((s32[]{:T(128)}, f32[4,3072,64]{2,1,0:T(8,128)}, ...), condition=%wide.region_8.9_spmd.clone, body=%wide.region_3.8_spmd.clone.sunk | while | flops 630048000 | bytes 36645192 | solution.py:117
  199.6 23.3 %while.61 = (s32[]{:T(128)}, f32[4,768,64]{1,2,0:T(8,128)S(1)}, f32[4,768]{1,0:T(4,128)S(1)}, pred[3072]{0:T(1024)(128)(4,1)S(1)}, bf16[4,768,64]{2,1,0:T(8,128)...) while((s32[]{:T(128)}, f32[4,768,64]{1,2,0:T(8,128)S(1)}, ...), condition=%wide.region_7.7_spmd, body=%wide.region_4.6_spmd.sunk | while | flops 629980416 | bytes 30325872 | solution.py:114
  228.7 23.3 %while.61 = (s32[]{:T(128)}, f32[4,768,64]{1,2,0:T(8,128)S(1)}, f32[4,768]{1,0:T(4,128)S(1)}, pred[3072]{0:T(1024)(128)(4,1)S(1)}, bf16[4,768,64]{2,1,0:T(8,128)...) while((s32[]{:T(128)}, f32[4,768,64]{1,2,0:T(8,128)S(1)}, ...), condition=%wide.region_7.7_spmd, body=%wide.region_4.6_spmd.sunk | while | flops 629980416 | bytes 30325872 | solution.py:114
  257.7 23.3 %while.61 = (s32[]{:T(128)}, f32[4,768,64]{1,2,0:T(8,128)S(1)}, f32[4,768]{1,0:T(4,128)S(1)}, pred[3072]{0:T(1024)(128)(4,1)S(1)}, bf16[4,768,64]{2,1,0:T(8,128)...) while((s32[]{:T(128)}, f32[4,768,64]{1,2,0:T(8,128)S(1)}, ...), condition=%wide.region_7.7_spmd, body=%wide.region_4.6_spmd.sunk | while | flops 629980416 | bytes 30325872 | solution.py:114
  286.8 23.3 %while.61 = (s32[]{:T(128)}, f32[4,768,64]{1,2,0:T(8,128)S(1)}, f32[4,768]{1,0:T(4,128)S(1)}, pred[3072]{0:T(1024)(128)(4,1)S(1)}, bf16[4,768,64]{2,1,0:T(8,128)...) while((s32[]{:T(128)}, f32[4,768,64]{1,2,0:T(8,128)S(1)}, ...), condition=%wide.region_7.7_spmd, body=%wide.region_4.6_spmd.sunk | while | flops 629980416 | bytes 30325872 | solution.py:114
  339.1 8.0 collective-permute-done.6
  347.2 7.7 collective-permute-done.7
  359.3 7.2 fusion.115
  371.9 12.1 fusion.76
  386.5 18.6 %fusion.71 = bf16[1536,2048]{1,0:T(8,128)(2,1)S(1)} fusion(f32[1536,2048]{1,0:T(8,128)} %fusion.76, bf16[2048,1024]{1,0:T(8,128)(2,1)} %all-gather.14.cloned.1.call-done, bf16[768,1024]{1,0:T(8,128)(2,1)} %collective-permute-done.11, bf16[768,1024]{1,0:T(8,128)(2,1)} %fusion.74), kind=kOutput, calls=%fused_computation.98 | convolution fusion | flops 6511656960 | bytes 26214400 | tf_op jit(solution)/shard_map/dot_general | solution.py:39
  405.1 6.9 fusion.123
  431.9 9.2 collective-permute-done.15
  441.1 8.7 collective-permute-done.14
  449.8 28.5 %pad_maximum_fusion.12 = bf16[2,3072,128]{2,0,1:T(2,128)(2,1)S(1)} fusion(bf16[2,768,128]{2,0,1:T(2,128)(2,1)S(1)} %collective-permute-done.15, bf16[2,768,128]{2,0,1:T(2,128)(2,1)S(1)} %collective-permute-done.14, bf16[2,768,128]{2,0,1:T(2,128)(2,1)S(1)} %collective-permute-done.13, bf16[2,768,128]{2,0,1:T(2,128)(2,1)S(1)} %get-tuple-element.535), kind=kLoop, calls=%fused_computation.154 | loop fusion | flops 2359296 | bytes 3145728 | tf_op jit(solution)/shard_map/concatenate | solution.py:292
  481.3 28.4 %pad_maximum_fusion.4 = bf16[2,6144,64]{2,0,1:T(2,128)(2,1)S(1)} fusion(bf16[2,3072,64]{2,0,1:T(2,128)(2,1)S(1)} %get-tuple-element.534, bf16[2,3072,64]{2,0,1:T(2,128)(2,1)S(1)} %get-tuple-element.533), kind=kLoop, calls=%fused_computation.123 | loop fusion | flops 786432 | bytes 3145728 | tf_op jit(solution)/shard_map/concatenate
  514.1 203.0 %while.60 = (s32[]{:T(128)}, bf16[4,3072,64]{1,2,0:T(8,128)(2,1)}, bf16[4,3072,64]{1,2,0:T(8,128)(2,1)}, bf16[4,3072,64]{1,2,0:T(8,128)(2,1)}, bf16[4,3072,64]{2...) while((s32[]{:T(128)}, bf16[4,3072,64]{1,2,0:T(8,128)(2,1)}, ...), condition=%wide.region_17.18_spmd.clone, body=%wide.region_14.17_spmd.clone.sunk | while | flops 1535084544 | bytes 59950588 | solution.py:157
  521.2 40.9 %while.62 = (s32[]{:T(128)}, f32[3072,64]{0,1:T(8,128)S(1)}, f32[3072,64]{0,1:T(8,128)S(1)}, bf16[4,768,64]{1,2,0:T(8,128)(2,1)S(1)}, pred[3072]{0:T(1024)(128)(...) while((s32[]{:T(128)}, f32[3072,64]{0,1:T(8,128)S(1)}, ...), condition=%wide.region_16.16_spmd.clone, body=%wide.region_15.15_spmd.clone.sunk | while | flops 1534623744 | bytes 52033756 | solution.py:148
  571.9 40.9 %while.62 = (s32[]{:T(128)}, f32[3072,64]{0,1:T(8,128)S(1)}, f32[3072,64]{0,1:T(8,128)S(1)}, bf16[4,768,64]{1,2,0:T(8,128)(2,1)S(1)}, pred[3072]{0:T(1024)(128)(...) while((s32[]{:T(128)}, f32[3072,64]{0,1:T(8,128)S(1)}, ...), condition=%wide.region_16.16_spmd.clone, body=%wide.region_15.15_spmd.clone.sunk | while | flops 1534623744 | bytes 52033756 | solution.py:148
  622.6 40.9 %while.62 = (s32[]{:T(128)}, f32[3072,64]{0,1:T(8,128)S(1)}, f32[3072,64]{0,1:T(8,128)S(1)}, bf16[4,768,64]{1,2,0:T(8,128)(2,1)S(1)}, pred[3072]{0:T(1024)(128)(...) while((s32[]{:T(128)}, f32[3072,64]{0,1:T(8,128)S(1)}, ...), condition=%wide.region_16.16_spmd.clone, body=%wide.region_15.15_spmd.clone.sunk | while | flops 1534623744 | bytes 52033756 | solution.py:148
  673.2 40.9 %while.62 = (s32[]{:T(128)}, f32[3072,64]{0,1:T(8,128)S(1)}, f32[3072,64]{0,1:T(8,128)S(1)}, bf16[4,768,64]{1,2,0:T(8,128)(2,1)S(1)}, pred[3072]{0:T(1024)(128)(...) while((s32[]{:T(128)}, f32[3072,64]{0,1:T(8,128)S(1)}, ...), condition=%wide.region_16.16_spmd.clone, body=%wide.region_15.15_spmd.clone.sunk | while | flops 1534623744 | bytes 52033756 | solution.py:148
  720.2 5.2 fusion.124
  725.4 8.0 fusion.105
  733.4 6.4 convolution_convert_fusion.4
  748.0 8.3 convert_element_type.220
  759.9 11.6 fusion.104
  783.2 32.5 %collective-permute-done.18 = bf16[12,64,1024]{2,1,0:T(8,128)(2,1)} collective-permute-done((bf16[12,64,1024]{2,1,0:T(8,128)(2,1)}, bf16[12,64,1024]{2,1,0:T(8,128)(2,1)}, u32[]{:S(2)}, u32[]{:S(2)}) %collective-permute-start.18) | collective-permute-done | bytes 1572896 | tf_op jit(solution)/shard_map/ppermute | solution.py:60
  815.8 5.8 multiply_reduce_fusion.3
  825.2 5.9 collective-permute-done.23
  831.8 11.3 convolution_convert_fusion.2
  843.6 13.2 %convolution_convert_fusion.1 = bf16[2048,1024]{1,0:T(8,128)(2,1)} fusion(bf16[768,1024]{1,0:T(8,128)(2,1)} %collective-permute-done.11, bf16[768,1024]{1,0:T(8,128)(2,1)} %fusion.74, f32[1536,2048]{1,0:T(8,128)} %fusion.76), kind=kOutput, calls=%fused_computation.115 | convolution fusion | flops 6479151104 | bytes 19922944 | tf_op jit(solution)/shard_map/dot_general | solution.py:29
  864.0 32.3 %all-gather = f32[192,1024]{1,0:T(8,128)S(1)} all-gather(f32[24,1024]{1,0:T(8,128)S(1)} %add.325), channel_id=2, replica_groups=mesh['clip'=8,'pair'=2,'half'=2] {'clip'}, dimensions={0}, use_global_device_ids=true | all-gather | bytes 884736 | tf_op jit(solution)/shard_map/all_gather | solution.py:326
  900.4 5.1 fusion.114
  906.2 35.7 %reduce-scatter.10.cloned.1.call-done = bf16[32,1024]{1,0:T(8,128)(2,1)} async-done(((bf16[1024,1024]{1,0:T(8,128)(2,1)}), bf16[32,1024]{1,0:T(8,128)(2,1)}) %reduce-scatter.10.cloned.1.call-update) | async-done | bytes 65552 | tf_op jit(solution)/shard_map/reduce_scatter | solution.py:311
  944.7 40.7 %all-gather.16.cloned.1.call-done = f32[384,1024]{1,0:T(8,128)} async-done(((f32[48,1024]{1,0:T(8,128)}), f32[384,1024]{1,0:T(8,128)}) %all-gather.16.cloned.1.call-update) | async-done | bytes 1572880 | tf_op jit(solution)/shard_map/all_gather | solution.py:313
  992.9 88.9 %reduce-scatter.12.cloned.1.call-done = bf16[64,2048]{1,0:T(8,128)(2,1)} async-done(((bf16[1024,2048]{1,0:T(8,128)(2,1)}), bf16[64,2048]{1,0:T(8,128)(2,1)}) %reduce-scatter.12.cloned.1.call-update) | async-done | bytes 262160 | tf_op jit(solution)/shard_map/reduce_scatter | solution.py:308
  1083.5 4.2 multiply_reduce_fusion.10
  1087.7 90.6 %reduce-scatter.14.cloned.1.call-done = bf16[128,1024]{1,0:T(8,128)(2,1)} async-done(((bf16[2048,1024]{1,0:T(8,128)(2,1)}), bf16[128,1024]{1,0:T(8,128)(2,1)}) %reduce-scatter.14.cloned.1.call-update) | async-done | bytes 262160 | tf_op jit(solution)/shard_map/reduce_scatter | solution.py:306
  1187.6 37.6 %psum.7 = f32[]{:T(128)} all-reduce(f32[]{:T(128)S(6)} %add.328), channel_id=1, replica_groups=mesh['clip'=8,'pair'=2,'half'=2] {'clip','pair','half'}, use_global_device_ids=true, to_apply=%region_37.38 | all-reduce | flops 1 | bytes 8 | tf_op jit(solution)/shard_map/psum | solution.py:358
  (652 shorter events, 488.8 us)
Async XLA Ops:
  7.2 117.1 %reduce-scatter.6.cloned.1.call-start = ((), (), s32[]{:S(2)}) async-start(), calls=%async_computation.7 | async-start | bytes 2654208 | tf_op jit(solution)/shard_map/reduce_scatter | solution.py:225
  54.2 116.1 %all-gather.8.cloned.1.call-start = ((), (), s32[]{:S(2)}) async-start(), calls=%async_computation.8 | async-start | bytes 1769472 | tf_op jit(solution)/shard_map/all_gather | solution.py:235
  63.5 269.7 %all-gather.10.cloned.1.call-start = ((), (), s32[]{:S(2)}) async-start(), calls=%async_computation.9 | async-start | bytes 2162688 | tf_op jit(solution)/shard_map/all_gather | solution.py:244
  64.2 307.7 %all-gather.12.cloned.1.call-start = ((), (), s32[]{:S(2)}) async-start(), calls=%async_computation.10 | async-start | bytes 4456448 | tf_op jit(solution)/shard_map/all_gather | solution.py:242
  65.1 1.4 collective-permute-start.9
  67.4 319.2 %all-gather.14.cloned.1.call-start = ((), (), s32[]{:S(2)}) async-start(), calls=%async_computation.11 | async-start | bytes 4456448 | tf_op jit(solution)/shard_map/all_gather | solution.py:243
  67.4 36.5 %collective-permute-start.3 = (bf16[768,1024]{1,0:T(8,128)(2,1)S(1)}, bf16[768,1024]{1,0:T(8,128)(2,1)S(1)}, u32[]{:S(2)}, u32[]{:S(2)}) collective-permute-start(bf16[768,1024]{1,0:T(8,128)(2,1)S(1)} %bitcast.267), channel_id=1, source_target_pairs={{0,2},{2,0},{1,3},{3,1},{4,6},{6,4},{5,7},{7,5},{8,10},{10,8},{9,1... | collective-permute-start | bytes 4718600 | tf_op jit(solution)/shard_map/ppermute | solution.py:60
  67.8 56.5 %collective-permute-start.2 = (bf16[768,1024]{1,0:T(8,128)(2,1)S(1)}, bf16[768,1024]{1,0:T(8,128)(2,1)}, u32[]{:S(2)}, u32[]{:S(2)}) collective-permute-start(bf16[768,1024]{1,0:T(8,128)(2,1)S(1)} %bitcast.268), channel_id=1, source_target_pairs={{0,1},{1,0},{2,3},{3,2},{4,5},{5,4},{6,7},{7,6},{8,9},{9,8},{10,11... | collective-permute-start | bytes 4718600 | tf_op jit(solution)/shard_map/ppermute | solution.py:56
  103.9 34.9 %copy-start.9 = (bf16[768,1024]{1,0:T(8,128)(2,1)}, bf16[768,1024]{1,0:T(8,128)(2,1)S(1)}, u32[]{:S(2)}) copy-start(bf16[768,1024]{1,0:T(8,128)(2,1)S(1)} %collective-permute-done.3) | copy-start | bytes 4718596
  103.9 20.4 %collective-permute-start.4 = (bf16[768,1024]{1,0:T(8,128)(2,1)S(1)}, bf16[768,1024]{1,0:T(8,128)(2,1)}, u32[]{:S(2)}, u32[]{:S(2)}) collective-permute-start(bf16[768,1024]{1,0:T(8,128)(2,1)S(1)} %collective-permute-done.3), channel_id=1, source_target_pairs={{0,1},{1,0},{2,3},{3,2},{4,5},{5,4},{6,7},{7,6},{8,9},{9,8},{10,11... | collective-permute-start | bytes 4718600 | tf_op jit(solution)/shard_map/ppermute | solution.py:56
  106.1 790.2 %reduce-scatter.8.cloned.1.call-start = ((), (), s32[]{:S(2)}) async-start(), calls=%async_computation.12 | async-start | bytes 1769472 | tf_op jit(solution)/shard_map/reduce_scatter | solution.py:320
  124.3 3.2 collective-permute-start
  127.6 9.6 collective-permute-start.1
  133.0 15.7 %copy-start.51 = (f32[4,12,64]{2,1,0:T(8,128)}, f32[4,12,64]{2,1,0:T(8,128)S(1)}, u32[]{:S(2)}) copy-start(f32[4,12,64]{2,1,0:T(8,128)S(1)} %add_rsqrt_fusion) | copy-start | bytes 36868
  331.3 7.8 collective-permute-start.5
  331.3 15.9 %collective-permute-start.6 = (bf16[2,768,128]{2,1,0:T(8,128)(2,1)}, bf16[2,768,128]{2,1,0:T(8,128)(2,1)S(1)}, u32[]{:S(2)}, u32[]{:S(2)}) collective-permute-start(bf16[2,768,128]{2,1,0:T(8,128)(2,1)} %bitcast.26), channel_id=1, source_target_pairs={{0,2},{2,0},{1,3},{3,1},{4,6},{6,4},{5,7},{7,5},{8,10},{10,8},{9,1... | collective-permute-start | bytes 1179656 | tf_op jit(solution)/shard_map/ppermute | solution.py:60
  332.8 22.0 %collective-permute-start.7 = (bf16[2,768,128]{2,1,0:T(8,128)(2,1)S(1)}, bf16[2,768,128]{2,1,0:T(8,128)(2,1)S(1)}, u32[]{:S(2)}, u32[]{:S(2)}) collective-permute-start(bf16[2,768,128]{2,1,0:T(8,128)(2,1)S(1)} %bitcast.333), channel_id=1, source_target_pairs={{0,3},{1,2},{2,1},{3,0},{4,7},{5,6},{6,5},{7,4},{8,11},{9,10},{10,... | collective-permute-start | bytes 1179656 | tf_op jit(solution)/shard_map/ppermute | solution.py:64
  366.5 53.3 %copy-start = (f32[12,64,1024]{2,1,0:T(8,128)}, f32[12,64,1024]{2,1,0:T(8,128)S(1)}, u32[]{:S(2)}) copy-start(f32[12,64,1024]{2,1,0:T(8,128)S(1)} %get-tuple-element.509) | copy-start | bytes 9437188
  368.2 3.6 collective-permute-start.8
  370.7 13.2 %collective-permute-start.11 = (bf16[768,1024]{1,0:T(8,128)(2,1)}, bf16[768,1024]{1,0:T(8,128)(2,1)}, u32[]{:S(2)}, u32[]{:S(2)}) collective-permute-start(bf16[768,1024]{1,0:T(8,128)(2,1)} %fusion.74), channel_id=1, source_target_pairs={{0,1},{1,0},{2,3},{3,2},{4,5},{5,4},{6,7},{7,6},{8,9},{9,8},{10,11... | collective-permute-start | bytes 4718600 | tf_op jit(solution)/shard_map/ppermute | solution.py:56
  386.5 18.6 %copy-start.58 = (bf16[1024,2048]{1,0:T(8,128)(2,1)S(1)}, bf16[1024,2048]{1,0:T(8,128)(2,1)}, u32[]{:S(2)}) copy-start(bf16[1024,2048]{1,0:T(8,128)(2,1)} %all-gather.12.cloned.1.call-done) | copy-start | bytes 12582916
  412.3 3.5 collective-permute-start.12
  429.9 11.2 collective-permute-start.15
  431.2 18.6 %collective-permute-start.14 = (bf16[2,768,128]{2,0,1:T(2,128)(2,1)S(1)}, bf16[2,768,128]{2,0,1:T(2,128)(2,1)S(1)}, u32[]{:S(2)}, u32[]{:S(2)}) collective-permute-start(bf16[2,768,128]{2,0,1:T(2,128)(2,1)S(1)} %get-tuple-element.537), channel_id=1, source_target_pairs={{0,2},{2,0},{1,3},{3,1},{4,6},{6,4},{5,7},{7,5},{8,10},{10,8},{9,1... | collective-permute-start | bytes 1179656 | tf_op jit(solution)/shard_map/ppermute | solution.py:60
  431.8 18.1 %collective-permute-start.13 = (bf16[2,768,128]{2,0,1:T(2,128)(2,1)S(1)}, bf16[2,768,128]{2,0,1:T(2,128)(2,1)S(1)}, u32[]{:S(2)}, u32[]{:S(2)}) collective-permute-start(bf16[2,768,128]{2,0,1:T(2,128)(2,1)S(1)} %get-tuple-element.538), channel_id=1, source_target_pairs={{0,1},{1,0},{2,3},{3,2},{4,5},{5,4},{6,7},{7,6},{8,9},{9,8},{10,11... | collective-permute-start | bytes 1179656 | tf_op jit(solution)/shard_map/ppermute | solution.py:56
  478.4 33.4 %slice-start.3 = ((s8[6291456]{0:T(1024)(128)(4,1)}), s8[4194304]{0:T(1024)(128)(4,1)S(1)}, s32[]{:S(2)}) async-start(s8[6291456]{0:T(1024)(128)(4,1)} %bitcast.284), calls=%async_computation.20 | async-start | bytes 8388608
  481.3 30.5 %slice-start.4 = ((s8[6291456]{0:T(1024)(128)(4,1)}), s8[2097152]{0:T(1024)(128)(4,1)S(1)}, s32[]{:S(2)}) async-start(s8[6291456]{0:T(1024)(128)(4,1)} %bitcast.284), calls=%async_computation.21 | async-start | bytes 4194304
  739.8 202.2 %reduce-scatter.10.cloned.1.call-start = ((), (), s32[]{:S(2)}) async-start(), calls=%async_computation.13 | async-start | bytes 2162688 | tf_op jit(solution)/shard_map/reduce_scatter | solution.py:311
  747.7 237.7 %all-gather.16.cloned.1.call-start = ((), (), s32[]{:S(2)}) async-start(), calls=%async_computation.16 | async-start | bytes 1769472 | tf_op jit(solution)/shard_map/all_gather | solution.py:313
  756.2 17.7 %slice-start = ((s8[12582912]{0:T(1024)(128)(4,1)}), s8[4194304]{0:T(1024)(128)(4,1)S(1)}, s32[]{:S(2)}) async-start(s8[12582912]{0:T(1024)(128)(4,1)} %bitcast.263), calls=%async_computation.17 | async-start | bytes 8388608
  759.9 14.0 %slice-start.2 = ((s8[12582912]{0:T(1024)(128)(4,1)}), s8[4194304]{0:T(1024)(128)(4,1)S(1)}, s32[]{:S(2)}) async-start(s8[12582912]{0:T(1024)(128)(4,1)} %bitcast.263), calls=%async_computation.19 | async-start | bytes 8388608
  759.9 16.6 %collective-permute-start.17 = (bf16[12,64,1024]{2,1,0:T(8,128)(2,1)S(1)}, bf16[12,64,1024]{2,1,0:T(8,128)(2,1)S(1)}, u32[]{:S(2)}, u32[]{:S(2)}) collective-permute-start(bf16[12,64,1024]{2,1,0:T(8,128)(2,1)S(1)} %get-tuple-element.530), channel_id=1, source_target_pairs={{0,1},{1,0},{2,3},{3,2},{4,5},{5,4},{6,7},{7,6},{8,9},{9,8},{10,11... | collective-permute-start | bytes 4718600 | tf_op jit(solution)/shard_map/ppermute | solution.py:56
  773.2 6.9 collective-permute-start.10
  776.3 6.9 collective-permute-start.16
  778.3 37.4 %collective-permute-start.18 = (bf16[12,64,1024]{2,1,0:T(8,128)(2,1)}, bf16[12,64,1024]{2,1,0:T(8,128)(2,1)}, u32[]{:S(2)}, u32[]{:S(2)}) collective-permute-start(bf16[12,64,1024]{2,1,0:T(8,128)(2,1)} %add_convert_fusion.1), channel_id=1, source_target_pairs={{0,2},{2,0},{1,3},{3,1},{4,6},{6,4},{5,7},{7,5},{8,10},{10,8},{9,1... | collective-permute-start | bytes 4718600 | tf_op jit(solution)/shard_map/ppermute | solution.py:60
  780.1 35.6 %copy-start.1 = (f32[12,64,1024]{2,1,0:T(8,128)S(1)}, f32[12,64,1024]{2,1,0:T(8,128)}, u32[]{:S(2)}) copy-start(f32[12,64,1024]{2,1,0:T(8,128)} %copy-done) | copy-start | bytes 9437188
  780.1 35.6 %copy-start.8 = (f32[12,64,1024]{2,1,0:T(8,128)S(1)}, f32[12,64,1024]{2,1,0:T(8,128)}, u32[]{:S(2)}) copy-start(f32[12,64,1024]{2,1,0:T(8,128)} %get-tuple-element.510) | copy-start | bytes 9437188
  780.1 35.6 %copy-start.39 = (f32[12,1024]{1,0:T(8,128)S(1)}, f32[12,1024]{1,0:T(8,128)}, u32[]{:S(2)}) copy-start(f32[12,1024]{1,0:T(8,128)} %get-tuple-element.543) | copy-start | bytes 147460
  821.6 1.5 collective-permute-start.22
  823.2 7.9 collective-permute-start.23
  831.8 250.0 %reduce-scatter.12.cloned.1.call-start = ((), (), s32[]{:S(2)}) async-start(), calls=%async_computation.14 | async-start | bytes 4456448 | tf_op jit(solution)/shard_map/reduce_scatter | solution.py:308
  843.1 335.2 %reduce-scatter.14.cloned.1.call-start = ((), (), s32[]{:S(2)}) async-start(), calls=%async_computation.15 | async-start | bytes 4456448 | tf_op jit(solution)/shard_map/reduce_scatter | solution.py:306
  856.8 1.4 collective-permute-start.20
  858.2 5.8 collective-permute-start.21
  896.3 9.2 all-to-all-start.1
  992.9 190.8 %copy-start.7 = (f32[12,64,1024]{2,1,0:T(8,128)S(1)}, f32[12,64,1024]{2,1,0:T(8,128)}, u32[]{:S(2)}) copy-start(f32[12,64,1024]{2,1,0:T(8,128)} %copy-done.6) | copy-start | bytes 9437188
  1083.5 96.5 %collective-permute-start.19 = (bf16[32,16,128]{2,1,0:T(8,128)(2,1)}, bf16[32,16,128]{2,1,0:T(8,128)(2,1)}, u32[]{:S(2)}, u32[]{:S(2)}) collective-permute-start(bf16[32,16,128]{2,1,0:T(8,128)(2,1)} %bitcast.116), channel_id=1, source_target_pairs={{0,1},{1,0},{2,3},{3,2},{4,5},{5,4},{6,7},{7,6},{8,9},{9,8},{10,11... | collective-permute-start | bytes 393224 | tf_op jit(solution)/shard_map/ppermute | solution.py:56
  1187.6 41.0 %copy-start.31 = (f32[32,3072]{1,0:T(8,128)S(1)}, f32[32,3072]{1,0:T(8,128)}, u32[]{:S(2)}) copy-start(f32[32,3072]{1,0:T(8,128)} %param.31) | copy-start | bytes 1179652
  (83 other events, 273.6 us)
Sparse Core Ops, SparseCore 0:
  54.4 69.9 reduce-scatter.5
  127.1 43.1 all-gather.7
  173.8 55.2 all-gather.9
  232.2 74.7 all-gather.11
  310.2 76.2 all-gather.13
  739.9 63.5 reduce-scatter.7
  805.8 136.0 reduce-scatter.9
  944.7 40.6 all-gather.15
  987.8 94.0 reduce-scatter.11
  1084.0 94.3 reduce-scatter.13

commit v2 on v1

--- a/solution.py
+++ b/solution.py
@@ -69,6 +69,37 @@
     return tensor + to_pair(tensor)
 
 
+def clip_exchange(tensor, distance, clips):
+    return lax.ppermute(tensor, "clip", [(place, place ^ distance) for place in range(clips)])
+
+
+def clip_gather(tensor, clip, clips):
+    distance = 1
+    while distance < clips:
+        other = clip_exchange(tensor, distance, clips)
+        later = (clip // distance) % 2 == 1
+        tensor = jnp.where(
+            later, jnp.concatenate([other, tensor]), jnp.concatenate([tensor, other])
+        )
+        distance *= 2
+    return tensor
+
+
+def sum_everywhere(tensor, clips):
+    tensor = band_sum(tensor)
+    distance = 1
+    while distance < clips:
+        tensor = tensor + clip_exchange(tensor, distance, clips)
+        distance *= 2
+    return tensor
+
+
+def in_order(own, other, index, axis=0):
+    return jnp.where(
+        index == 0, jnp.stack([own, other], axis=axis), jnp.stack([other, own], axis=axis)
+    )
+
+
 def relative_order(blocks, pair, half):
     rest = blocks.shape[1:]
     blocks = blocks.reshape((2, 2) + rest)
@@ -77,14 +108,12 @@
     return blocks.reshape((BANDS,) + rest)
 
 
-def heads_of(blocks):
-    count, rows, _ = blocks.shape
-    return blocks.reshape(count, rows, 2, HEAD_DIM).transpose(0, 2, 1, 3).reshape(-1, rows, HEAD_DIM)
-
-
-def blocks_of(heads):
-    count, rows, _ = heads.shape
-    return heads.reshape(-1, 2, rows, HEAD_DIM).transpose(0, 2, 1, 3).reshape(-1, rows, LANES)
+def heads_of(tensor):
+    return tensor.reshape(tensor.shape[0], -1, HEAD_DIM).transpose(1, 0, 2)
+
+
+def columns_of(heads):
+    return heads.transpose(1, 0, 2).reshape(heads.shape[1], -1)
 
 
 def valid_keys(count, rows, local_rows):
@@ -92,7 +121,7 @@
 
 
 def attend(count, projected, local_rows):
-    rows = projected.shape[1]
+    rows = projected.shape[0]
     key_valid = valid_keys(count, rows, local_rows)
     heads = heads_of(projected).reshape(3, BANDS, rows, HEAD_DIM)
 
@@ -115,11 +144,11 @@
         return outcome.reshape(rows, HEAD_DIM), logs
 
     outcome, logs = lax.map(one_head, (heads[0], heads[1], heads[2]))
-    return blocks_of(outcome.astype(jnp.bfloat16)), (outcome, logs)
+    return columns_of(outcome.astype(jnp.bfloat16)), (outcome, logs)
 
 
 def attend_back(count, projected, grad_attended, raw, local_rows):
-    rows = projected.shape[1]
+    rows = projected.shape[0]
     key_valid = valid_keys(count, rows, local_rows)
     heads = heads_of(projected).reshape(3, BANDS, rows, HEAD_DIM)
     outcome, logs = raw
@@ -155,15 +184,7 @@
         )
 
     results = lax.map(one_head, (*heads, logs, deltas, grads))
-    return tuple(blocks_of(result) for result in results)
-
-
-def to_columns(blocks):
-    return blocks.transpose(1, 0, 2).reshape(blocks.shape[1], -1)
-
-
-def to_blocks(tensor):
-    return tensor.reshape(tensor.shape[0], -1, LANES).transpose(1, 0, 2)
+    return jnp.concatenate([columns_of(result) for result in results], axis=1)
 
 
 def adam_step(master, clipped, first, second):
@@ -214,25 +235,30 @@
     pair_tokens = to_pair(own_tokens)
     clip_tokens = jnp.stack([own_tokens, half_tokens, pair_tokens, to_half(pair_tokens)])
 
+    w_first = jnp.concatenate(
+        [
+            qkv_master.astype(jnp.bfloat16)
+            .reshape(own_rows, 3, BANDS, OWN_COLS)
+            .transpose(2, 0, 1, 3)
+            .reshape(BANDS, own_rows, 3 * OWN_COLS),
+            ada_master.astype(jnp.bfloat16)
+            .reshape(own_rows, BANDS, 6 * OWN_COLS)
+            .transpose(1, 0, 2),
+        ],
+        axis=2,
+    )
+    w_first = lax.all_to_all(w_first, ("pair", "half"), 0, 0)
+    w_first = lax.all_gather(w_first.reshape(BANDS * own_rows, 9 * OWN_COLS), "clip", tiled=True)
+    w_qkv = w_first[:, : 3 * OWN_COLS]
+
     condition = embed_levels(noise_levels[0]).astype(jnp.bfloat16)
-    conditions = lax.all_gather(condition.reshape(-1, LANES), "clip", tiled=True)
-    device = (clip * 2 + pair) * 2 + half
-    condition = lax.dynamic_slice_in_dim(
-        conditions.reshape(clips * FRAMES, D), device * own_rows, own_rows, axis=1
-    )
-    part = jnp.dot(condition, ada_master.astype(jnp.bfloat16), preferred_element_type=jnp.float32)
-    part = part.reshape(clips, FRAMES, 6, D).transpose(0, 2, 1, 3)
-    modulation = lax.psum_scatter(
-        part.reshape(clips * 6 * FRAMES, D), "clip", scatter_dimension=0, tiled=True
-    )
-    modulation = band_sum(modulation)
-    shift_one, scale_one, gate_one, shift_two, scale_two, gate_two = modulation.reshape(
-        6, FRAMES, D
-    )
-
-    w_qkv = qkv_master.astype(jnp.bfloat16).reshape(own_rows, 3, BANDS, OWN_COLS)
-    w_qkv = lax.all_to_all(w_qkv.transpose(2, 0, 1, 3), ("pair", "half"), 0, 0)
-    w_qkv = lax.all_gather(w_qkv.reshape(BANDS * own_rows, 3 * OWN_COLS), "clip", tiled=True)
+    modulation = jnp.dot(condition, w_first[:, 3 * OWN_COLS :], preferred_element_type=jnp.float32)
+    modulation = in_order(modulation, to_half(modulation), half)
+    modulation = in_order(modulation, to_pair(modulation), pair)
+    modulation = modulation.reshape(BANDS, FRAMES, 6 * OWN_COLS).transpose(1, 0, 2)
+    shift_one, scale_one, gate_one, shift_two, scale_two, gate_two = jnp.split(
+        modulation.reshape(FRAMES, 6 * D), 6, axis=1
+    )
 
     up_low = up_master.astype(jnp.bfloat16).reshape(own_rows, up_groups, 2, LANES)
     mine = jnp.where(half == 0, up_low[:, :, 0], up_low[:, :, 1])
@@ -249,14 +275,10 @@
     first_in = normed * (1.0 + scale_one[None, :, None, :]) + shift_one[None, :, None, :]
     first_in = first_in.astype(jnp.bfloat16).reshape(BANDS * local_rows, D)
     projected = jnp.dot(first_in, w_qkv, preferred_element_type=jnp.float32).astype(jnp.bfloat16)
-    projected = to_blocks(projected)
     attended, raw = attend(frame_counts, projected, local_rows)
-    attended = attended.reshape(-1, BANDS, local_rows, LANES)
-    attended = [attended[:, place] for place in range(BANDS)]
-    attended = to_columns(
-        jnp.concatenate(
-            [attended[0], to_half(attended[1]), to_pair(attended[2]), to_both(attended[3])]
-        )
+    attended = attended.reshape(BANDS, local_rows, OWN_COLS)
+    attended = jnp.concatenate(
+        [attended[0], to_half(attended[1]), to_pair(attended[2]), to_both(attended[3])], axis=1
     )
 
     residual = own_tokens.astype(jnp.float32).reshape(FRAMES, frame_rows, D)
@@ -288,9 +310,9 @@
     )
     grad_gate_one = jnp.sum(grad_middle * branch_one, axis=1)
     grad_attended = contract_cols(grad_branch_one, w_out).astype(jnp.bfloat16)
-    pieces = to_blocks(grad_attended).reshape(BANDS, -1, local_rows, LANES)
+    pieces = jnp.split(grad_attended, BANDS, axis=1)
     grad_attended = jnp.concatenate(
-        [pieces[0], to_half(pieces[1]), to_pair(pieces[2]), to_both(pieces[3])], axis=1
+        [pieces[0], to_half(pieces[1]), to_pair(pieces[2]), to_both(pieces[3])]
     )
 
     branch_two = jnp.dot(hidden, w_down, preferred_element_type=jnp.float32)
@@ -302,20 +324,39 @@
         (middle + gate_two[:, None, :] * branch_two).astype(jnp.bfloat16).reshape(1, local_rows, D)
     )
     grad_gate_two = jnp.sum(upstream * branch_two, axis=1)
+    groups = clips * (BANDS // 2)
+    down_rows = down_master.shape[0]
     grad_down = contract_rows(hidden, grad_branch_both).astype(jnp.bfloat16)
-    grad_down = lax.psum_scatter(grad_down, ("clip", "pair"), scatter_dimension=0, tiled=True)
     grad_up = contract_rows(second_both, grad_pre).astype(jnp.bfloat16)
-    grad_up = lax.psum_scatter(grad_up, ("clip", "pair"), scatter_dimension=0, tiled=True)
-    grad_out = contract_rows(attended, grad_branch_one).astype(jnp.bfloat16)
-    grad_out = relative_order(grad_out.reshape(BANDS, OWN_COLS, D), pair, half).reshape(D, D)
-    grad_out = lax.psum_scatter(grad_out, everywhere, scatter_dimension=0, tiled=True)
-    early = jnp.concatenate([grad_gate_one, grad_shift_two, grad_scale_two, grad_gate_two])
-    early = lax.all_gather(band_sum(early), "clip")
-
-    grad_query, grad_key, grad_value = attend_back(
-        frame_counts, projected, grad_attended, raw, local_rows
-    )
-    grad_projected = to_columns(jnp.concatenate([grad_query, grad_key, grad_value]))
+    grad_out = contract_rows(attended, grad_branch_one)
+    grad_out = relative_order(grad_out.reshape(BANDS, OWN_COLS, D), pair, half)
+    grad_out = grad_out.reshape(groups, 2, own_rows, D)
+    mine = jnp.where(half == 0, grad_out[:, 0], grad_out[:, 1])
+    other = jnp.where(half == 0, grad_out[:, 1], grad_out[:, 0]).astype(jnp.bfloat16)
+    grad_out = (mine + to_half(other).astype(jnp.float32)).astype(jnp.bfloat16)
+    packed = jnp.concatenate(
+        [
+            grad_down.reshape(groups, down_rows, D),
+            grad_up.reshape(groups, 2, own_rows, 2, D)
+            .transpose(0, 1, 3, 2, 4)
+            .reshape(groups, 4 * own_rows, D),
+            grad_out,
+        ],
+        axis=1,
+    )
+    packed = lax.psum_scatter(
+        packed.reshape(-1, D), ("clip", "pair"), scatter_dimension=0, tiled=True
+    )
+    early = band_sum(
+        jnp.concatenate([grad_gate_one, grad_shift_two, grad_scale_two, grad_gate_two])
+    )
+    early = jnp.concatenate(
+        [early, condition.astype(jnp.float32), jnp.zeros((4, D), jnp.float32)]
+    )
+    early = lax.all_gather(early, "clip")
+
+    grad_projected = attend_back(frame_counts, projected, grad_attended, raw, local_rows)
+    grad_projected, packed, early = lax.optimization_barrier((grad_projected, packed, early))
     grad_qkv = contract_rows(first_in, grad_projected).astype(jnp.bfloat16)
     grad_qkv = lax.psum_scatter(grad_qkv, "clip", scatter_dimension=0, tiled=True)
     grad_first = contract_cols(grad_projected, w_qkv)
@@ -323,7 +364,7 @@
     late = jnp.concatenate(
         [jnp.sum(grad_first, axis=(0, 2)), jnp.sum(grad_first * normed, axis=(0, 2))]
     )
-    late = lax.all_gather(band_sum(late), "clip")
+    late = clip_gather(band_sum(late), clip, clips).reshape(clips, 2 * FRAMES, D)
     low = grad_first.astype(jnp.bfloat16)
     own_part = grad_first[0] + to_half(low[1]).astype(jnp.float32)
     far_part = grad_first[2] + to_half(low[3]).astype(jnp.float32)
@@ -335,17 +376,27 @@
     grad_qkv = lax.all_to_all(grad_qkv, ("pair", "half"), 0, 0)
     grad_qkv = grad_qkv.reshape(BANDS, own_rows, 3, OWN_COLS).transpose(1, 2, 0, 3)
     grad_qkv = grad_qkv.reshape(own_rows, 3 * D).astype(jnp.float32)
-    grad_up = grad_up.reshape(2, own_rows, up_groups, LANES)
+    grad_down = packed[:down_rows]
+    grad_up = packed[down_rows : down_rows + 4 * own_rows].reshape(2, 2, own_rows, D)
+    grad_out = packed[down_rows + 4 * own_rows :]
     mine = jnp.where(half == 0, grad_up[0], grad_up[1])
     other = to_half(jnp.where(half == 0, grad_up[1], grad_up[0]))
-    grad_up = jnp.where(
-        half == 0, jnp.stack([mine, other], axis=2), jnp.stack([other, mine], axis=2)
-    )
+
+    def to_groups(tensor):
+        tensor = tensor.transpose(1, 0, 2).reshape(own_rows, up_groups, LANES)
+        return tensor
+
+    grad_up = in_order(to_groups(mine), to_groups(other), half, axis=2)
     grad_up = grad_up.reshape(own_rows, FF).astype(jnp.float32)
-    grad_modulation = jnp.concatenate([late, early], axis=1).reshape(clips, 6, FRAMES, D)
+    conditions = early[:, 4 * FRAMES : 5 * FRAMES].reshape(clips * FRAMES, D)
+    grad_modulation = jnp.concatenate([late, early[:, : 4 * FRAMES]], axis=1)
+    grad_modulation = grad_modulation.reshape(clips, 6, FRAMES, D)
     grad_modulation = grad_modulation.transpose(0, 2, 1, 3).reshape(clips * FRAMES, 6 * D)
+    device = (clip * 2 + pair) * 2 + half
     grad_ada = contract_rows(
-        condition.astype(jnp.float32), grad_modulation, precision=lax.Precision.HIGHEST
+        lax.dynamic_slice_in_dim(conditions, device * own_rows, own_rows, axis=1),
+        grad_modulation,
+        precision=lax.Precision.HIGHEST,
     )
     reduced = (
         grad_qkv,
@@ -355,7 +406,8 @@
         grad_ada,
     )
     local_squares = sum((jnp.sum(piece * piece) for piece in reduced))
-    grad_norm = jnp.sqrt(lax.psum(local_squares, everywhere))
+    squares = sum_everywhere(jnp.full((8, LANES), local_squares), clips)
+    grad_norm = jnp.sqrt(squares[0, 0])
     factor = jnp.minimum(1.0, clip_limit / (grad_norm + 1e-06))
     results = []
     for master, gradient, first, second in zip(masters, reduced, firsts, seconds):

time: 1250 us -> 1040 us (0.83)
  waiting for transfers between devices: 422 us -> 105 us
  matrix products: 324 us -> 469 us
  blocking collectives: 110 us -> 13.8 us
  local copies, waits for them, and re-layouts: 142 us -> 235 us
  other arithmetic: 206 us -> 166 us
    reduce_scatter x4 -> x1, waiting for transfers between devices: 233 us -> 0.01 us  [per_device(): lax.psum_scatter(packed.reshape(-1, D), ('clip', 'pair'), scatter_dimensi...]
    while x64 -> x224, local copies, waits for them, and re-layouts: 0.2 us -> 95.4 us
    dot_general x37, matrix products: 90.4 us -> 160 us  [contract_rows(): lax.dot_general(left, right, (((0,), (0,)), ((), ())), precision=precisio...]
    all_gather x2 -> x0, blocking collectives: 64.7 us -> none  [the longest x1 32.4 us: per_device(): lax.all_gather(condition.reshape(-1, LANES), 'clip', tiled=True)]
    dot_general x16, matrix products: 35.2 us -> 82 us  [one_block(): jnp.dot(exponent.astype(jnp.bfloat16), value, preferred_element_type=jnp....]
    ppermute x7 -> x8, waiting for transfers between devices: 98.5 us -> 52.2 us  [to_pair(): return lax.ppermute(tensor, 'pair', [(0, 1), (1, 0)])]
    psum x1 -> x0, blocking collectives: 37.6 us -> none  [per_device(): grad_norm = jnp.sqrt(lax.psum(local_squares, everywhere))]
    all_gather x2, waiting for transfers between devices: 62.4 us -> 29.8 us  [the longest x1 29.8 us: per_device(): lax.all_gather(w_first.reshape(BANDS * own_rows, 9 * OWN_COLS), 'clip', t...]
  transfers between devices with their start and end apart: 35 -> 41, of which waited for: 21 -> 18; matrix products, arithmetic and copies ran while one was open for 25% -> 72% of each run, Pallas kernels for 0% -> 0%
where the time goes in v2:
time: 1040 us
  matrix products  469 us (45%)
  local copies, waits for them, and re-layouts  235 us (23%)
  other arithmetic  166 us (16%)
  waiting for transfers between devices  105 us (10%)
  starting transfers between devices  24.9 us (2%)
  between operations  20.8 us (2%)
  blocking collectives  13.8 us (1%)
    dot_general x52, matrix products, contract_cols(): lax.dot_general(left, right, (((1,), (1,)), ((), ())), preferred_element_...  160 us
    dot_general x37, matrix products, contract_rows(): lax.dot_general(left, right, (((0,), (0,)), ((), ())), precision=precisio...  160 us
    while x224, local copies, waits for them, and re-layouts  95.4 us
    dot_general x16, matrix products, one_block(): jnp.dot(exponent.astype(jnp.bfloat16), value, preferred_element_type=jnp....  82 us
    ppermute x8, waiting for transfers between devices, to_pair(): return lax.ppermute(tensor, 'pair', [(0, 1), (1, 0)])  52.2 us
    reduce_sum x16, other arithmetic, one_block(): totals = jnp.sum(exponent, axis=1, keepdims=True)  32.9 us
    all_gather x1, waiting for transfers between devices, per_device(): lax.all_gather(w_first.reshape(BANDS * own_rows, 9 * OWN_COLS), 'clip', t...  29.8 us
    dot_general x16, matrix products, one_block(): jnp.dot(grad_scores, key, preferred_element_type=jnp.float32) * 0.125  24.9 us
  transfers between devices with their start and end apart: 41, of which 18 were waited for; matrix products, arithmetic and copies ran while one was open for 72% of the time, Pallas kernels for 0%

profile of v2, /device:TPU:0, one launch (start us, length us, event | category | flops | bytes accessed | tf_op | source)
XLA Modules:
  0.0 1036.9 jit_solution(8948956199815498291)
XLA Ops:
  10.8 13.8 %all_to_all.10 = bf16[4,32,2304]{2,1,0:T(8,128)(2,1)} all-to-all(bf16[4,32,2304]{2,1,0:T(8,128)(2,1)S(1)} %copy.134), channel_id=1, replica_groups=mesh['clip'=8,'pair'=2,'half'=2] {'pair','half'}, dimensions={0} | all-to-all | bytes 1179648 | tf_op jit(solution)/shard_map/all_to_all | solution.py:250
  29.0 36.1 %collective-permute-done.3 = bf16[768,1024]{1,0:T(8,128)(2,1)S(1)} collective-permute-done((bf16[768,1024]{1,0:T(8,128)(2,1)S(1)}, bf16[768,1024]{1,0:T(8,128)(2,1)S(1)}, u32[]{:S(2)}, u32[]{:S(2)}) %collective-permute-start.3) | collective-permute-done | bytes 1572896 | tf_op jit(solution)/shard_map/ppermute | solution.py:60
  75.6 29.8 %all-gather.7.cloned.1.call-done = bf16[1024,2304]{1,0:T(8,128)(2,1)} async-done(((bf16[128,2304]{1,0:T(8,128)(2,1)}), bf16[1024,2304]{1,0:T(8,128)(2,1)}) %all-gather.7.cloned.1.call-update) | async-done | bytes 4718608 | tf_op jit(solution)/shard_map/all_gather | solution.py:251
  110.7 5.5 collective-permute-done.1
  117.3 6.6 fusion.72
  123.8 9.4 convolution_convert_fusion
  133.3 9.6 copy.136
  142.8 6.7 fusion.129
  149.5 189.3 %while.58 = (s32[]{:T(128)}, f32[4,3072,64]{1,2,0:T(8,128)}, f32[4,4,768]{2,1,0:T(4,128)}, bf16[4,3072,64]{2,1,0:T(8,128)(2,1)}, bf16[4,3072,64]{2,1,0:T(8,128)(...) while((s32[]{:T(128)}, f32[4,3072,64]{1,2,0:T(8,128)}, ...), condition=%wide.region_7.8_spmd.clone, body=%wide.region_2.7_spmd.clone.sunk | while | flops 630048000 | bytes 75181384 | solution.py:146
  153.1 41.6 %while.61 = (s32[]{:T(128)}, f32[4,768,64]{1,2,0:T(8,128)S(1)}, f32[4,768]{1,0:T(4,128)S(1)}, pred[3072]{0:T(1024)(128)(4,1)S(1)}, bf16[4,768,64]{2,1,0:T(8,128)...) while((s32[]{:T(128)}, f32[4,768,64]{1,2,0:T(8,128)S(1)}, ...), condition=%wide.region_6.6_spmd, body=%wide.region_3.5_spmd.sunk | while | flops 629980416 | bytes 68074624 | solution.py:143
  158.3 5.2 fusion.205
  168.7 5.1 fusion.205
  179.1 5.1 fusion.205
  189.4 5.3 fusion.205
  200.6 41.3 %while.61 = (s32[]{:T(128)}, f32[4,768,64]{1,2,0:T(8,128)S(1)}, f32[4,768]{1,0:T(4,128)S(1)}, pred[3072]{0:T(1024)(128)(4,1)S(1)}, bf16[4,768,64]{2,1,0:T(8,128)...) while((s32[]{:T(128)}, f32[4,768,64]{1,2,0:T(8,128)S(1)}, ...), condition=%wide.region_6.6_spmd, body=%wide.region_3.5_spmd.sunk | while | flops 629980416 | bytes 68074624 | solution.py:143
  205.8 5.1 fusion.205
  216.1 5.1 fusion.205
  226.5 5.1 fusion.205
  236.8 5.1 fusion.205
  247.8 41.3 %while.61 = (s32[]{:T(128)}, f32[4,768,64]{1,2,0:T(8,128)S(1)}, f32[4,768]{1,0:T(4,128)S(1)}, pred[3072]{0:T(1024)(128)(4,1)S(1)}, bf16[4,768,64]{2,1,0:T(8,128)...) while((s32[]{:T(128)}, f32[4,768,64]{1,2,0:T(8,128)S(1)}, ...), condition=%wide.region_6.6_spmd, body=%wide.region_3.5_spmd.sunk | while | flops 629980416 | bytes 68074624 | solution.py:143
  253.0 5.1 fusion.205
  263.3 5.1 fusion.205
  273.7 5.1 fusion.205
  284.0 5.1 fusion.205
  295.0 41.3 %while.61 = (s32[]{:T(128)}, f32[4,768,64]{1,2,0:T(8,128)S(1)}, f32[4,768]{1,0:T(4,128)S(1)}, pred[3072]{0:T(1024)(128)(4,1)S(1)}, bf16[4,768,64]{2,1,0:T(8,128)...) while((s32[]{:T(128)}, f32[4,768,64]{1,2,0:T(8,128)S(1)}, ...), condition=%wide.region_6.6_spmd, body=%wide.region_3.5_spmd.sunk | while | flops 629980416 | bytes 68074624 | solution.py:143
  300.2 5.1 fusion.205
  320.8 5.1 fusion.205
  331.2 5.1 fusion.205
  354.0 6.6 collective-permute-done.7
  361.5 7.1 fusion.127
  380.7 12.1 %fusion.79 = f32[1536,2048]{1,0:T(8,128)} fusion(bf16[1024,2048]{1,0:T(8,128)(2,1)} %all-gather.11.cloned.1.call-done, bf16[768,1024]{1,0:T(8,128)(2,1)} %collective-permute-done.8, bf16[768,1024]{1,0:T(8,128)(2,1)} %bitcast.35), kind=kOutput, calls=%fused_computation.153 | convolution fusion | flops 6448742400 | bytes 19922944 | tf_op jit(solution)/shard_map/dot_general | solution.py:295
  392.8 11.5 %fusion.116 = f32[1536,1024]{1,0:T(8,128)S(1)} fusion(bf16[2048,1024]{1,0:T(8,128)(2,1)} %all-gather.13.cloned.1.call-done, f32[1536,2048]{1,0:T(8,128)} %fusion.79), kind=kOutput, calls=%fused_computation.261 | convolution fusion | flops 6470762496 | bytes 23068672 | tf_op jit(solution)/shard_map/dot_general | solution.py:318
  404.9 20.0 %fusion.71 = bf16[1536,2048]{1,0:T(8,128)(2,1)} fusion(f32[1536,2048]{1,0:T(8,128)} %fusion.79, bf16[2048,1024]{1,0:T(8,128)(2,1)} %all-gather.13.cloned.1.call-done, bf16[768,1024]{1,0:T(8,128)(2,1)} %collective-permute-done.11, bf16[768,1024]{1,0:T(8,128)(2,1)} %fusion.76), kind=kOutput, calls=%fused_computation.98 | convolution fusion | flops 6511656960 | bytes 26214400 | tf_op jit(solution)/shard_map/dot_general | solution.py:39
  424.9 10.1 fusion.134
  435.6 13.4 %convolution_convert_fusion.2 = bf16[2048,1024]{1,0:T(8,128)(2,1)} fusion(bf16[768,1024]{1,0:T(8,128)(2,1)} %collective-permute-done.11, bf16[768,1024]{1,0:T(8,128)(2,1)} %fusion.76, f32[1536,2048]{1,0:T(8,128)} %fusion.79), kind=kOutput, calls=%fused_computation.117 | convolution fusion | flops 6479151104 | bytes 19922944 | tf_op jit(solution)/shard_map/dot_general | solution.py:29
  475.3 11.8 %convolution_convert_fusion.1 = bf16[1024,2048]{1,0:T(8,128)(2,1)} fusion(bf16[1536,2048]{1,0:T(8,128)(2,1)} %fusion.71, bf16[768,1024]{1,0:T(8,128)(2,1)} %collective-permute-done.8, bf16[768,1024]{1,0:T(8,128)(2,1)} %bitcast.35), kind=kOutput, calls=%fused_computation.116 | convolution fusion | flops 6450839552 | bytes 13631488 | tf_op jit(solution)/shard_map/dot_general | solution.py:29
  487.1 7.8 reshape.480
  494.9 5.6 copy.148
  513.8 6.6 pad_maximum_fusion
  520.4 367.1 %while.60 = (s32[]{:T(128)}, bf16[4,3072,64]{1,2,0:T(8,128)(2,1)}, bf16[4,3072,64]{1,2,0:T(8,128)(2,1)}, bf16[4,3072,64]{1,2,0:T(8,128)(2,1)}, bf16[4,3072,64]{2...) while((s32[]{:T(128)}, bf16[4,3072,64]{1,2,0:T(8,128)(2,1)}, ...), condition=%wide.region_16.17_spmd.clone, body=%wide.region_13.16_spmd.clone.sunk | while | flops 1535084544 | bytes 153562224 | solution.py:186
  528.2 80.6 %while.62 = (s32[]{:T(128)}, f32[3072,64]{0,1:T(8,128)S(1)}, f32[3072,64]{0,1:T(8,128)}, bf16[4,768,64]{1,2,0:T(8,128)(2,1)S(1)}, pred[3072]{0:T(1024)(128)(4,1)...) while((s32[]{:T(128)}, f32[3072,64]{0,1:T(8,128)S(1)}, ...), condition=%wide.region_15.15_spmd.clone, body=%wide.region_14.14_spmd.clone.sunk | while | flops 1534623744 | bytes 144857424 | solution.py:177
  620.4 80.7 %while.62 = (s32[]{:T(128)}, f32[3072,64]{0,1:T(8,128)S(1)}, f32[3072,64]{0,1:T(8,128)}, bf16[4,768,64]{1,2,0:T(8,128)(2,1)S(1)}, pred[3072]{0:T(1024)(128)(4,1)...) while((s32[]{:T(128)}, f32[3072,64]{0,1:T(8,128)S(1)}, ...), condition=%wide.region_15.15_spmd.clone, body=%wide.region_14.14_spmd.clone.sunk | while | flops 1534623744 | bytes 144857424 | solution.py:177
  712.9 79.4 %while.62 = (s32[]{:T(128)}, f32[3072,64]{0,1:T(8,128)S(1)}, f32[3072,64]{0,1:T(8,128)}, bf16[4,768,64]{1,2,0:T(8,128)(2,1)S(1)}, pred[3072]{0:T(1024)(128)(4,1)...) while((s32[]{:T(128)}, f32[3072,64]{0,1:T(8,128)S(1)}, ...), condition=%wide.region_15.15_spmd.clone, body=%wide.region_14.14_spmd.clone.sunk | while | flops 1534623744 | bytes 144857424 | solution.py:177
  804.0 79.4 %while.62 = (s32[]{:T(128)}, f32[3072,64]{0,1:T(8,128)S(1)}, f32[3072,64]{0,1:T(8,128)}, bf16[4,768,64]{1,2,0:T(8,128)(2,1)S(1)}, pred[3072]{0:T(1024)(128)(4,1)...) while((s32[]{:T(128)}, f32[3072,64]{0,1:T(8,128)S(1)}, ...), condition=%wide.region_15.15_spmd.clone, body=%wide.region_14.14_spmd.clone.sunk | while | flops 1534623744 | bytes 144857424 | solution.py:177
  891.5 9.5 convolution_convert_fusion.3
  901.1 10.9 %fusion.88 = f32[3072,1024]{1,0:T(8,128)} fusion(bf16[3072,768]{0,1:T(8,128)(2,1)} %pad_maximum_fusion.2, bf16[1024,2304]{1,0:T(8,128)(2,1)} %all-gather.7.cloned.1.call-done), kind=kOutput, calls=%fused_computation.170 | convolution fusion | flops 4831838208 | bytes 18874368 | tf_op jit(solution)/shard_map/dot_general | solution.py:39
  911.9 5.6 convert_element_type.219
  920.6 7.1 fusion.117
  (837 shorter events, 674.3 us)
Async XLA Ops:
  7.2 98.2 %all-gather.7.cloned.1.call-start = ((), (), s32[]{:S(2)}) async-start(), calls=%async_computation.4 | async-start | bytes 5308416 | tf_op jit(solution)/shard_map/all_gather | solution.py:251
  8.9 16.5 %copy-start.20 = (f32[32,4096]{1,0:T(8,128)S(1)}, f32[32,4096]{1,0:T(8,128)}, u32[]{:S(2)}) copy-start(f32[32,4096]{1,0:T(8,128)} %param.33) | copy-start | bytes 1572868
  10.8 17.8 %copy-start.4 = (bf16[1,768,1024]{2,1,0:T(8,128)(2,1)S(1)}, bf16[1,768,1024]{2,1,0:T(8,128)(2,1)}, u32[]{:S(2)}) copy-start(bf16[1,768,1024]{2,1,0:T(8,128)(2,1)} %param.27) | copy-start | bytes 4718596
  24.6 43.0 %copy-start.65 = (s32[1,12]{1,0:T(1,128)S(1)}, s32[1,12]{1,0:T(1,128)}, u32[]{:S(2)}) copy-start(s32[1,12]{1,0:T(1,128)} %param.30) | copy-start | bytes 148
  24.6 318.3 %all-gather.9.cloned.1.call-start = ((), (), s32[]{:S(2)}) async-start(), calls=%async_computation.5 | async-start | bytes 2162688 | tf_op jit(solution)/shard_map/all_gather | solution.py:270
  25.4 355.3 %all-gather.11.cloned.1.call-start = ((), (), s32[]{:S(2)}) async-start(), calls=%async_computation.6 | async-start | bytes 4456448 | tf_op jit(solution)/shard_map/all_gather | solution.py:268
  26.3 1.4 collective-permute-start.9
  28.6 364.3 %all-gather.13.cloned.1.call-start = ((), (), s32[]{:S(2)}) async-start(), calls=%async_computation.7 | async-start | bytes 4456448 | tf_op jit(solution)/shard_map/all_gather | solution.py:269
  28.6 36.5 %collective-permute-start.3 = (bf16[768,1024]{1,0:T(8,128)(2,1)S(1)}, bf16[768,1024]{1,0:T(8,128)(2,1)S(1)}, u32[]{:S(2)}, u32[]{:S(2)}) collective-permute-start(bf16[768,1024]{1,0:T(8,128)(2,1)S(1)} %bitcast.279), channel_id=1, source_target_pairs={{0,2},{2,0},{1,3},{3,1},{4,6},{6,4},{5,7},{7,5},{8,10},{10,8},{9,1... | collective-permute-start | bytes 4718600 | tf_op jit(solution)/shard_map/ppermute | solution.py:60
  29.0 38.8 %collective-permute-start.2 = (bf16[768,1024]{1,0:T(8,128)(2,1)S(1)}, bf16[768,1024]{1,0:T(8,128)(2,1)}, u32[]{:S(2)}, u32[]{:S(2)}) collective-permute-start(bf16[768,1024]{1,0:T(8,128)(2,1)S(1)} %bitcast.280), channel_id=1, source_target_pairs={{0,1},{1,0},{2,3},{3,2},{4,5},{5,4},{6,7},{7,6},{8,9},{9,8},{10,11... | collective-permute-start | bytes 4718600 | tf_op jit(solution)/shard_map/ppermute | solution.py:56
  65.1 52.1 %copy-start.9 = (bf16[768,1024]{1,0:T(8,128)(2,1)}, bf16[768,1024]{1,0:T(8,128)(2,1)S(1)}, u32[]{:S(2)}) copy-start(bf16[768,1024]{1,0:T(8,128)(2,1)S(1)} %collective-permute-done.3) | copy-start | bytes 4718596
  65.1 3.5 collective-permute-start.4
  67.3 824.2 %all-gather.15.cloned.1.call-start = ((), (), s32[]{:S(2)}) async-start(), calls=%async_computation.10 | async-start | bytes 2359296 | tf_op jit(solution)/shard_map/all_gather | solution.py:356
  67.8 37.5 %copy-start.57 = (f32[12,512]{1,0:T(8,128)}, f32[12,512]{1,0:T(8,128)S(1)}, u32[]{:S(2)}) copy-start(f32[12,512]{1,0:T(8,128)S(1)} %get-tuple-element.512) | copy-start | bytes 73732
  67.8 37.5 %copy-start.58 = (f32[12,512]{1,0:T(8,128)}, f32[12,512]{1,0:T(8,128)S(1)}, u32[]{:S(2)}) copy-start(f32[12,512]{1,0:T(8,128)S(1)} %get-tuple-element.513) | copy-start | bytes 73732
  71.8 36.0 %copy-start.42 = (f32[4,12,64]{2,1,0:T(8,128)}, f32[4,12,64]{2,1,0:T(8,128)S(1)}, u32[]{:S(2)}) copy-start(f32[4,12,64]{2,1,0:T(8,128)S(1)} %broadcast_multiply_fusion) | copy-start | bytes 36868
  107.8 1.3 collective-permute-start
  109.1 7.0 collective-permute-start.1
  341.0 9.3 collective-permute-start.5
  341.1 12.0 %collective-permute-start.6 = (bf16[768,256]{0,1:T(8,128)(2,1)S(1)}, bf16[768,256]{0,1:T(8,128)(2,1)S(1)}, u32[]{:S(2)}, u32[]{:S(2)}) collective-permute-start(bf16[768,256]{0,1:T(8,128)(2,1)S(1)} %bitcast.339), channel_id=1, source_target_pairs={{0,2},{2,0},{1,3},{3,1},{4,6},{6,4},{5,7},{7,5},{8,10},{10,8},{9,1... | collective-permute-start | bytes 1179656 | tf_op jit(solution)/shard_map/ppermute | solution.py:60
  342.7 17.9 %collective-permute-start.7 = (bf16[768,256]{0,1:T(8,128)(2,1)S(1)}, bf16[768,256]{0,1:T(8,128)(2,1)S(1)}, u32[]{:S(2)}, u32[]{:S(2)}) collective-permute-start(bf16[768,256]{0,1:T(8,128)(2,1)S(1)} %bitcast.338), channel_id=1, source_target_pairs={{0,3},{1,2},{2,1},{3,0},{4,7},{5,6},{6,5},{7,4},{8,11},{9,10},{10,... | collective-permute-start | bytes 1179656 | tf_op jit(solution)/shard_map/ppermute | solution.py:64
  371.6 9.1 collective-permute-start.8
  379.2 25.7 %collective-permute-start.11 = (bf16[768,1024]{1,0:T(8,128)(2,1)}, bf16[768,1024]{1,0:T(8,128)(2,1)}, u32[]{:S(2)}, u32[]{:S(2)}) collective-permute-start(bf16[768,1024]{1,0:T(8,128)(2,1)} %fusion.76), channel_id=1, source_target_pairs={{0,1},{1,0},{2,3},{3,2},{4,5},{5,4},{6,7},{7,6},{8,9},{9,8},{10,11... | collective-permute-start | bytes 4718600 | tf_op jit(solution)/shard_map/ppermute | solution.py:56
  404.5 50.4 %collective-permute-start.10 = (bf16[768,1024]{1,0:T(8,128)(2,1)S(1)}, bf16[768,1024]{1,0:T(8,128)(2,1)S(1)}, u32[]{:S(2)}, u32[]{:S(2)}) collective-permute-start(bf16[768,1024]{1,0:T(8,128)(2,1)S(1)} %slice.196), channel_id=1, source_target_pairs={{0,1},{1,0},{2,3},{3,2},{4,5},{5,4},{6,7},{7,6},{8,9},{9,8},{10,11... | collective-permute-start | bytes 4718600 | tf_op jit(solution)/shard_map/ppermute | solution.py:56
  435.2 13.7 %collective-permute-start.12 = (bf16[768,1024]{1,0:T(8,128)(2,1)S(1)}, bf16[768,1024]{1,0:T(8,128)(2,1)S(1)}, u32[]{:S(2)}, u32[]{:S(2)}) collective-permute-start(bf16[768,1024]{1,0:T(8,128)(2,1)S(1)} %slice.195), channel_id=1, source_target_pairs={{0,1},{1,0},{2,3},{3,2},{4,5},{5,4},{6,7},{7,6},{8,9},{9,8},{10,11... | collective-permute-start | bytes 4718600 | tf_op jit(solution)/shard_map/ppermute | solution.py:56
  458.3 6.3 collective-permute-start.17
  464.3 45.7 %collective-permute-start.16 = (bf16[16,32,1024]{2,1,0:T(8,128)(2,1)}, bf16[16,32,1024]{2,1,0:T(8,128)(2,1)}, u32[]{:S(2)}, u32[]{:S(2)}) collective-permute-start(bf16[16,32,1024]{2,1,0:T(8,128)(2,1)} %fusion.91), channel_id=1, source_target_pairs={{0,1},{1,0},{2,3},{3,2},{4,5},{5,4},{6,7},{7,6},{8,9},{9,8},{10,11... | collective-permute-start | bytes 3145736 | tf_op jit(solution)/shard_map/ppermute | solution.py:56
  464.6 7.1 collective-permute-start.18
  472.6 418.9 %reduce-scatter.3.cloned.1.call-start = ((), (), s32[]{:S(2)}) async-start(), calls=%async_computation.8 | async-start | bytes 10027008 | tf_op jit(solution)/shard_map/reduce_scatter | solution.py:347
  473.5 27.1 %collective-permute-start.13 = (bf16[768,256]{1,0:T(8,128)(2,1)}, bf16[768,256]{1,0:T(8,128)(2,1)S(1)}, u32[]{:S(2)}, u32[]{:S(2)}) collective-permute-start(bf16[768,256]{1,0:T(8,128)(2,1)} %get-tuple-element.495), channel_id=1, source_target_pairs={{0,1},{1,0},{2,3},{3,2},{4,5},{5,4},{6,7},{7,6},{8,9},{9,8},{10,11... | collective-permute-start | bytes 1179656 | tf_op jit(solution)/shard_map/ppermute | solution.py:56
  473.5 27.1 %collective-permute-start.14 = (bf16[768,256]{1,0:T(8,128)(2,1)S(1)}, bf16[768,256]{1,0:T(8,128)(2,1)S(1)}, u32[]{:S(2)}, u32[]{:S(2)}) collective-permute-start(bf16[768,256]{1,0:T(8,128)(2,1)S(1)} %get-tuple-element.494), channel_id=1, source_target_pairs={{0,2},{2,0},{1,3},{3,1},{4,6},{6,4},{5,7},{7,5},{8,10},{10,8},{9,1... | collective-permute-start | bytes 1179656 | tf_op jit(solution)/shard_map/ppermute | solution.py:60
  475.0 25.6 %collective-permute-start.15 = (bf16[768,256]{1,0:T(8,128)(2,1)S(1)}, bf16[768,256]{1,0:T(8,128)(2,1)S(1)}, u32[]{:S(2)}, u32[]{:S(2)}) collective-permute-start(bf16[768,256]{1,0:T(8,128)(2,1)S(1)} %get-tuple-element.493), channel_id=1, source_target_pairs={{0,3},{1,2},{2,1},{3,0},{4,7},{5,6},{6,5},{7,4},{8,11},{9,10},{10,... | collective-permute-start | bytes 1179656 | tf_op jit(solution)/shard_map/ppermute | solution.py:64
  520.4 461.7 %reduce-scatter.5.cloned.1.call-start = ((), (), s32[]{:S(2)}) async-start(), calls=%async_computation.9 | async-start | bytes 1769472 | tf_op jit(solution)/shard_map/reduce_scatter | solution.py:361
  919.6 20.7 %collective-permute-start.20 = (bf16[12,64,1024]{2,1,0:T(8,128)(2,1)}, bf16[12,64,1024]{2,1,0:T(8,128)(2,1)}, u32[]{:S(2)}, u32[]{:S(2)}) collective-permute-start(bf16[12,64,1024]{2,1,0:T(8,128)(2,1)} %get-tuple-element.489), channel_id=1, source_target_pairs={{0,1},{1,0},{2,3},{3,2},{4,5},{5,4},{6,7},{7,6},{8,9},{9,8},{10,11... | collective-permute-start | bytes 4718600 | tf_op jit(solution)/shard_map/ppermute | solution.py:56
  927.7 1.6 collective-permute-start.23
  929.3 5.1 collective-permute-start.24
  934.5 4.7 collective-permute-start.25
  938.8 56.4 %collective-permute-start.19 = (bf16[12,64,1024]{2,1,0:T(8,128)(2,1)}, bf16[12,64,1024]{2,1,0:T(8,128)(2,1)}, u32[]{:S(2)}, u32[]{:S(2)}) collective-permute-start(bf16[12,64,1024]{2,1,0:T(8,128)(2,1)} %get-tuple-element.488), channel_id=1, source_target_pairs={{0,1},{1,0},{2,3},{3,2},{4,5},{5,4},{6,7},{7,6},{8,9},{9,8},{10,11... | collective-permute-start | bytes 4718600 | tf_op jit(solution)/shard_map/ppermute | solution.py:56
  939.2 7.2 collective-permute-start.26
  943.5 51.7 %collective-permute-start.21 = (bf16[12,64,1024]{2,1,0:T(8,128)(2,1)}, bf16[12,64,1024]{2,1,0:T(8,128)(2,1)}, u32[]{:S(2)}, u32[]{:S(2)}) collective-permute-start(bf16[12,64,1024]{2,1,0:T(8,128)(2,1)} %add_convert_fusion), channel_id=1, source_target_pairs={{0,2},{2,0},{1,3},{3,1},{4,6},{6,4},{5,7},{7,5},{8,10},{10,8},{9,1... | collective-permute-start | bytes 4718600 | tf_op jit(solution)/shard_map/ppermute | solution.py:60
  947.7 25.8 %collective-permute-start.27 = (f32[96,1024]{1,0:T(8,128)S(1)}, f32[96,1024]{1,0:T(8,128)}, u32[]{:S(2)}, u32[]{:S(2)}) collective-permute-start(f32[96,1024]{1,0:T(8,128)S(1)} %maximum_select_fusion.2), channel_id=1, source_target_pairs={{0,16},{4,20},{8,24},{12,28},{16,0},{20,4},{24,8},{28,12},{1,17},{... | collective-permute-start | bytes 1179656 | tf_op jit(solution)/shard_map/ppermute | solution.py:73
  959.0 6.5 collective-permute-start.22
  982.1 9.0 all-to-all-start.1
  995.1 4.0 collective-permute-start.28
  999.1 3.7 collective-permute-start.29
  1002.8 5.0 collective-permute-start.30
  1007.9 3.7 collective-permute-start.31
  1011.5 4.5 collective-permute-start.32
  (164 other events, 736.3 us)
Sparse Core Ops, SparseCore 0:
  24.8 80.5 all-gather.6
  108.8 54.5 all-gather.8
  166.7 74.5 all-gather.10
  244.5 74.5 all-gather.12
  472.7 47.7 all-gather.14
  526.1 169.5 reduce-scatter.2
  901.2 73.1 reduce-scatter.4

commit v3 on v2

--- a/solution.py
+++ b/solution.py
@@ -12,6 +12,7 @@
 FRAMES = 12
 STEP = 10
 BANDS = 4
+PARTS = 8
 OWN_COLS = D // BANDS
 LANES = 128
 
@@ -140,7 +141,7 @@
             )
             return outcome / totals, (maxima + jnp.log(totals))[:, 0]
 
-        outcome, logs = lax.map(one_block, query.reshape(BANDS, local_rows, HEAD_DIM))
+        outcome, logs = lax.map(one_block, query.reshape(PARTS, rows // PARTS, HEAD_DIM))
         return outcome.reshape(rows, HEAD_DIM), logs
 
     outcome, logs = lax.map(one_head, (heads[0], heads[1], heads[2]))
@@ -173,7 +174,7 @@
             return (key_sum, value_sum), grad_query.astype(jnp.bfloat16)
 
         zero = jnp.zeros((rows, HEAD_DIM), jnp.float32)
-        split = (BANDS, local_rows, HEAD_DIM)
+        split = (PARTS, rows // PARTS, HEAD_DIM)
         (key_sum, value_sum), grad_query = lax.scan(
             one_block, (zero, zero), (query.reshape(split), log_head, delta_head, grad.reshape(split))
         )
@@ -260,15 +261,23 @@
         modulation.reshape(FRAMES, 6 * D), 6, axis=1
     )
 
+    groups = clips * (BANDS // 2)
+    down_rows = down_master.shape[0]
     up_low = up_master.astype(jnp.bfloat16).reshape(own_rows, up_groups, 2, LANES)
-    mine = jnp.where(half == 0, up_low[:, :, 0], up_low[:, :, 1])
-    other = to_half(jnp.where(half == 0, up_low[:, :, 1], up_low[:, :, 0]))
-    up_low = jnp.where(half == 0, jnp.stack([mine, other]), jnp.stack([other, mine]))
-    up_low = up_low.reshape(2 * own_rows, FF // 2)
-    w_up = lax.all_gather(up_low, ("clip", "pair"), tiled=True)
-    w_down = lax.all_gather(down_master.astype(jnp.bfloat16), ("clip", "pair"), tiled=True)
-    w_out = lax.all_gather(out_master.astype(jnp.bfloat16), everywhere, tiled=True)
+    mine = jnp.where(half == 0, up_low[:, :, 0], up_low[:, :, 1]).reshape(own_rows, FF // 2)
+    other = jnp.where(half == 0, up_low[:, :, 1], up_low[:, :, 0]).reshape(own_rows, FF // 2)
+    up_low = in_order(mine, to_half(other), half).reshape(2, own_rows, 2, D)
+    up_low = up_low.transpose(0, 2, 1, 3).reshape(4 * own_rows, D)
+    w_rest = jnp.concatenate(
+        [down_master.astype(jnp.bfloat16), up_low, out_master.astype(jnp.bfloat16)]
+    )
+    w_rest = lax.all_gather(w_rest, ("clip", "pair"))
+    w_out = w_rest[:, down_rows + 4 * own_rows :]
+    w_out = in_order(w_out, to_half(w_out), half, axis=1)
     w_out = relative_order(w_out.reshape(BANDS, OWN_COLS, D), pair, half).reshape(D, D)
+    w_down = w_rest[:, :down_rows].reshape(FF // 2, D)
+    w_up = w_rest[:, down_rows : down_rows + 4 * own_rows].reshape(groups, 2, 2, own_rows, D)
+    w_up = w_up.transpose(0, 1, 3, 2, 4).reshape(D, FF // 2)
 
     wide = clip_tokens.astype(jnp.float32).reshape(BANDS, FRAMES, frame_rows, D)
     normed = normalize(wide)
@@ -324,8 +333,6 @@
         (middle + gate_two[:, None, :] * branch_two).astype(jnp.bfloat16).reshape(1, local_rows, D)
     )
     grad_gate_two = jnp.sum(upstream * branch_two, axis=1)
-    groups = clips * (BANDS // 2)
-    down_rows = down_master.shape[0]
     grad_down = contract_rows(hidden, grad_branch_both).astype(jnp.bfloat16)
     grad_up = contract_rows(second_both, grad_pre).astype(jnp.bfloat16)
     grad_out = contract_rows(attended, grad_branch_one)

time: 1040 us -> 1260 us (1.21)
  matrix products: 469 us -> 601 us
  local copies, waits for them, and re-layouts: 235 us -> 327 us
    dot_general x16 -> x32, matrix products: 24.9 us -> 82.4 us  [one_block(): jnp.dot(grad_scores, key, preferred_element_type=jnp.float32) * 0.125]
    dot_general x37 -> x69, matrix products: 160 us -> 216 us  [contract_rows(): lax.dot_general(left, right, (((0,), (0,)), ((), ())), precision=precisio...]
    while x228 -> x476, local copies, waits for them, and re-layouts: 97.3 us -> 146 us
    dot_general x16 -> x32, matrix products: 82 us -> 104 us  [one_block(): jnp.dot(exponent.astype(jnp.bfloat16), value, preferred_element_type=jnp....]
    reduce_sum x16 -> x32, other arithmetic: 32.9 us -> 24.7 us  [one_block(): totals = jnp.sum(exponent, axis=1, keepdims=True)]
    dot_general x52 -> x100, matrix products: 160 us -> 160 us  [contract_cols(): lax.dot_general(left, right, (((1,), (1,)), ((), ())), preferred_element_...]
  transfers between devices with their start and end apart: 41 -> 40, of which waited for: 18 -> 16; matrix products, arithmetic and copies ran while one was open for 72% -> 71% of each run, Pallas kernels for 0% -> 0%
where the time goes in v3:
time: 1260 us; the launch traced here: 1250 us
  matrix products  601 us (48%)
  local copies, waits for them, and re-layouts  327 us (26%)
  other arithmetic  156 us (12%)
  waiting for transfers between devices  103 us (8%)
  starting transfers between devices  24.3 us (2%)
  between operations  20.4 us (2%)
  blocking collectives  13.7 us (1%)
    dot_general x69, matrix products, contract_rows(): lax.dot_general(left, right, (((0,), (0,)), ((), ())), precision=precisio...  216 us
    dot_general x100, matrix products, contract_cols(): lax.dot_general(left, right, (((1,), (1,)), ((), ())), preferred_element_...  160 us
    while x472, local copies, waits for them, and re-layouts  144 us
    dot_general x32, matrix products, one_block(): jnp.dot(exponent.astype(jnp.bfloat16), value, preferred_element_type=jnp....  104 us
    dot_general x32, matrix products, one_block(): jnp.dot(grad_scores, key, preferred_element_type=jnp.float32) * 0.125  82.4 us
    ppermute x8, waiting for transfers between devices, to_pair(): return lax.ppermute(tensor, 'pair', [(0, 1), (1, 0)])  57.4 us
  transfers between devices with their start and end apart: 40, of which 16 were waited for; matrix products, arithmetic and copies ran while one was open for 71% of the time, Pallas kernels for 0%

profile of v3, /device:TPU:0, one launch (start us, length us, event | category | flops | bytes accessed | tf_op | source)
XLA Modules:
  0.0 1250.3 jit_solution(17944711665345526312)
XLA Ops:
  10.8 13.7 %all_to_all.10 = bf16[4,32,2304]{2,1,0:T(8,128)(2,1)} all-to-all(bf16[4,32,2304]{2,1,0:T(8,128)(2,1)S(1)} %copy.110), channel_id=1, replica_groups=mesh['clip'=8,'pair'=2,'half'=2] {'pair','half'}, dimensions={0} | all-to-all | bytes 1179648 | tf_op jit(solution)/shard_map/all_to_all | solution.py:251
  25.0 35.7 %collective-permute-done.3 = bf16[768,1024]{1,0:T(8,128)(2,1)S(1)} collective-permute-done((bf16[768,1024]{1,0:T(8,128)(2,1)S(1)}, bf16[768,1024]{1,0:T(8,128)(2,1)S(1)}, u32[]{:S(2)}, u32[]{:S(2)}) %collective-permute-start.3) | collective-permute-done | bytes 1572896 | tf_op jit(solution)/shard_map/ppermute | solution.py:61
  77.2 3.8 multiply_reduce_fusion.1
  81.0 24.2 %all-gather.6.cloned.1.call-done = bf16[1024,2304]{1,0:T(8,128)(2,1)} async-done(((bf16[128,2304]{1,0:T(8,128)(2,1)}), bf16[1024,2304]{1,0:T(8,128)(2,1)}) %all-gather.6.cloned.1.call-update) | async-done | bytes 4718608 | tf_op jit(solution)/shard_map/all_gather | solution.py:252
  110.6 5.5 collective-permute-done.1
  117.2 6.6 fusion.59
  123.8 9.5 convolution_convert_fusion
  133.3 9.6 copy.112
  142.9 6.9 fusion.119
  149.8 258.3 %while.58 = (s32[]{:T(128)}, f32[4,3072,64]{1,2,0:T(8,128)}, f32[4,8,384]{2,1,0:T(8,128)}, bf16[4,3072,64]{2,1,0:T(8,128)(2,1)}, bf16[4,3072,64]{2,1,0:T(8,128)(...) while((s32[]{:T(128)}, f32[4,3072,64]{1,2,0:T(8,128)}, ...), condition=%wide.region_7.8_spmd.clone, body=%wide.region_2.7_spmd.clone.sunk | while | flops 310339200 | bytes 41929036 | solution.py:147
  153.3 59.6 %while.61 = (s32[]{:T(128)}, f32[8,384,64]{1,2,0:T(8,128)S(1)}, f32[8,384]{1,0:T(8,128)S(1)}, pred[3072]{0:T(1024)(128)(4,1)S(1)}, bf16[8,384,64]{2,1,0:T(8,128)...) while((s32[]{:T(128)}, f32[8,384,64]{1,2,0:T(8,128)S(1)}, ...), condition=%wide.region_6.6_spmd, body=%wide.region_3.5_spmd.sunk | while | flops 310271616 | bytes 34822276 | solution.py:144
  172.0 4.2 fusion.192
  209.6 3.3 fusion.192
  218.7 58.4 %while.61 = (s32[]{:T(128)}, f32[8,384,64]{1,2,0:T(8,128)S(1)}, f32[8,384]{1,0:T(8,128)S(1)}, pred[3072]{0:T(1024)(128)(4,1)S(1)}, bf16[8,384,64]{2,1,0:T(8,128)...) while((s32[]{:T(128)}, f32[8,384,64]{1,2,0:T(8,128)S(1)}, ...), condition=%wide.region_6.6_spmd, body=%wide.region_3.5_spmd.sunk | while | flops 310271616 | bytes 34822276 | solution.py:144
  283.0 58.4 %while.61 = (s32[]{:T(128)}, f32[8,384,64]{1,2,0:T(8,128)S(1)}, f32[8,384]{1,0:T(8,128)S(1)}, pred[3072]{0:T(1024)(128)(4,1)S(1)}, bf16[8,384,64]{2,1,0:T(8,128)...) while((s32[]{:T(128)}, f32[8,384,64]{1,2,0:T(8,128)S(1)}, ...), condition=%wide.region_6.6_spmd, body=%wide.region_3.5_spmd.sunk | while | flops 310271616 | bytes 34822276 | solution.py:144
  347.2 58.4 %while.61 = (s32[]{:T(128)}, f32[8,384,64]{1,2,0:T(8,128)S(1)}, f32[8,384]{1,0:T(8,128)S(1)}, pred[3072]{0:T(1024)(128)(4,1)S(1)}, bf16[8,384,64]{2,1,0:T(8,128)...) while((s32[]{:T(128)}, f32[8,384,64]{1,2,0:T(8,128)S(1)}, ...), condition=%wide.region_6.6_spmd, body=%wide.region_3.5_spmd.sunk | while | flops 310271616 | bytes 34822276 | solution.py:144
  417.2 7.8 collective-permute-done.6
  425.9 5.8 collective-permute-done.7
  437.9 4.7 fusion.115
  452.8 6.5 fusion.118
  459.4 8.6 copy.122
  467.9 3.6 copy.172
  471.6 11.6 fusion.66
  483.2 10.2 fusion.104
  497.8 18.5 %fusion.58 = bf16[1536,2048]{1,0:T(8,128)(2,1)} fusion(f32[1536,2048]{1,0:T(8,128)} %fusion.66, bf16[2048,1024]{1,0:T(8,128)(2,1)S(1)} %bitcast.334, bf16[768,1024]{1,0:T(8,128)(2,1)} %collective-permute-done.12, bf16[768,1024]{1,0:T(8,128)(2,1)S(1)} %fusion.63), kind=kOutput, calls=%fused_computation.89 | convolution fusion | flops 6511656960 | bytes 26214400 | tf_op jit(solution)/shard_map/dot_general | solution.py:40
  516.3 8.9 fusion.125
  525.7 12.9 %convolution_convert_fusion.2 = bf16[2048,1024]{1,0:T(8,128)(2,1)} fusion(bf16[768,1024]{1,0:T(8,128)(2,1)} %collective-permute-done.12, bf16[768,1024]{1,0:T(8,128)(2,1)S(1)} %copy-done.38, f32[1536,2048]{1,0:T(8,128)} %fusion.66), kind=kOutput, calls=%fused_computation.108 | convolution fusion | flops 6479151104 | bytes 19922944 | tf_op jit(solution)/shard_map/dot_general | solution.py:30
  559.7 3.5 collective-permute-done.19
  566.8 11.8 convolution_convert_fusion.1
  578.6 7.8 reshape.507
  586.4 5.6 copy.129
  600.5 6.6 pad_maximum_fusion
  607.2 494.6 %while.60 = (s32[]{:T(128)}, bf16[4,3072,64]{1,2,0:T(8,128)(2,1)}, bf16[4,3072,64]{1,2,0:T(8,128)(2,1)}, bf16[4,3072,64]{1,2,0:T(8,128)(2,1)}, bf16[4,3072,64]{2...) while((s32[]{:T(128)}, bf16[4,3072,64]{1,2,0:T(8,128)(2,1)}, ...), condition=%wide.region_16.17_spmd.clone, body=%wide.region_13.16_spmd.clone.sunk | while | flops 764725248 | bytes 95276712 | solution.py:187
  613.8 111.9 %while.62 = (s32[]{:T(128)}, f32[3072,64]{0,1:T(8,128)}, f32[3072,64]{0,1:T(8,128)}, bf16[8,384,64]{1,2,0:T(8,128)(2,1)}, pred[3072]{0:T(1024)(128)(4,1)S(1)}, /...) while((s32[]{:T(128)}, f32[3072,64]{0,1:T(8,128)}, ...), condition=%wide.region_15.15_spmd.clone, body=%wide.region_14.14_spmd.clone.sunk | while | flops 764264448 | bytes 70843192 | solution.py:178
  737.7 111.7 %while.62 = (s32[]{:T(128)}, f32[3072,64]{0,1:T(8,128)}, f32[3072,64]{0,1:T(8,128)}, bf16[8,384,64]{1,2,0:T(8,128)(2,1)}, pred[3072]{0:T(1024)(128)(4,1)S(1)}, /...) while((s32[]{:T(128)}, f32[3072,64]{0,1:T(8,128)}, ...), condition=%wide.region_15.15_spmd.clone, body=%wide.region_14.14_spmd.clone.sunk | while | flops 764264448 | bytes 70843192 | solution.py:178
  861.2 111.7 %while.62 = (s32[]{:T(128)}, f32[3072,64]{0,1:T(8,128)}, f32[3072,64]{0,1:T(8,128)}, bf16[8,384,64]{1,2,0:T(8,128)(2,1)}, pred[3072]{0:T(1024)(128)(4,1)S(1)}, /...) while((s32[]{:T(128)}, f32[3072,64]{0,1:T(8,128)}, ...), condition=%wide.region_15.15_spmd.clone, body=%wide.region_14.14_spmd.clone.sunk | while | flops 764264448 | bytes 70843192 | solution.py:178
  984.7 111.7 %while.62 = (s32[]{:T(128)}, f32[3072,64]{0,1:T(8,128)}, f32[3072,64]{0,1:T(8,128)}, bf16[8,384,64]{1,2,0:T(8,128)(2,1)}, pred[3072]{0:T(1024)(128)(4,1)S(1)}, /...) while((s32[]{:T(128)}, f32[3072,64]{0,1:T(8,128)}, ...), condition=%wide.region_15.15_spmd.clone, body=%wide.region_14.14_spmd.clone.sunk | while | flops 764264448 | bytes 70843192 | solution.py:178
  1101.7 3.9 pad_maximum_fusion.2
  1105.7 9.5 convolution_convert_fusion.3
  1115.2 10.7 fusion.75
  1125.9 5.6 convert_element_type.219
  1134.6 7.2 fusion.105
  1148.9 3.5 fusion.117
  1182.1 4.6 collective-permute-done.28
  1195.4 3.7 all-to-all-start.1
  1199.2 4.5 multiply_reduce_fusion.10
  1208.6 3.9 multiply_reduce_fusion.2
  1221.8 3.6 collective-permute-done.32
  (1301 shorter events, 907.1 us)
Async XLA Ops:
  7.2 98.1 %all-gather.6.cloned.1.call-start = ((), (), s32[]{:S(2)}) async-start(), calls=%async_computation.4 | async-start | bytes 5308416 | tf_op jit(solution)/shard_map/all_gather | solution.py:252
  10.8 57.3 %copy-start.75 = (s32[1,12]{1,0:T(1,128)S(1)}, s32[1,12]{1,0:T(1,128)}, u32[]{:S(2)}) copy-start(s32[1,12]{1,0:T(1,128)} %param.30) | copy-start | bytes 148
  24.5 383.5 %all-gather.8.cloned.1.call-start = ((), (), s32[]{:S(2)}) async-start(), calls=%async_computation.7 | async-start | bytes 10027008 | tf_op jit(solution)/shard_map/all_gather | solution.py:274
  24.6 36.1 %collective-permute-start.3 = (bf16[768,1024]{1,0:T(8,128)(2,1)S(1)}, bf16[768,1024]{1,0:T(8,128)(2,1)S(1)}, u32[]{:S(2)}, u32[]{:S(2)}) collective-permute-start(bf16[768,1024]{1,0:T(8,128)(2,1)S(1)} %bitcast.293), channel_id=1, source_target_pairs={{0,2},{2,0},{1,3},{3,1},{4,6},{6,4},{5,7},{7,5},{8,10},{10,8},{9,1... | collective-permute-start | bytes 4718600 | tf_op jit(solution)/shard_map/ppermute | solution.py:61
  25.0 49.0 %collective-permute-start.2 = (bf16[768,1024]{1,0:T(8,128)(2,1)S(1)}, bf16[768,1024]{1,0:T(8,128)(2,1)}, u32[]{:S(2)}, u32[]{:S(2)}) collective-permute-start(bf16[768,1024]{1,0:T(8,128)(2,1)S(1)} %bitcast.294), channel_id=1, source_target_pairs={{0,1},{1,0},{2,3},{3,2},{4,5},{5,4},{6,7},{7,6},{8,9},{9,8},{10,11... | collective-permute-start | bytes 4718600 | tf_op jit(solution)/shard_map/ppermute | solution.py:57
  60.7 56.4 %copy-start.15 = (bf16[768,1024]{1,0:T(8,128)(2,1)}, bf16[768,1024]{1,0:T(8,128)(2,1)S(1)}, u32[]{:S(2)}) copy-start(bf16[768,1024]{1,0:T(8,128)(2,1)S(1)} %collective-permute-done.3) | copy-start | bytes 4718596
  60.7 13.3 %collective-permute-start.4 = (bf16[768,1024]{1,0:T(8,128)(2,1)S(1)}, bf16[768,1024]{1,0:T(8,128)(2,1)}, u32[]{:S(2)}, u32[]{:S(2)}) collective-permute-start(bf16[768,1024]{1,0:T(8,128)(2,1)S(1)} %collective-permute-done.3), channel_id=1, source_target_pairs={{0,1},{1,0},{2,3},{3,2},{4,5},{5,4},{6,7},{7,6},{8,9},{9,8},{10,11... | collective-permute-start | bytes 4718600 | tf_op jit(solution)/shard_map/ppermute | solution.py:57
  65.2 3.8 collective-permute-start.8
  73.8 1031.8 %all-gather.10.cloned.1.call-start = ((), (), s32[]{:S(2)}) async-start(), calls=%async_computation.8 | async-start | bytes 2359296 | tf_op jit(solution)/shard_map/all_gather | solution.py:363
  77.2 30.5 %copy-start.54 = (f32[4,12,64]{2,1,0:T(8,128)}, f32[4,12,64]{2,1,0:T(8,128)S(1)}, u32[]{:S(2)}) copy-start(f32[4,12,64]{2,1,0:T(8,128)S(1)} %broadcast_multiply_fusion) | copy-start | bytes 36868
  77.2 28.1 %copy-start.70 = (f32[12,512]{1,0:T(8,128)S(1)}, f32[12,512]{1,0:T(8,128)}, u32[]{:S(2)}) copy-start(f32[12,512]{1,0:T(8,128)} %get-tuple-element.507) | copy-start | bytes 73732
  77.2 28.1 %copy-start.71 = (f32[12,512]{1,0:T(8,128)S(1)}, f32[12,512]{1,0:T(8,128)}, u32[]{:S(2)}) copy-start(f32[12,512]{1,0:T(8,128)} %get-tuple-element.508) | copy-start | bytes 73732
  107.7 1.3 collective-permute-start
  109.0 7.0 collective-permute-start.1
  411.0 21.6 %collective-permute-start.9 = (bf16[16,32,1024]{2,1,0:T(8,128)(2,1)}, bf16[16,32,1024]{2,1,0:T(8,128)(2,1)}, u32[]{:S(2)}, u32[]{:S(2)}) collective-permute-start(bf16[16,32,1024]{2,1,0:T(8,128)(2,1)} %get-tuple-element.480), channel_id=1, source_target_pairs={{0,1},{1,0},{2,3},{3,2},{4,5},{5,4},{6,7},{7,6},{8,9},{9,8},{10,11... | collective-permute-start | bytes 3145736 | tf_op jit(solution)/shard_map/ppermute | solution.py:57
  412.3 20.4 %copy-start.24 = (bf16[16,1,32,1024]{3,2,0,1:T(8,128)(2,1)S(1)}, bf16[16,1,32,1024]{3,2,0,1:T(8,128)(2,1)}, u32[]{:S(2)}) copy-start(bf16[16,1,32,1024]{3,2,0,1:T(8,128)(2,1)} %get-tuple-element.479) | copy-start | bytes 3145732
  412.3 4.0 collective-permute-start.5
  412.8 12.2 collective-permute-start.6
  414.5 17.3 %collective-permute-start.7 = (bf16[768,256]{0,1:T(8,128)(2,1)}, bf16[768,256]{0,1:T(8,128)(2,1)S(1)}, u32[]{:S(2)}, u32[]{:S(2)}) collective-permute-start(bf16[768,256]{0,1:T(8,128)(2,1)} %bitcast.30), channel_id=1, source_target_pairs={{0,3},{1,2},{2,1},{3,0},{4,7},{5,6},{6,5},{7,4},{8,11},{9,10},{10,... | collective-permute-start | bytes 1179656 | tf_op jit(solution)/shard_map/ppermute | solution.py:65
  416.3 18.3 %copy-start.39 = (bf16[768,256]{0,1:T(8,128)(2,1)}, bf16[768,256]{0,1:T(8,128)(2,1)S(1)}, u32[]{:S(2)}) copy-start(bf16[768,256]{0,1:T(8,128)(2,1)S(1)} %collective-permute-done.5) | copy-start | bytes 1179652
  445.6 26.0 %collective-permute-start.10 = (bf16[768,1024]{1,0:T(8,128)(2,1)}, bf16[768,1024]{1,0:T(8,128)(2,1)}, u32[]{:S(2)}, u32[]{:S(2)}) collective-permute-start(bf16[768,1024]{1,0:T(8,128)(2,1)} %bitcast.40), channel_id=1, source_target_pairs={{0,1},{1,0},{2,3},{3,2},{4,5},{5,4},{6,7},{7,6},{8,9},{9,8},{10,11... | collective-permute-start | bytes 4718600 | tf_op jit(solution)/shard_map/ppermute | solution.py:57
  451.2 46.5 %copy-start.37 = (bf16[768,1024]{1,0:T(8,128)(2,1)}, bf16[768,1024]{1,0:T(8,128)(2,1)S(1)}, u32[]{:S(2)}) copy-start(bf16[768,1024]{1,0:T(8,128)(2,1)S(1)} %fusion.63) | copy-start | bytes 4718596
  451.3 46.5 %collective-permute-start.12 = (bf16[768,1024]{1,0:T(8,128)(2,1)S(1)}, bf16[768,1024]{1,0:T(8,128)(2,1)}, u32[]{:S(2)}, u32[]{:S(2)}) collective-permute-start(bf16[768,1024]{1,0:T(8,128)(2,1)S(1)} %fusion.63), channel_id=1, source_target_pairs={{0,1},{1,0},{2,3},{3,2},{4,5},{5,4},{6,7},{7,6},{8,9},{9,8},{10,11... | collective-permute-start | bytes 4718600 | tf_op jit(solution)/shard_map/ppermute | solution.py:57
  497.5 46.5 %collective-permute-start.11 = (bf16[768,1024]{1,0:T(8,128)(2,1)}, bf16[768,1024]{1,0:T(8,128)(2,1)}, u32[]{:S(2)}, u32[]{:S(2)}) collective-permute-start(bf16[768,1024]{1,0:T(8,128)(2,1)} %slice.208), channel_id=1, source_target_pairs={{0,1},{1,0},{2,3},{3,2},{4,5},{5,4},{6,7},{7,6},{8,9},{9,8},{10,11... | collective-permute-start | bytes 4718600 | tf_op jit(solution)/shard_map/ppermute | solution.py:57
  525.4 13.2 %collective-permute-start.13 = (bf16[768,1024]{1,0:T(8,128)(2,1)S(1)}, bf16[768,1024]{1,0:T(8,128)(2,1)S(1)}, u32[]{:S(2)}, u32[]{:S(2)}) collective-permute-start(bf16[768,1024]{1,0:T(8,128)(2,1)S(1)} %slice.207), channel_id=1, source_target_pairs={{0,1},{1,0},{2,3},{3,2},{4,5},{5,4},{6,7},{7,6},{8,9},{9,8},{10,11... | collective-permute-start | bytes 4718600 | tf_op jit(solution)/shard_map/ppermute | solution.py:57
  549.7 6.4 collective-permute-start.18
  555.8 42.2 %collective-permute-start.17 = (bf16[16,32,1024]{2,1,0:T(8,128)(2,1)}, bf16[16,32,1024]{2,1,0:T(8,128)(2,1)}, u32[]{:S(2)}, u32[]{:S(2)}) collective-permute-start(bf16[16,32,1024]{2,1,0:T(8,128)(2,1)} %fusion.78), channel_id=1, source_target_pairs={{0,1},{1,0},{2,3},{3,2},{4,5},{5,4},{6,7},{7,6},{8,9},{9,8},{10,11... | collective-permute-start | bytes 3145736 | tf_op jit(solution)/shard_map/ppermute | solution.py:57
  556.1 7.1 collective-permute-start.19
  564.1 541.6 %reduce-scatter.3.cloned.1.call-start = ((), (), s32[]{:S(2)}) async-start(), calls=%async_computation.5 | async-start | bytes 10027008 | tf_op jit(solution)/shard_map/reduce_scatter | solution.py:354
  565.0 27.1 %collective-permute-start.14 = (bf16[768,256]{1,0:T(8,128)(2,1)}, bf16[768,256]{1,0:T(8,128)(2,1)S(1)}, u32[]{:S(2)}, u32[]{:S(2)}) collective-permute-start(bf16[768,256]{1,0:T(8,128)(2,1)} %get-tuple-element.488), channel_id=1, source_target_pairs={{0,1},{1,0},{2,3},{3,2},{4,5},{5,4},{6,7},{7,6},{8,9},{9,8},{10,11... | collective-permute-start | bytes 1179656 | tf_op jit(solution)/shard_map/ppermute | solution.py:57
  565.0 27.1 %collective-permute-start.15 = (bf16[768,256]{1,0:T(8,128)(2,1)S(1)}, bf16[768,256]{1,0:T(8,128)(2,1)S(1)}, u32[]{:S(2)}, u32[]{:S(2)}) collective-permute-start(bf16[768,256]{1,0:T(8,128)(2,1)S(1)} %get-tuple-element.487), channel_id=1, source_target_pairs={{0,2},{2,0},{1,3},{3,1},{4,6},{6,4},{5,7},{7,5},{8,10},{10,8},{9,1... | collective-permute-start | bytes 1179656 | tf_op jit(solution)/shard_map/ppermute | solution.py:61
  566.6 25.4 %collective-permute-start.16 = (bf16[768,256]{1,0:T(8,128)(2,1)S(1)}, bf16[768,256]{1,0:T(8,128)(2,1)S(1)}, u32[]{:S(2)}, u32[]{:S(2)}) collective-permute-start(bf16[768,256]{1,0:T(8,128)(2,1)S(1)} %get-tuple-element.486), channel_id=1, source_target_pairs={{0,3},{1,2},{2,1},{3,0},{4,7},{5,6},{6,5},{7,4},{8,11},{9,10},{10,... | collective-permute-start | bytes 1179656 | tf_op jit(solution)/shard_map/ppermute | solution.py:65
  607.1 588.3 %reduce-scatter.5.cloned.1.call-start = ((), (), s32[]{:S(2)}) async-start(), calls=%async_computation.6 | async-start | bytes 1769472 | tf_op jit(solution)/shard_map/reduce_scatter | solution.py:368
  1133.5 20.1 %collective-permute-start.21 = (bf16[12,64,1024]{2,1,0:T(8,128)(2,1)}, bf16[12,64,1024]{2,1,0:T(8,128)(2,1)}, u32[]{:S(2)}, u32[]{:S(2)}) collective-permute-start(bf16[12,64,1024]{2,1,0:T(8,128)(2,1)} %get-tuple-element.482), channel_id=1, source_target_pairs={{0,1},{1,0},{2,3},{3,2},{4,5},{5,4},{6,7},{7,6},{8,9},{9,8},{10,11... | collective-permute-start | bytes 4718600 | tf_op jit(solution)/shard_map/ppermute | solution.py:57
  1141.8 1.4 collective-permute-start.24
  1143.2 5.1 collective-permute-start.25
  1148.4 4.7 collective-permute-start.26
  1152.3 56.2 %collective-permute-start.20 = (bf16[12,64,1024]{2,1,0:T(8,128)(2,1)}, bf16[12,64,1024]{2,1,0:T(8,128)(2,1)}, u32[]{:S(2)}, u32[]{:S(2)}) collective-permute-start(bf16[12,64,1024]{2,1,0:T(8,128)(2,1)} %get-tuple-element.481), channel_id=1, source_target_pairs={{0,1},{1,0},{2,3},{3,2},{4,5},{5,4},{6,7},{7,6},{8,9},{9,8},{10,11... | collective-permute-start | bytes 4718600 | tf_op jit(solution)/shard_map/ppermute | solution.py:57
  1153.1 6.8 collective-permute-start.27
  1156.9 51.7 %collective-permute-start.22 = (bf16[12,64,1024]{2,1,0:T(8,128)(2,1)}, bf16[12,64,1024]{2,1,0:T(8,128)(2,1)}, u32[]{:S(2)}, u32[]{:S(2)}) collective-permute-start(bf16[12,64,1024]{2,1,0:T(8,128)(2,1)} %add_convert_fusion), channel_id=1, source_target_pairs={{0,2},{2,0},{1,3},{3,1},{4,6},{6,4},{5,7},{7,5},{8,10},{10,8},{9,1... | collective-permute-start | bytes 4718600 | tf_op jit(solution)/shard_map/ppermute | solution.py:61
  1161.2 25.6 %collective-permute-start.28 = (f32[96,1024]{1,0:T(8,128)S(1)}, f32[96,1024]{1,0:T(8,128)}, u32[]{:S(2)}, u32[]{:S(2)}) collective-permute-start(f32[96,1024]{1,0:T(8,128)S(1)} %maximum_select_fusion.3), channel_id=1, source_target_pairs={{0,16},{4,20},{8,24},{12,28},{16,0},{20,4},{24,8},{28,12},{1,17},{... | collective-permute-start | bytes 1179656 | tf_op jit(solution)/shard_map/ppermute | solution.py:74
  1172.1 6.5 collective-permute-start.23
  1195.4 9.0 all-to-all-start.1
  1208.4 4.0 collective-permute-start.29
  1212.5 3.7 collective-permute-start.30
  1216.1 5.6 collective-permute-start.31
  1221.7 3.7 collective-permute-start.32
  1225.4 4.5 collective-permute-start.33
  (296 other events, 933.7 us)
Sparse Core Ops, SparseCore 0:
  24.7 80.5 all-gather.5
  108.6 120.5 all-gather.7
  564.2 47.5 all-gather.9
  617.3 169.9 reduce-scatter.2
  1115.3 72.2 reduce-scatter.4

commit v4 on v3

--- a/solution.py
+++ b/solution.py
@@ -12,7 +12,6 @@
 FRAMES = 12
 STEP = 10
 BANDS = 4
-PARTS = 8
 OWN_COLS = D // BANDS
 LANES = 128
 
@@ -141,8 +140,12 @@
             )
             return outcome / totals, (maxima + jnp.log(totals))[:, 0]
 
-        outcome, logs = lax.map(one_block, query.reshape(PARTS, rows // PARTS, HEAD_DIM))
-        return outcome.reshape(rows, HEAD_DIM), logs
+        parts = []
+        for part in jnp.split(query, BANDS):
+            if parts:
+                part, parts[-1] = lax.optimization_barrier((part, parts[-1]))
+            parts.append(one_block(part))
+        return jnp.concatenate([part[0] for part in parts]), jnp.stack([part[1] for part in parts])
 
     outcome, logs = lax.map(one_head, (heads[0], heads[1], heads[2]))
     return columns_of(outcome.astype(jnp.bfloat16)), (outcome, logs)
@@ -173,13 +176,17 @@
             value_sum = value_sum + contract_rows(probability.astype(jnp.bfloat16), grad_part)
             return (key_sum, value_sum), grad_query.astype(jnp.bfloat16)
 
-        zero = jnp.zeros((rows, HEAD_DIM), jnp.float32)
-        split = (PARTS, rows // PARTS, HEAD_DIM)
-        (key_sum, value_sum), grad_query = lax.scan(
-            one_block, (zero, zero), (query.reshape(split), log_head, delta_head, grad.reshape(split))
-        )
+        running = (0.0, 0.0)
+        grad_query = []
+        for place in range(BANDS):
+            part = slice(place * local_rows, (place + 1) * local_rows)
+            running, grad_part = one_block(
+                running, (query[part], log_head[place], delta_head[place], grad[part])
+            )
+            grad_query.append(grad_part)
+        key_sum, value_sum = running
         return (
-            grad_query.reshape(rows, HEAD_DIM),
+            jnp.concatenate(grad_query),
             key_sum.astype(jnp.bfloat16),
             value_sum.astype(jnp.bfloat16),
         )

time: 1260 us -> 904 us (0.72)
  local copies, waits for them, and re-layouts: 327 us -> 113 us
  matrix products: 601 us -> 409 us
  loops' own time: 4.43 us -> 29.2 us
  other arithmetic: 156 us -> 170 us
  waiting for transfers between devices: 103 us -> 117 us
    while x480 -> x24, local copies, waits for them, and re-layouts: 152 us -> 0.07 us
    dot_general x69 -> x37, matrix products: 216 us -> 133 us  [contract_rows(): lax.dot_general(left, right, (((0,), (0,)), ((), ())), precision=precisio...]
    dot_general x32 -> x16, matrix products: 104 us -> 35.1 us  [one_block(): jnp.dot(exponent.astype(jnp.bfloat16), value, preferred_element_type=jnp....]
    dot_general x32 -> x16, matrix products: 82.4 us -> 25.3 us  [one_block(): jnp.dot(grad_scores, key, preferred_element_type=jnp.float32) * 0.125]
    dynamic_slice x48 -> x0, local copies, waits for them, and re-layouts: 39.2 us -> none  [the longest x32 24.9 us: one_head(): lax.scan(one_block, (zero, zero), (query.reshape(split), log_head, delta_...]
    another operation x1, loops' own time: 0.47 us -> 28.3 us  [attend_back(): results = lax.map(one_head, (*heads, logs, deltas, grads))]
    dot_general x100 -> x52, matrix products: 160 us -> 179 us  [contract_cols(): lax.dot_general(left, right, (((1,), (1,)), ((), ())), preferred_element_...]
    dynamic_update_slice x52 -> x0, local copies, waits for them, and re-layouts: 13.9 us -> none  [the longest x12 7.99 us: attend(): outcome, logs = lax.map(one_head, (heads[0], heads[1], heads[2]))]
  transfers between devices with their start and end apart: 40 -> 40, of which waited for: 16 -> 16; matrix products, arithmetic and copies ran while one was open for 71% -> 68% of each run, Pallas kernels for 0% -> 0%
where the time goes in v4:
time: 904 us; the launch traced here: 896 us
  matrix products  409 us (45%)
  other arithmetic  170 us (19%)
  waiting for transfers between devices  117 us (13%)
  local copies, waits for them, and re-layouts  113 us (12%)
  loops' own time  29.2 us (3%)
  starting transfers between devices  24.7 us (3%)
  between operations  20.5 us (2%)
  blocking collectives  13.7 us (2%)
    dot_general x52, matrix products, contract_cols(): lax.dot_general(left, right, (((1,), (1,)), ((), ())), preferred_element_...  179 us
    dot_general x37, matrix products, contract_rows(): lax.dot_general(left, right, (((0,), (0,)), ((), ())), precision=precisio...  133 us
    ppermute x8, waiting for transfers between devices, to_pair(): return lax.ppermute(tensor, 'pair', [(0, 1), (1, 0)])  67.5 us
    dot_general x16, matrix products, one_block(): jnp.dot(exponent.astype(jnp.bfloat16), value, preferred_element_type=jnp....  35.1 us
    reduce_sum x16, other arithmetic, one_block(): totals = jnp.sum(exponent, axis=1, keepdims=True)  32.9 us
    another operation x1, loops' own time, attend_back(): results = lax.map(one_head, (*heads, logs, deltas, grads))  28.3 us
    dot_general x16, matrix products, one_block(): jnp.dot(grad_scores, key, preferred_element_type=jnp.float32) * 0.125  25.3 us
    all_gather x1, waiting for transfers between devices, per_device(): lax.all_gather(w_first.reshape(BANDS * own_rows, 9 * OWN_COLS), 'clip', t...  23.6 us
  transfers between devices with their start and end apart: 40, of which 16 were waited for; matrix products, arithmetic and copies ran while one was open for 68% of the time, Pallas kernels for 0%

profile of v4, /device:TPU:0, one launch (start us, length us, event | category | flops | bytes accessed | tf_op | source)
XLA Modules:
  0.0 896.5 jit_solution(11744041724392896622)
XLA Ops:
  10.8 13.7 %all_to_all.10 = bf16[4,32,2304]{2,1,0:T(8,128)(2,1)} all-to-all(bf16[4,32,2304]{2,1,0:T(8,128)(2,1)S(1)} %copy.99), channel_id=1, replica_groups=mesh['clip'=8,'pair'=2,'half'=2] {'pair','half'}, dimensions={0} | all-to-all | bytes 1179648 | tf_op jit(solution)/shard_map/all_to_all | solution.py:258
  25.0 35.7 %collective-permute-done.3 = bf16[768,1024]{1,0:T(8,128)(2,1)S(1)} collective-permute-done((bf16[768,1024]{1,0:T(8,128)(2,1)S(1)}, bf16[768,1024]{1,0:T(8,128)(2,1)S(1)}, u32[]{:S(2)}, u32[]{:S(2)}) %collective-permute-start.3) | collective-permute-done | bytes 1572896 | tf_op jit(solution)/shard_map/ppermute | solution.py:60
  81.7 23.6 %all-gather.6.cloned.1.call-done = bf16[1024,2304]{1,0:T(8,128)(2,1)} async-done(((bf16[128,2304]{1,0:T(8,128)(2,1)}), bf16[1024,2304]{1,0:T(8,128)(2,1)}) %all-gather.6.cloned.1.call-update) | async-done | bytes 4718608 | tf_op jit(solution)/shard_map/all_gather | solution.py:259
  110.6 5.5 collective-permute-done.1
  117.2 6.6 fusion.207
  123.8 9.4 %convolution_convert_fusion = bf16[3072,768]{0,1:T(8,128)(2,1)} fusion(bf16[3072,1024]{1,0:T(8,128)(2,1)S(1)} %fusion.207, bf16[1024,2304]{1,0:T(8,128)(2,1)} %all-gather.6.cloned.1.call-done), kind=kOutput, calls=%fused_computation.256 | convolution fusion | flops 4834197504 | bytes 12582912 | tf_op jit(solution)/shard_map/dot_general | solution.py:293
  133.2 9.6 %copy.101 = bf16[3072,12,64]{2,0,1:T(8,128)(2,1)} copy(bf16[3072,12,64]{0,2,1:T(8,128)(2,1)} %bitcast.459) | data formatting | bytes 9437184 | tf_op jit(solution)/shard_map/reshape | solution.py:112
  142.8 6.0 fusion.266
  148.7 110.2 %while.28 = (s32[]{:T(128)}, f32[4,3072,64]{1,2,0:T(8,128)}, f32[4,4,768]{2,1,0:T(4,128)S(1)}, bf16[4,3072,64]{2,1,0:T(8,128)(2,1)}, bf16[4,3072,64]{2,1,0:T(8,1...) while((s32[]{:T(128)}, f32[4,3072,64]{1,2,0:T(8,128)}, ...), condition=%wide.region_11.12_spmd.clone, body=%wide.region_2.11_spmd.clone.sunk | while | flops 2520588288 | bytes 129761512 | solution.py:150
  277.0 5.5 collective-permute-done.6
  282.5 6.5 collective-permute-done.7
  289.8 5.9 fusion.263
  313.0 6.3 fusion.265
  319.3 8.5 copy.110
  331.4 8.9 fusion.214
  340.4 10.0 %fusion.252 = f32[1536,1024]{1,0:T(8,128)} fusion(bf16[2048,1024]{1,0:T(8,128)(2,1)S(1)} %bitcast.463, f32[1536,2048]{1,0:T(8,128)S(1)} %fusion.214), kind=kOutput, calls=%fused_computation.407 | convolution fusion | flops 6470762496 | bytes 23068672 | tf_op jit(solution)/shard_map/dot_general | solution.py:334
  350.4 18.5 %fusion.206 = bf16[1536,2048]{1,0:T(8,128)(2,1)} fusion(f32[1536,2048]{1,0:T(8,128)} %copy-done.70, bf16[2048,1024]{1,0:T(8,128)(2,1)S(1)} %bitcast.464, bf16[768,1024]{1,0:T(8,128)(2,1)} %collective-permute-done.12, bf16[768,1024]{1,0:T(8,128)(2,1)} %fusion.211), kind=kOutput, calls=%fused_computation.242 | convolution fusion | flops 6511656960 | bytes 26214400 | tf_op jit(solution)/shard_map/dot_general | solution.py:39
  368.9 9.1 %fusion.272 = f32[1536,1024]{1,0:T(8,128)S(1)} fusion(bf16[1536,2048]{1,0:T(8,128)(2,1)} %fusion.206, bf16[1024,2048]{1,0:T(8,128)(2,1)S(1)} %bitcast.461), kind=kOutput, calls=%fused_computation.420 | convolution fusion | flops 6442450944 | bytes 16777216 | tf_op jit(solution)/shard_map/dot_general | solution.py:39
  379.2 13.2 %convolution_convert_fusion.2 = bf16[2048,1024]{1,0:T(8,128)(2,1)} fusion(bf16[768,1024]{1,0:T(8,128)(2,1)} %collective-permute-done.12, bf16[768,1024]{1,0:T(8,128)(2,1)} %fusion.211, f32[1536,2048]{1,0:T(8,128)} %copy-done.70), kind=kOutput, calls=%fused_computation.261 | convolution fusion | flops 6479151104 | bytes 19922944 | tf_op jit(solution)/shard_map/dot_general | solution.py:29
  416.4 15.3 %collective-permute-done.19 = f32[48,1024]{1,0:T(8,128)S(1)} collective-permute-done((f32[48,1024]{1,0:T(8,128)S(1)}, f32[48,1024]{1,0:T(8,128)S(1)}, u32[]{:S(2)}, u32[]{:S(2)}) %collective-permute-start.19) | collective-permute-done | bytes 196640 | tf_op jit(solution)/shard_map/ppermute | solution.py:60
  436.0 11.8 %convolution_convert_fusion.1 = bf16[1024,2048]{1,0:T(8,128)(2,1)} fusion(bf16[1536,2048]{1,0:T(8,128)(2,1)} %fusion.206, bf16[768,1024]{1,0:T(8,128)(2,1)} %collective-permute-done.10, bf16[768,1024]{1,0:T(8,128)(2,1)} %bitcast.38), kind=kOutput, calls=%fused_computation.260 | convolution fusion | flops 6450839552 | bytes 13631488 | tf_op jit(solution)/shard_map/dot_general | solution.py:29
  447.8 7.9 reshape.540
  455.7 5.7 copy.113
  474.0 6.6 pad_maximum_fusion
  482.5 264.6 %while.29 = (s32[]{:T(128)}, bf16[4,3072,64]{1,2,0:T(8,128)(2,1)}, bf16[4,3072,64]{1,2,0:T(8,128)(2,1)}, bf16[4,3072,64]{1,2,0:T(8,128)(2,1)}, bf16[4,3072,64]{2...) while((s32[]{:T(128)}, bf16[4,3072,64]{1,2,0:T(8,128)(2,1)}, ...), condition=%wide.region_18.19_spmd.clone, body=%wide.region_17.18_spmd.clone.sunk | while | flops 6137972736 | bytes 199488368 | solution.py:194
  508.2 4.5 multiply_convert_fusion.17
  522.4 4.5 multiply_convert_fusion.16
  536.6 4.5 multiply_convert_fusion.15
  554.0 4.5 multiply_convert_fusion.14
  567.5 4.5 multiply_convert_fusion.17
  581.7 4.4 multiply_convert_fusion.16
  595.9 4.4 multiply_convert_fusion.15
  613.2 4.5 multiply_convert_fusion.14
  626.8 4.5 multiply_convert_fusion.17
  640.9 4.4 multiply_convert_fusion.16
  655.1 4.5 multiply_convert_fusion.15
  672.4 4.5 multiply_convert_fusion.14
  685.9 4.5 multiply_convert_fusion.17
  700.1 4.4 multiply_convert_fusion.16
  714.3 4.5 multiply_convert_fusion.15
  731.6 4.5 multiply_convert_fusion.14
  747.1 3.9 pad_maximum_fusion.2
  751.0 9.5 %convolution_convert_fusion.3 = bf16[1024,768]{1,0:T(8,128)(2,1)} fusion(bf16[3072,1024]{1,0:T(8,128)(2,1)} %copy-done.14, bf16[3072,768]{0,1:T(8,128)(2,1)} %pad_maximum_fusion.2), kind=kOutput, calls=%fused_computation.299 | convolution fusion | flops 4832624640 | bytes 12582912 | tf_op jit(solution)/shard_map/dot_general | solution.py:29
  760.5 10.6 %fusion.223 = f32[3072,1024]{1,0:T(8,128)} fusion(bf16[3072,768]{0,1:T(8,128)(2,1)} %pad_maximum_fusion.2, bf16[1024,2304]{1,0:T(8,128)(2,1)} %all-gather.6.cloned.1.call-done), kind=kOutput, calls=%fused_computation.315 | convolution fusion | flops 4831838208 | bytes 18874368 | tf_op jit(solution)/shard_map/dot_general | solution.py:39
  771.2 5.6 convert_element_type.255
  779.9 7.3 fusion.253
  824.5 8.4 collective-permute-done.28
  845.3 4.5 multiply_reduce_fusion.10
  (558 shorter events, 475.8 us)
Async XLA Ops:
  7.2 98.1 %all-gather.6.cloned.1.call-start = ((), (), s32[]{:S(2)}) async-start(), calls=%async_computation.4 | async-start | bytes 5308416 | tf_op jit(solution)/shard_map/all_gather | solution.py:259
  10.7 55.3 %copy-start.43 = (f32[32,1024]{1,0:T(8,128)S(1)}, f32[32,1024]{1,0:T(8,128)}, u32[]{:S(2)}) copy-start(f32[32,1024]{1,0:T(8,128)} %param.28) | copy-start | bytes 393220
  10.8 57.9 %copy-start.67 = (s32[1,12]{1,0:T(1,128)S(1)}, s32[1,12]{1,0:T(1,128)}, u32[]{:S(2)}) copy-start(s32[1,12]{1,0:T(1,128)} %param.26) | copy-start | bytes 148
  24.6 234.4 %all-gather.8.cloned.1.call-start = ((), (), s32[]{:S(2)}) async-start(), calls=%async_computation.7 | async-start | bytes 10027008 | tf_op jit(solution)/shard_map/all_gather | solution.py:281
  24.6 36.1 %collective-permute-start.3 = (bf16[768,1024]{1,0:T(8,128)(2,1)S(1)}, bf16[768,1024]{1,0:T(8,128)(2,1)S(1)}, u32[]{:S(2)}, u32[]{:S(2)}) collective-permute-start(bf16[768,1024]{1,0:T(8,128)(2,1)S(1)} %bitcast.425), channel_id=1, source_target_pairs={{0,2},{2,0},{1,3},{3,1},{4,6},{6,4},{5,7},{7,5},{8,10},{10,8},{9,1... | collective-permute-start | bytes 4718600 | tf_op jit(solution)/shard_map/ppermute | solution.py:60
  25.0 49.7 %collective-permute-start.2 = (bf16[768,1024]{1,0:T(8,128)(2,1)S(1)}, bf16[768,1024]{1,0:T(8,128)(2,1)}, u32[]{:S(2)}, u32[]{:S(2)}) collective-permute-start(bf16[768,1024]{1,0:T(8,128)(2,1)S(1)} %bitcast.426), channel_id=1, source_target_pairs={{0,1},{1,0},{2,3},{3,2},{4,5},{5,4},{6,7},{7,6},{8,9},{9,8},{10,11... | collective-permute-start | bytes 4718600 | tf_op jit(solution)/shard_map/ppermute | solution.py:56
  60.7 56.4 %copy-start.7 = (bf16[768,1024]{1,0:T(8,128)(2,1)}, bf16[768,1024]{1,0:T(8,128)(2,1)S(1)}, u32[]{:S(2)}) copy-start(bf16[768,1024]{1,0:T(8,128)(2,1)S(1)} %collective-permute-done.3) | copy-start | bytes 4718596
  60.8 14.0 %collective-permute-start.4 = (bf16[768,1024]{1,0:T(8,128)(2,1)S(1)}, bf16[768,1024]{1,0:T(8,128)(2,1)}, u32[]{:S(2)}, u32[]{:S(2)}) collective-permute-start(bf16[768,1024]{1,0:T(8,128)(2,1)S(1)} %collective-permute-done.3), channel_id=1, source_target_pairs={{0,1},{1,0},{2,3},{3,2},{4,5},{5,4},{6,7},{7,6},{8,9},{9,8},{10,11... | collective-permute-start | bytes 4718600 | tf_op jit(solution)/shard_map/ppermute | solution.py:56
  65.8 3.8 collective-permute-start.8
  74.5 676.5 %all-gather.10.cloned.1.call-start = ((), (), s32[]{:S(2)}) async-start(), calls=%async_computation.8 | async-start | bytes 2359296 | tf_op jit(solution)/shard_map/all_gather | solution.py:370
  77.9 29.8 %copy-start.39 = (f32[4,12,64]{2,1,0:T(8,128)}, f32[4,12,64]{2,1,0:T(8,128)S(1)}, u32[]{:S(2)}) copy-start(f32[4,12,64]{2,1,0:T(8,128)S(1)} %broadcast_multiply_fusion) | copy-start | bytes 36868
  77.9 27.4 %copy-start.59 = (f32[12,512]{1,0:T(8,128)S(1)}, f32[12,512]{1,0:T(8,128)}, u32[]{:S(2)}) copy-start(f32[12,512]{1,0:T(8,128)} %get-tuple-element.342) | copy-start | bytes 73732
  77.9 27.4 %copy-start.60 = (f32[12,512]{1,0:T(8,128)S(1)}, f32[12,512]{1,0:T(8,128)}, u32[]{:S(2)}) copy-start(f32[12,512]{1,0:T(8,128)} %get-tuple-element.343) | copy-start | bytes 73732
  107.7 1.3 collective-permute-start
  109.0 7.0 collective-permute-start.1
  262.7 10.9 %collective-permute-start.9 = (bf16[16,32,1024]{2,1,0:T(8,128)(2,1)}, bf16[16,32,1024]{2,1,0:T(8,128)(2,1)}, u32[]{:S(2)}, u32[]{:S(2)}) collective-permute-start(bf16[16,32,1024]{2,1,0:T(8,128)(2,1)} %get-tuple-element.315), channel_id=1, source_target_pairs={{0,1},{1,0},{2,3},{3,2},{4,5},{5,4},{6,7},{7,6},{8,9},{9,8},{10,11... | collective-permute-start | bytes 3145736 | tf_op jit(solution)/shard_map/ppermute | solution.py:56
  269.8 7.1 collective-permute-start.5
  270.3 12.2 %collective-permute-start.6 = (bf16[768,256]{1,0:T(8,128)(2,1)}, bf16[768,256]{1,0:T(8,128)(2,1)S(1)}, u32[]{:S(2)}, u32[]{:S(2)}) collective-permute-start(bf16[768,256]{1,0:T(8,128)(2,1)} %copy.104), channel_id=1, source_target_pairs={{0,2},{2,0},{1,3},{3,1},{4,6},{6,4},{5,7},{7,5},{8,10},{10,8},{9,1... | collective-permute-start | bytes 1179656 | tf_op jit(solution)/shard_map/ppermute | solution.py:60
  271.8 17.3 %collective-permute-start.7 = (bf16[768,256]{1,0:T(8,128)(2,1)}, bf16[768,256]{1,0:T(8,128)(2,1)S(1)}, u32[]{:S(2)}, u32[]{:S(2)}) collective-permute-start(bf16[768,256]{1,0:T(8,128)(2,1)} %copy.105), channel_id=1, source_target_pairs={{0,3},{1,2},{2,1},{3,0},{4,7},{5,6},{6,5},{7,4},{8,11},{9,10},{10,... | collective-permute-start | bytes 1179656 | tf_op jit(solution)/shard_map/ppermute | solution.py:64
  298.7 32.7 %collective-permute-start.10 = (bf16[768,1024]{1,0:T(8,128)(2,1)}, bf16[768,1024]{1,0:T(8,128)(2,1)}, u32[]{:S(2)}, u32[]{:S(2)}) collective-permute-start(bf16[768,1024]{1,0:T(8,128)(2,1)} %bitcast.38), channel_id=1, source_target_pairs={{0,1},{1,0},{2,3},{3,2},{4,5},{5,4},{6,7},{7,6},{8,9},{9,8},{10,11... | collective-permute-start | bytes 4718600 | tf_op jit(solution)/shard_map/ppermute | solution.py:56
  306.7 43.7 %collective-permute-start.12 = (bf16[768,1024]{1,0:T(8,128)(2,1)}, bf16[768,1024]{1,0:T(8,128)(2,1)}, u32[]{:S(2)}, u32[]{:S(2)}) collective-permute-start(bf16[768,1024]{1,0:T(8,128)(2,1)} %fusion.211), channel_id=1, source_target_pairs={{0,1},{1,0},{2,3},{3,2},{4,5},{5,4},{6,7},{7,6},{8,9},{9,8},{10,11... | collective-permute-start | bytes 4718600 | tf_op jit(solution)/shard_map/ppermute | solution.py:56
  378.5 19.8 %collective-permute-start.11 = (bf16[768,1024]{1,0:T(8,128)(2,1)S(1)}, bf16[768,1024]{1,0:T(8,128)(2,1)}, u32[]{:S(2)}, u32[]{:S(2)}) collective-permute-start(bf16[768,1024]{1,0:T(8,128)(2,1)S(1)} %slice.316), channel_id=1, source_target_pairs={{0,1},{1,0},{2,3},{3,2},{4,5},{5,4},{6,7},{7,6},{8,9},{9,8},{10,11... | collective-permute-start | bytes 4718600 | tf_op jit(solution)/shard_map/ppermute | solution.py:56
  379.1 13.3 %collective-permute-start.13 = (bf16[768,1024]{1,0:T(8,128)(2,1)S(1)}, bf16[768,1024]{1,0:T(8,128)(2,1)S(1)}, u32[]{:S(2)}, u32[]{:S(2)}) collective-permute-start(bf16[768,1024]{1,0:T(8,128)(2,1)S(1)} %slice.315), channel_id=1, source_target_pairs={{0,1},{1,0},{2,3},{3,2},{4,5},{5,4},{6,7},{7,6},{8,9},{9,8},{10,11... | collective-permute-start | bytes 4718600 | tf_op jit(solution)/shard_map/ppermute | solution.py:56
  404.1 8.3 collective-permute-start.18
  407.6 53.8 %collective-permute-start.16 = (bf16[768,256]{1,0:T(8,128)(2,1)S(1)}, bf16[768,256]{1,0:T(8,128)(2,1)S(1)}, u32[]{:S(2)}, u32[]{:S(2)}) collective-permute-start(bf16[768,256]{1,0:T(8,128)(2,1)S(1)} %get-tuple-element.321), channel_id=1, source_target_pairs={{0,3},{1,2},{2,1},{3,0},{4,7},{5,6},{6,5},{7,4},{8,11},{9,10},{10,... | collective-permute-start | bytes 1179656 | tf_op jit(solution)/shard_map/ppermute | solution.py:64
  409.1 52.2 %collective-permute-start.15 = (bf16[768,256]{1,0:T(8,128)(2,1)S(1)}, bf16[768,256]{1,0:T(8,128)(2,1)S(1)}, u32[]{:S(2)}, u32[]{:S(2)}) collective-permute-start(bf16[768,256]{1,0:T(8,128)(2,1)S(1)} %get-tuple-element.322), channel_id=1, source_target_pairs={{0,2},{2,0},{1,3},{3,1},{4,6},{6,4},{5,7},{7,5},{8,10},{10,8},{9,1... | collective-permute-start | bytes 1179656 | tf_op jit(solution)/shard_map/ppermute | solution.py:60
  409.7 51.7 %collective-permute-start.14 = (bf16[768,256]{1,0:T(8,128)(2,1)S(1)}, bf16[768,256]{1,0:T(8,128)(2,1)S(1)}, u32[]{:S(2)}, u32[]{:S(2)}) collective-permute-start(bf16[768,256]{1,0:T(8,128)(2,1)S(1)} %get-tuple-element.323), channel_id=1, source_target_pairs={{0,1},{1,0},{2,3},{3,2},{4,5},{5,4},{6,7},{7,6},{8,9},{9,8},{10,11... | collective-permute-start | bytes 1179656 | tf_op jit(solution)/shard_map/ppermute | solution.py:56
  412.4 19.3 %copy-start.58 = (f32[12,1024]{1,0:T(8,128)S(1)}, f32[12,1024]{1,0:T(8,128)}, u32[]{:S(2)}) copy-start(f32[12,1024]{1,0:T(8,128)} %fusion.251) | copy-start | bytes 147460
  412.4 19.3 %copy-start.66 = (f32[64]{0:T(128)S(1)}, f32[64]{0:T(128)}, u32[]{:S(2)}) copy-start(f32[64]{0:T(128)} %pad.34.clone) | copy-start | bytes 772
  412.4 19.3 %collective-permute-start.19 = (f32[48,1024]{1,0:T(8,128)S(1)}, f32[48,1024]{1,0:T(8,128)S(1)}, u32[]{:S(2)}, u32[]{:S(2)}) collective-permute-start(f32[48,1024]{1,0:T(8,128)S(1)} %fusion.303), channel_id=1, source_target_pairs={{0,2},{2,0},{1,3},{3,1},{4,6},{6,4},{5,7},{7,5},{8,10},{10,8},{9,1... | collective-permute-start | bytes 589832 | tf_op jit(solution)/shard_map/ppermute | solution.py:60
  432.6 318.4 %reduce-scatter.3.cloned.1.call-start = ((), (), s32[]{:S(2)}) async-start(), calls=%async_computation.5 | async-start | bytes 10027008 | tf_op jit(solution)/shard_map/reduce_scatter | solution.py:361
  436.0 34.1 %collective-permute-start.17 = (bf16[16,32,1024]{2,1,0:T(8,128)(2,1)}, bf16[16,32,1024]{2,1,0:T(8,128)(2,1)}, u32[]{:S(2)}, u32[]{:S(2)}) collective-permute-start(bf16[16,32,1024]{2,1,0:T(8,128)(2,1)} %fusion.226), channel_id=1, source_target_pairs={{0,1},{1,0},{2,3},{3,2},{4,5},{5,4},{6,7},{7,6},{8,9},{9,8},{10,11... | collective-permute-start | bytes 3145736 | tf_op jit(solution)/shard_map/ppermute | solution.py:56
  480.6 360.9 %reduce-scatter.5.cloned.1.call-start = ((), (), s32[]{:S(2)}) async-start(), calls=%async_computation.6 | async-start | bytes 1769472 | tf_op jit(solution)/shard_map/reduce_scatter | solution.py:375
  778.8 20.5 %collective-permute-start.21 = (bf16[12,64,1024]{2,1,0:T(8,128)(2,1)}, bf16[12,64,1024]{2,1,0:T(8,128)(2,1)}, u32[]{:S(2)}, u32[]{:S(2)}) collective-permute-start(bf16[12,64,1024]{2,1,0:T(8,128)(2,1)} %get-tuple-element.317), channel_id=1, source_target_pairs={{0,1},{1,0},{2,3},{3,2},{4,5},{5,4},{6,7},{7,6},{8,9},{9,8},{10,11... | collective-permute-start | bytes 4718600 | tf_op jit(solution)/shard_map/ppermute | solution.py:56
  787.2 1.7 collective-permute-start.24
  788.8 5.1 collective-permute-start.25
  794.0 4.7 collective-permute-start.26
  798.0 56.6 %collective-permute-start.20 = (bf16[12,64,1024]{2,1,0:T(8,128)(2,1)}, bf16[12,64,1024]{2,1,0:T(8,128)(2,1)}, u32[]{:S(2)}, u32[]{:S(2)}) collective-permute-start(bf16[12,64,1024]{2,1,0:T(8,128)(2,1)} %get-tuple-element.316), channel_id=1, source_target_pairs={{0,1},{1,0},{2,3},{3,2},{4,5},{5,4},{6,7},{7,6},{8,9},{9,8},{10,11... | collective-permute-start | bytes 4718600 | tf_op jit(solution)/shard_map/ppermute | solution.py:56
  798.7 6.9 collective-permute-start.27
  802.6 52.1 %collective-permute-start.22 = (bf16[12,64,1024]{2,1,0:T(8,128)(2,1)}, bf16[12,64,1024]{2,1,0:T(8,128)(2,1)}, u32[]{:S(2)}, u32[]{:S(2)}) collective-permute-start(bf16[12,64,1024]{2,1,0:T(8,128)(2,1)} %add_convert_fusion), channel_id=1, source_target_pairs={{0,2},{2,0},{1,3},{3,1},{4,6},{6,4},{5,7},{7,5},{8,10},{10,8},{9,1... | collective-permute-start | bytes 4718600 | tf_op jit(solution)/shard_map/ppermute | solution.py:60
  806.9 26.0 %collective-permute-start.28 = (f32[96,1024]{1,0:T(8,128)S(1)}, f32[96,1024]{1,0:T(8,128)}, u32[]{:S(2)}, u32[]{:S(2)}) collective-permute-start(f32[96,1024]{1,0:T(8,128)S(1)} %maximum_select_fusion.3), channel_id=1, source_target_pairs={{0,16},{4,20},{8,24},{12,28},{16,0},{20,4},{24,8},{28,12},{1,17},{... | collective-permute-start | bytes 1179656 | tf_op jit(solution)/shard_map/ppermute | solution.py:73
  816.0 5.0 collective-permute-start.23
  841.5 9.0 %all-to-all-start.1 = ((bf16[4,32,768]{2,1,0:T(8,128)(2,1)}), bf16[4,32,768]{2,1,0:T(8,128)(2,1)S(1)}, u32[]{:S(2)}, u32[]{:S(2)}) async-start(bf16[4,32,768]{2,1,0:T(8,128)(2,1)} %bitcast.501), calls=%async_computation.3 | async-start | bytes 393216 | tf_op jit(solution)/shard_map/all_to_all | solution.py:390
  854.5 4.0 collective-permute-start.29
  858.5 3.7 collective-permute-start.30
  862.2 5.0 collective-permute-start.31
  867.2 3.7 collective-permute-start.32
  870.9 4.5 collective-permute-start.33
  (72 other events, 374.5 us)
Sparse Core Ops, SparseCore 0:
  24.7 80.5 all-gather.5
  108.6 120.6 all-gather.7
  432.7 47.6 all-gather.9
  485.9 169.8 reduce-scatter.2
  760.7 69.8 reduce-scatter.4

commit v5 on v4

--- a/solution.py
+++ b/solution.py
@@ -120,25 +120,31 @@
     return jnp.arange(rows, dtype=jnp.int32) % local_rows // (local_rows // FRAMES) < count[0]
 
 
+def with_mask(query, key, count, local_rows):
+    rows = key.shape[1]
+    bias = jnp.where(valid_keys(count, rows, local_rows), 0.0, masked_score).astype(jnp.bfloat16)
+    bias = jnp.broadcast_to(bias[None, :, None], (key.shape[0], rows, 1))
+    query = query * jnp.bfloat16(0.125)
+    return (
+        jnp.concatenate([query, jnp.ones_like(bias)], axis=2),
+        jnp.concatenate([key, bias], axis=2),
+    )
+
+
 def attend(count, projected, local_rows):
     rows = projected.shape[0]
-    key_valid = valid_keys(count, rows, local_rows)
     heads = heads_of(projected).reshape(3, BANDS, rows, HEAD_DIM)
 
     def one_head(pieces):
         query, key, value = pieces
 
         def one_block(query_part):
-            scores = jnp.where(
-                key_valid[None, :], contract_cols(query_part, key) * 0.125, masked_score
-            )
+            scores = contract_cols(query_part, key)
             maxima = jnp.max(scores, axis=1, keepdims=True)
-            exponent = jnp.exp(scores - maxima)
-            totals = jnp.sum(exponent, axis=1, keepdims=True)
-            outcome = jnp.dot(
-                exponent.astype(jnp.bfloat16), value, preferred_element_type=jnp.float32
-            )
-            return outcome / totals, (maxima + jnp.log(totals))[:, 0]
+            exponent = jnp.exp(scores - maxima).astype(jnp.bfloat16)
+            outcome = jnp.dot(exponent, value, preferred_element_type=jnp.float32)
+            totals = outcome[:, HEAD_DIM:]
+            return outcome[:, :HEAD_DIM] / totals, (maxima + jnp.log(totals))[:, 0]
 
         parts = []
         for part in jnp.split(query, BANDS):
@@ -147,33 +153,34 @@
             parts.append(one_block(part))
         return jnp.concatenate([part[0] for part in parts]), jnp.stack([part[1] for part in parts])
 
-    outcome, logs = lax.map(one_head, (heads[0], heads[1], heads[2]))
+    query, key = with_mask(heads[0], heads[1], count, local_rows)
+    value = jnp.concatenate([heads[2], jnp.ones_like(heads[2][:, :, :1])], axis=2)
+    outcome, logs = lax.map(one_head, (query, key, value))
     return columns_of(outcome.astype(jnp.bfloat16)), (outcome, logs)
 
 
 def attend_back(count, projected, grad_attended, raw, local_rows):
     rows = projected.shape[0]
-    key_valid = valid_keys(count, rows, local_rows)
     heads = heads_of(projected).reshape(3, BANDS, rows, HEAD_DIM)
     outcome, logs = raw
     grads = heads_of(grad_attended)
     deltas = jnp.sum(outcome * grads.astype(jnp.float32), axis=-1).reshape(logs.shape)
 
     def one_head(pieces):
-        query, key, value, log_head, delta_head, grad = pieces
+        query, masked_query, key, masked_key, value, log_head, delta_head, grad = pieces
 
         def one_block(running, inputs):
             key_sum, value_sum = running
-            query_part, log_part, delta_part, grad_part = inputs
-            scores = jnp.where(
-                key_valid[None, :], contract_cols(query_part, key) * 0.125, masked_score
-            )
-            probability = jnp.exp(scores - log_part[:, None])
-            grad_prob = contract_cols(grad_part, value)
-            grad_scores = (probability * (grad_prob - delta_part[:, None])).astype(jnp.bfloat16)
+            query_part, masked_part, log_part, delta_part, grad_part = inputs
+            scores = contract_cols(masked_part, masked_key)
+            probability = jnp.exp(scores - log_part[:, None]).astype(jnp.bfloat16)
+            probability = lax.optimization_barrier(probability)
+            grad_prob = contract_cols(grad_part, value) - delta_part[:, None]
+            grad_scores = (probability.astype(jnp.float32) * grad_prob).astype(jnp.bfloat16)
+            grad_scores = lax.optimization_barrier(grad_scores)
             grad_query = jnp.dot(grad_scores, key, preferred_element_type=jnp.float32) * 0.125
             key_sum = key_sum + contract_rows(grad_scores, query_part) * 0.125
-            value_sum = value_sum + contract_rows(probability.astype(jnp.bfloat16), grad_part)
+            value_sum = value_sum + contract_rows(probability, grad_part)
             return (key_sum, value_sum), grad_query.astype(jnp.bfloat16)
 
         running = (0.0, 0.0)
@@ -181,7 +188,8 @@
         for place in range(BANDS):
             part = slice(place * local_rows, (place + 1) * local_rows)
             running, grad_part = one_block(
-                running, (query[part], log_head[place], delta_head[place], grad[part])
+                running,
+                (query[part], masked_query[part], log_head[place], delta_head[place], grad[part]),
             )
             grad_query.append(grad_part)
         key_sum, value_sum = running
@@ -191,7 +199,11 @@
             value_sum.astype(jnp.bfloat16),
         )
 
-    results = lax.map(one_head, (*heads, logs, deltas, grads))
+    masked_query, masked_key = with_mask(heads[0], heads[1], count, local_rows)
+    results = lax.map(
+        one_head,
+        (heads[0], masked_query, heads[1], masked_key, heads[2], logs, deltas, grads),
+    )
     return jnp.concatenate([columns_of(result) for result in results], axis=1)
 
 

time: 904 us -> 808 us (0.89)
  other arithmetic: 170 us -> 136 us
  matrix products: 409 us -> 380 us
  loops' own time: 29.2 us -> 2.74 us
  waiting for transfers between devices: 117 us -> 100 us
    reduce_sum x16 -> x0, other arithmetic: 32.9 us -> none  [one_block(): totals = jnp.sum(exponent, axis=1, keepdims=True)]
    another operation x2, loops' own time: 29.2 us -> 2.74 us  [the longest x1 2.14 us: attend_back(): lax.map(one_head, (heads[0], masked_query, heads[1], masked_key, heads[2]...]
    dot_general x52, matrix products: 179 us -> 161 us  [contract_cols(): lax.dot_general(left, right, (((1,), (1,)), ((), ())), preferred_element_...]
    dot_general x37, matrix products: 133 us -> 121 us  [contract_rows(): lax.dot_general(left, right, (((0,), (0,)), ((), ())), precision=precisio...]
    ppermute x8, waiting for transfers between devices: 67.5 us -> 55.9 us  [to_pair(): return lax.ppermute(tensor, 'pair', [(0, 1), (1, 0)])]
    while x24 -> x184, local copies, waits for them, and re-layouts: 0.07 us -> 10 us
  transfers between devices with their start and end apart: 40 -> 40, of which waited for: 16 -> 16; matrix products, arithmetic and copies ran while one was open for 68% -> 72% of each run, Pallas kernels for 0% -> 0%
where the time goes in v5:
time: 808 us; the launch traced here: 800 us
  matrix products  380 us (47%)
  other arithmetic  136 us (17%)
  local copies, waits for them, and re-layouts  121 us (15%)
  waiting for transfers between devices  100 us (12%)
  starting transfers between devices  26.5 us (3%)
  between operations  21.2 us (3%)
  blocking collectives  13.7 us (2%)
    dot_general x52, matrix products, contract_cols(): lax.dot_general(left, right, (((1,), (1,)), ((), ())), preferred_element_...  161 us
    dot_general x37, matrix products, contract_rows(): lax.dot_general(left, right, (((0,), (0,)), ((), ())), precision=precisio...  121 us
    ppermute x8, waiting for transfers between devices, to_pair(): return lax.ppermute(tensor, 'pair', [(0, 1), (1, 0)])  55.9 us
    dot_general x16, matrix products, one_block(): outcome = jnp.dot(exponent, value, preferred_element_type=jnp.float32)  33.1 us
    dot_general x16, matrix products, one_block(): jnp.dot(grad_scores, key, preferred_element_type=jnp.float32) * 0.125  25.1 us
    all_gather x1, waiting for transfers between devices, per_device(): lax.all_gather(w_first.reshape(BANDS * own_rows, 9 * OWN_COLS), 'clip', t...  23.2 us
  transfers between devices with their start and end apart: 40, of which 16 were waited for; matrix products, arithmetic and copies ran while one was open for 72% of the time, Pallas kernels for 0%

profile of v5, /device:TPU:0, one launch (start us, length us, event | category | flops | bytes accessed | tf_op | source)
XLA Modules:
  0.0 800.3 jit_solution(11295374441576964463)
XLA Ops:
  10.8 13.7 %all_to_all.10 = bf16[4,32,2304]{2,1,0:T(8,128)(2,1)} all-to-all(bf16[4,32,2304]{2,1,0:T(8,128)(2,1)S(1)} %copy.99), channel_id=1, replica_groups=mesh['clip'=8,'pair'=2,'half'=2] {'pair','half'}, dimensions={0} | all-to-all | bytes 1179648 | tf_op jit(solution)/shard_map/all_to_all | solution.py:270
  25.0 35.7 %collective-permute-done.3 = bf16[768,1024]{1,0:T(8,128)(2,1)S(1)} collective-permute-done((bf16[768,1024]{1,0:T(8,128)(2,1)S(1)}, bf16[768,1024]{1,0:T(8,128)(2,1)S(1)}, u32[]{:S(2)}, u32[]{:S(2)}) %collective-permute-start.3) | collective-permute-done | bytes 1572896 | tf_op jit(solution)/shard_map/ppermute | solution.py:60
  75.1 3.1 convert_reduce_fusion
  78.3 3.8 multiply_reduce_fusion.1
  82.1 23.2 %all-gather.6.cloned.1.call-done = bf16[1024,2304]{1,0:T(8,128)(2,1)} async-done(((bf16[128,2304]{1,0:T(8,128)(2,1)}), bf16[1024,2304]{1,0:T(8,128)(2,1)}) %all-gather.6.cloned.1.call-update) | async-done | bytes 4718608 | tf_op jit(solution)/shard_map/all_gather | solution.py:271
  110.6 5.5 collective-permute-done.1
  117.2 6.6 fusion.111
  123.8 9.4 %convolution_convert_fusion = bf16[3072,768]{0,1:T(8,128)(2,1)} fusion(bf16[3072,1024]{1,0:T(8,128)(2,1)S(1)} %fusion.111, bf16[1024,2304]{1,0:T(8,128)(2,1)} %all-gather.6.cloned.1.call-done), kind=kOutput, calls=%fused_computation.187 | convolution fusion | flops 4834197504 | bytes 12582912 | tf_op jit(solution)/shard_map/dot_general | solution.py:305
  133.2 9.6 %copy.101 = bf16[3072,12,64]{2,0,1:T(8,128)(2,1)} copy(bf16[3072,12,64]{0,2,1:T(8,128)(2,1)} %bitcast.497) | data formatting | bytes 9437184 | tf_op jit(solution)/shard_map/reshape | solution.py:112
  142.8 5.6 fusion.180
  155.6 73.3 %while.26 = (s32[]{:T(128)}, f32[4,3072,64]{1,2,0:T(8,128)}, f32[4,4,768]{2,1,0:T(4,128)S(1)}, bf16[4,3072,65]{2,1,0:T(8,128)(2,1)}, bf16[4,3072,65]{2,1,0:T(8,1...) while((s32[]{:T(128)}, f32[4,3072,64]{1,2,0:T(8,128)}, ...), condition=%wide.region_7.8_spmd, body=%wide.region_2.7_spmd.sunk | while | flops 2482775040 | bytes 93642960 | solution.py:158
  229.3 3.5 slice_bitcast_fusion.4
  245.5 6.2 collective-permute-done.6
  251.7 6.6 collective-permute-done.7
  258.4 5.8 fusion.174
  281.5 6.5 fusion.181
  288.0 8.6 %copy.110 = bf16[16,2,32,2,1024]{4,3,2,1,0:T(2,128)(2,1)} copy(bf16[16,2,32,2,1024]{4,2,3,1,0:T(8,128)(2,1)} %bitcast.487) | data formatting | bytes 8388608 | tf_op jit(solution)/shard_map/transpose | solution.py:299
  296.6 3.6 copy.136
  300.2 11.6 %fusion.118 = f32[1536,2048]{1,0:T(8,128)} fusion(bf16[1024,2048]{1,0:T(8,128)(2,1)S(1)} %bitcast.498, bf16[768,1024]{1,0:T(8,128)(2,1)} %collective-permute-done.10, bf16[768,1024]{1,0:T(8,128)(2,1)} %bitcast.65), kind=kOutput, calls=%fused_computation.230 | convolution fusion | flops 6448742400 | bytes 19922944 | tf_op jit(solution)/shard_map/dot_general | solution.py:323
  311.8 10.2 %fusion.163 = f32[1536,1024]{1,0:T(8,128)S(1)} fusion(bf16[2048,1024]{1,0:T(8,128)(2,1)S(1)} %bitcast.501, f32[1536,2048]{1,0:T(8,128)} %fusion.118), kind=kOutput, calls=%fused_computation.355 | convolution fusion | flops 6470762496 | bytes 23068672 | tf_op jit(solution)/shard_map/dot_general | solution.py:346
  326.6 18.6 %fusion.110 = bf16[1536,2048]{1,0:T(8,128)(2,1)} fusion(f32[1536,2048]{1,0:T(8,128)} %fusion.118, bf16[2048,1024]{1,0:T(8,128)(2,1)S(1)} %bitcast.502, bf16[768,1024]{1,0:T(8,128)(2,1)} %collective-permute-done.12, bf16[768,1024]{1,0:T(8,128)(2,1)} %fusion.115), kind=kOutput, calls=%fused_computation.173 | convolution fusion | flops 6511656960 | bytes 26214400 | tf_op jit(solution)/shard_map/dot_general | solution.py:39
  345.2 8.8 %fusion.187 = f32[1536,1024]{1,0:T(8,128)S(1)} fusion(bf16[1536,2048]{1,0:T(8,128)(2,1)} %fusion.110, bf16[1024,2048]{1,0:T(8,128)(2,1)S(1)} %bitcast.499), kind=kOutput, calls=%fused_computation.372 | convolution fusion | flops 6442450944 | bytes 16777216 | tf_op jit(solution)/shard_map/dot_general | solution.py:39
  354.4 13.4 %convolution_convert_fusion.2 = bf16[2048,1024]{1,0:T(8,128)(2,1)} fusion(bf16[768,1024]{1,0:T(8,128)(2,1)} %collective-permute-done.12, bf16[768,1024]{1,0:T(8,128)(2,1)} %fusion.115, f32[1536,2048]{1,0:T(8,128)} %fusion.118), kind=kOutput, calls=%fused_computation.192 | convolution fusion | flops 6479151104 | bytes 19922944 | tf_op jit(solution)/shard_map/dot_general | solution.py:29
  373.1 3.3 slice_add_fusion.1
  388.8 3.5 collective-permute-done.19
  395.3 11.8 %convolution_convert_fusion.1 = bf16[1024,2048]{1,0:T(8,128)(2,1)} fusion(bf16[1536,2048]{1,0:T(8,128)(2,1)} %fusion.110, bf16[768,1024]{1,0:T(8,128)(2,1)} %collective-permute-done.10, bf16[768,1024]{1,0:T(8,128)(2,1)} %bitcast.65), kind=kOutput, calls=%fused_computation.191 | convolution fusion | flops 6450839552 | bytes 13631488 | tf_op jit(solution)/shard_map/dot_general | solution.py:29
  407.0 7.9 reshape.535
  414.9 5.6 copy.113
  424.5 3.3 fusion.116
  428.3 6.5 pad_maximum_fusion
  436.7 215.1 %while.27 = (s32[]{:T(128)}, bf16[4,3072,64]{1,2,0:T(8,128)(2,1)}, bf16[4,3072,64]{1,2,0:T(8,128)(2,1)}, bf16[4,3072,64]{1,2,0:T(8,128)(2,1)}, bf16[4,3072,65]{2...) while((s32[]{:T(128)}, bf16[4,3072,64]{1,2,0:T(8,128)(2,1)}, ...), condition=%wide.region_14.15_spmd, body=%wide.region_13.14_spmd.sunk | while | flops 6119030784 | bytes 350448032 | solution.py:203
  460.0 3.1 multiply_convert_fusion.15
  504.8 3.1 multiply_convert_fusion.16
  513.6 3.1 multiply_convert_fusion.15
  567.3 3.1 multiply_convert_fusion.15
  620.9 3.1 multiply_convert_fusion.15
  651.8 4.0 pad_maximum_fusion.2
  655.8 9.5 %convolution_convert_fusion.3 = bf16[1024,768]{1,0:T(8,128)(2,1)} fusion(bf16[3072,1024]{1,0:T(8,128)(2,1)} %copy-done.27, bf16[3072,768]{0,1:T(8,128)(2,1)} %pad_maximum_fusion.2), kind=kOutput, calls=%fused_computation.231 | convolution fusion | flops 4832624640 | bytes 12582912 | tf_op jit(solution)/shard_map/dot_general | solution.py:29
  665.3 10.7 %fusion.127 = f32[3072,1024]{1,0:T(8,128)} fusion(bf16[3072,768]{0,1:T(8,128)(2,1)} %pad_maximum_fusion.2, bf16[1024,2304]{1,0:T(8,128)(2,1)} %all-gather.6.cloned.1.call-done), kind=kOutput, calls=%fused_computation.248 | convolution fusion | flops 4831838208 | bytes 18874368 | tf_op jit(solution)/shard_map/dot_general | solution.py:39
  676.0 5.6 convert_element_type.276
  684.7 7.3 fusion.164
  699.8 3.5 fusion.179
  704.6 3.3 add_convert_fusion
  733.4 4.4 collective-permute-done.28
  746.5 3.7 all-to-all-start.1
  750.2 4.5 multiply_reduce_fusion.10
  759.6 3.9 multiply_reduce_fusion.2
  771.9 3.6 collective-permute-done.32
  (736 shorter events, 435.7 us)
Async XLA Ops:
  7.2 98.1 %all-gather.6.cloned.1.call-start = ((), (), s32[]{:S(2)}) async-start(), calls=%async_computation.4 | async-start | bytes 5308416 | tf_op jit(solution)/shard_map/all_gather | solution.py:271
  8.9 15.7 %copy-start.15 = (bf16[1,768,1024]{2,1,0:T(8,128)(2,1)S(1)}, bf16[1,768,1024]{2,1,0:T(8,128)(2,1)}, u32[]{:S(2)}) copy-start(bf16[1,768,1024]{2,1,0:T(8,128)(2,1)} %param.23) | copy-start | bytes 4718596
  10.7 54.7 %copy-start.76 = (s32[1,12]{1,0:T(1,128)S(1)}, s32[1,12]{1,0:T(1,128)}, u32[]{:S(2)}) copy-start(s32[1,12]{1,0:T(1,128)} %param.26) | copy-start | bytes 148
  24.5 204.7 %all-gather.8.cloned.1.call-start = ((), (), s32[]{:S(2)}) async-start(), calls=%async_computation.7 | async-start | bytes 10027008 | tf_op jit(solution)/shard_map/all_gather | solution.py:293
  24.6 36.1 %collective-permute-start.3 = (bf16[768,1024]{1,0:T(8,128)(2,1)S(1)}, bf16[768,1024]{1,0:T(8,128)(2,1)S(1)}, u32[]{:S(2)}, u32[]{:S(2)}) collective-permute-start(bf16[768,1024]{1,0:T(8,128)(2,1)S(1)} %bitcast.463), channel_id=1, source_target_pairs={{0,2},{2,0},{1,3},{3,1},{4,6},{6,4},{5,7},{7,5},{8,10},{10,8},{9,1... | collective-permute-start | bytes 4718600 | tf_op jit(solution)/shard_map/ppermute | solution.py:60
  25.0 50.1 %collective-permute-start.2 = (bf16[768,1024]{1,0:T(8,128)(2,1)S(1)}, bf16[768,1024]{1,0:T(8,128)(2,1)}, u32[]{:S(2)}, u32[]{:S(2)}) collective-permute-start(bf16[768,1024]{1,0:T(8,128)(2,1)S(1)} %bitcast.464), channel_id=1, source_target_pairs={{0,1},{1,0},{2,3},{3,2},{4,5},{5,4},{6,7},{7,6},{8,9},{9,8},{10,11... | collective-permute-start | bytes 4718600 | tf_op jit(solution)/shard_map/ppermute | solution.py:56
  60.7 56.4 %copy-start.22 = (bf16[768,1024]{1,0:T(8,128)(2,1)}, bf16[768,1024]{1,0:T(8,128)(2,1)S(1)}, u32[]{:S(2)}) copy-start(bf16[768,1024]{1,0:T(8,128)(2,1)S(1)} %collective-permute-done.3) | copy-start | bytes 4718596
  60.7 14.4 %collective-permute-start.4 = (bf16[768,1024]{1,0:T(8,128)(2,1)S(1)}, bf16[768,1024]{1,0:T(8,128)(2,1)}, u32[]{:S(2)}, u32[]{:S(2)}) collective-permute-start(bf16[768,1024]{1,0:T(8,128)(2,1)S(1)} %collective-permute-done.3), channel_id=1, source_target_pairs={{0,1},{1,0},{2,3},{3,2},{4,5},{5,4},{6,7},{7,6},{8,9},{9,8},{10,11... | collective-permute-start | bytes 4718600 | tf_op jit(solution)/shard_map/ppermute | solution.py:56
  65.2 4.4 collective-permute-start.8
  74.5 581.2 %all-gather.10.cloned.1.call-start = ((), (), s32[]{:S(2)}) async-start(), calls=%async_computation.8 | async-start | bytes 2359296 | tf_op jit(solution)/shard_map/all_gather | solution.py:382
  78.3 29.5 %copy-start.52 = (f32[4,12,64]{2,1,0:T(8,128)}, f32[4,12,64]{2,1,0:T(8,128)S(1)}, u32[]{:S(2)}) copy-start(f32[4,12,64]{2,1,0:T(8,128)S(1)} %broadcast_multiply_fusion.1) | copy-start | bytes 36868
  78.3 27.0 %copy-start.68 = (f32[12,512]{1,0:T(8,128)S(1)}, f32[12,512]{1,0:T(8,128)}, u32[]{:S(2)}) copy-start(f32[12,512]{1,0:T(8,128)} %get-tuple-element.303) | copy-start | bytes 73732
  78.3 27.0 %copy-start.69 = (f32[12,512]{1,0:T(8,128)S(1)}, f32[12,512]{1,0:T(8,128)}, u32[]{:S(2)}) copy-start(f32[12,512]{1,0:T(8,128)} %get-tuple-element.304) | copy-start | bytes 73732
  107.7 1.3 collective-permute-start
  107.7 16.0 %copy-start.62 = (f32[4,12,64]{2,1,0:T(8,128)}, f32[4,12,64]{2,1,0:T(8,128)S(1)}, u32[]{:S(2)}) copy-start(f32[4,12,64]{2,1,0:T(8,128)S(1)} %add_rsqrt_fusion) | copy-start | bytes 36868
  109.0 7.0 collective-permute-start.1
  232.8 9.4 %collective-permute-start.9 = (bf16[16,32,1024]{2,1,0:T(8,128)(2,1)}, bf16[16,32,1024]{2,1,0:T(8,128)(2,1)}, u32[]{:S(2)}, u32[]{:S(2)}) collective-permute-start(bf16[16,32,1024]{2,1,0:T(8,128)(2,1)} %get-tuple-element.276), channel_id=1, source_target_pairs={{0,1},{1,0},{2,3},{3,2},{4,5},{5,4},{6,7},{7,6},{8,9},{9,8},{10,11... | collective-permute-start | bytes 3145736 | tf_op jit(solution)/shard_map/ppermute | solution.py:56
  239.0 6.5 collective-permute-start.5
  239.7 12.0 %collective-permute-start.6 = (bf16[768,256]{1,0:T(8,128)(2,1)S(1)}, bf16[768,256]{1,0:T(8,128)(2,1)S(1)}, u32[]{:S(2)}, u32[]{:S(2)}) collective-permute-start(bf16[768,256]{1,0:T(8,128)(2,1)S(1)} %copy.104), channel_id=1, source_target_pairs={{0,2},{2,0},{1,3},{3,1},{4,6},{6,4},{5,7},{7,5},{8,10},{10,8},{9,1... | collective-permute-start | bytes 1179656 | tf_op jit(solution)/shard_map/ppermute | solution.py:60
  242.2 16.2 %collective-permute-start.7 = (bf16[768,256]{1,0:T(8,128)(2,1)}, bf16[768,256]{1,0:T(8,128)(2,1)S(1)}, u32[]{:S(2)}, u32[]{:S(2)}) collective-permute-start(bf16[768,256]{1,0:T(8,128)(2,1)} %copy.105), channel_id=1, source_target_pairs={{0,3},{1,2},{2,1},{3,0},{4,7},{5,6},{6,5},{7,4},{8,11},{9,10},{10,... | collective-permute-start | bytes 1179656 | tf_op jit(solution)/shard_map/ppermute | solution.py:64
  245.5 18.8 %copy-start.35 = (bf16[2,2,256,1024]{3,2,1,0:T(8,128)(2,1)}, bf16[2,2,256,1024]{3,2,1,0:T(8,128)(2,1)S(1)}, u32[]{:S(2)}) copy-start(bf16[2,2,256,1024]{3,2,1,0:T(8,128)(2,1)S(1)} %reverse_select_fusion.2) | copy-start | bytes 6291460
  267.3 32.9 %collective-permute-start.10 = (bf16[768,1024]{1,0:T(8,128)(2,1)}, bf16[768,1024]{1,0:T(8,128)(2,1)}, u32[]{:S(2)}, u32[]{:S(2)}) collective-permute-start(bf16[768,1024]{1,0:T(8,128)(2,1)} %bitcast.65), channel_id=1, source_target_pairs={{0,1},{1,0},{2,3},{3,2},{4,5},{5,4},{6,7},{7,6},{8,9},{9,8},{10,11... | collective-permute-start | bytes 4718600 | tf_op jit(solution)/shard_map/ppermute | solution.py:56
  275.3 51.3 %collective-permute-start.12 = (bf16[768,1024]{1,0:T(8,128)(2,1)}, bf16[768,1024]{1,0:T(8,128)(2,1)}, u32[]{:S(2)}, u32[]{:S(2)}) collective-permute-start(bf16[768,1024]{1,0:T(8,128)(2,1)} %fusion.115), channel_id=1, source_target_pairs={{0,1},{1,0},{2,3},{3,2},{4,5},{5,4},{6,7},{7,6},{8,9},{9,8},{10,11... | collective-permute-start | bytes 4718600 | tf_op jit(solution)/shard_map/ppermute | solution.py:56
  326.1 47.0 %collective-permute-start.11 = (bf16[768,1024]{1,0:T(8,128)(2,1)}, bf16[768,1024]{1,0:T(8,128)(2,1)}, u32[]{:S(2)}, u32[]{:S(2)}) collective-permute-start(bf16[768,1024]{1,0:T(8,128)(2,1)} %slice.366), channel_id=1, source_target_pairs={{0,1},{1,0},{2,3},{3,2},{4,5},{5,4},{6,7},{7,6},{8,9},{9,8},{10,11... | collective-permute-start | bytes 4718600 | tf_op jit(solution)/shard_map/ppermute | solution.py:56
  354.3 13.5 %collective-permute-start.13 = (bf16[768,1024]{1,0:T(8,128)(2,1)S(1)}, bf16[768,1024]{1,0:T(8,128)(2,1)S(1)}, u32[]{:S(2)}, u32[]{:S(2)}) collective-permute-start(bf16[768,1024]{1,0:T(8,128)(2,1)S(1)} %slice.365), channel_id=1, source_target_pairs={{0,1},{1,0},{2,3},{3,2},{4,5},{5,4},{6,7},{7,6},{8,9},{9,8},{10,11... | collective-permute-start | bytes 4718600 | tf_op jit(solution)/shard_map/ppermute | solution.py:56
  378.8 6.5 collective-permute-start.18
  384.9 39.7 %collective-permute-start.17 = (bf16[16,32,1024]{2,1,0:T(8,128)(2,1)}, bf16[16,32,1024]{2,1,0:T(8,128)(2,1)}, u32[]{:S(2)}, u32[]{:S(2)}) collective-permute-start(bf16[16,32,1024]{2,1,0:T(8,128)(2,1)} %fusion.130), channel_id=1, source_target_pairs={{0,1},{1,0},{2,3},{3,2},{4,5},{5,4},{6,7},{7,6},{8,9},{9,8},{10,11... | collective-permute-start | bytes 3145736 | tf_op jit(solution)/shard_map/ppermute | solution.py:56
  385.4 6.9 collective-permute-start.19
  393.1 262.6 %reduce-scatter.3.cloned.1.call-start = ((), (), s32[]{:S(2)}) async-start(), calls=%async_computation.5 | async-start | bytes 10027008 | tf_op jit(solution)/shard_map/reduce_scatter | solution.py:373
  393.3 27.2 %collective-permute-start.14 = (bf16[768,256]{1,0:T(8,128)(2,1)S(1)}, bf16[768,256]{1,0:T(8,128)(2,1)S(1)}, u32[]{:S(2)}, u32[]{:S(2)}) collective-permute-start(bf16[768,256]{1,0:T(8,128)(2,1)S(1)} %get-tuple-element.284), channel_id=1, source_target_pairs={{0,1},{1,0},{2,3},{3,2},{4,5},{5,4},{6,7},{7,6},{8,9},{9,8},{10,11... | collective-permute-start | bytes 1179656 | tf_op jit(solution)/shard_map/ppermute | solution.py:56
  393.4 27.1 %collective-permute-start.15 = (bf16[768,256]{1,0:T(8,128)(2,1)S(1)}, bf16[768,256]{1,0:T(8,128)(2,1)S(1)}, u32[]{:S(2)}, u32[]{:S(2)}) collective-permute-start(bf16[768,256]{1,0:T(8,128)(2,1)S(1)} %get-tuple-element.283), channel_id=1, source_target_pairs={{0,2},{2,0},{1,3},{3,1},{4,6},{6,4},{5,7},{7,5},{8,10},{10,8},{9,1... | collective-permute-start | bytes 1179656 | tf_op jit(solution)/shard_map/ppermute | solution.py:60
  395.0 25.5 %collective-permute-start.16 = (bf16[768,256]{1,0:T(8,128)(2,1)S(1)}, bf16[768,256]{1,0:T(8,128)(2,1)S(1)}, u32[]{:S(2)}, u32[]{:S(2)}) collective-permute-start(bf16[768,256]{1,0:T(8,128)(2,1)S(1)} %get-tuple-element.282), channel_id=1, source_target_pairs={{0,3},{1,2},{2,1},{3,0},{4,7},{5,6},{6,5},{7,4},{8,11},{9,10},{10,... | collective-permute-start | bytes 1179656 | tf_op jit(solution)/shard_map/ppermute | solution.py:64
  434.9 311.6 %reduce-scatter.5.cloned.1.call-start = ((), (), s32[]{:S(2)}) async-start(), calls=%async_computation.6 | async-start | bytes 1769472 | tf_op jit(solution)/shard_map/reduce_scatter | solution.py:387
  683.6 20.9 %collective-permute-start.21 = (bf16[12,64,1024]{2,1,0:T(8,128)(2,1)}, bf16[12,64,1024]{2,1,0:T(8,128)(2,1)}, u32[]{:S(2)}, u32[]{:S(2)}) collective-permute-start(bf16[12,64,1024]{2,1,0:T(8,128)(2,1)} %get-tuple-element.278), channel_id=1, source_target_pairs={{0,1},{1,0},{2,3},{3,2},{4,5},{5,4},{6,7},{7,6},{8,9},{9,8},{10,11... | collective-permute-start | bytes 4718600 | tf_op jit(solution)/shard_map/ppermute | solution.py:56
  692.0 1.5 collective-permute-start.24
  693.5 5.1 collective-permute-start.25
  698.6 4.7 collective-permute-start.26
  703.3 56.3 %collective-permute-start.20 = (bf16[12,64,1024]{2,1,0:T(8,128)(2,1)}, bf16[12,64,1024]{2,1,0:T(8,128)(2,1)}, u32[]{:S(2)}, u32[]{:S(2)}) collective-permute-start(bf16[12,64,1024]{2,1,0:T(8,128)(2,1)} %get-tuple-element.277), channel_id=1, source_target_pairs={{0,1},{1,0},{2,3},{3,2},{4,5},{5,4},{6,7},{7,6},{8,9},{9,8},{10,11... | collective-permute-start | bytes 4718600 | tf_op jit(solution)/shard_map/ppermute | solution.py:56
  703.4 7.5 collective-permute-start.27
  707.8 51.7 %collective-permute-start.22 = (bf16[12,64,1024]{2,1,0:T(8,128)(2,1)}, bf16[12,64,1024]{2,1,0:T(8,128)(2,1)}, u32[]{:S(2)}, u32[]{:S(2)}) collective-permute-start(bf16[12,64,1024]{2,1,0:T(8,128)(2,1)} %add_convert_fusion), channel_id=1, source_target_pairs={{0,2},{2,0},{1,3},{3,1},{4,6},{6,4},{5,7},{7,5},{8,10},{10,8},{9,1... | collective-permute-start | bytes 4718600 | tf_op jit(solution)/shard_map/ppermute | solution.py:60
  712.1 25.7 %collective-permute-start.28 = (f32[96,1024]{1,0:T(8,128)S(1)}, f32[96,1024]{1,0:T(8,128)}, u32[]{:S(2)}, u32[]{:S(2)}) collective-permute-start(f32[96,1024]{1,0:T(8,128)S(1)} %maximum_select_fusion.3), channel_id=1, source_target_pairs={{0,16},{4,20},{8,24},{12,28},{16,0},{20,4},{24,8},{28,12},{1,17},{... | collective-permute-start | bytes 1179656 | tf_op jit(solution)/shard_map/ppermute | solution.py:73
  723.4 6.5 collective-permute-start.23
  746.5 9.0 %all-to-all-start.1 = ((bf16[4,32,768]{2,1,0:T(8,128)(2,1)}), bf16[4,32,768]{2,1,0:T(8,128)(2,1)S(1)}, u32[]{:S(2)}, u32[]{:S(2)}) async-start(bf16[4,32,768]{2,1,0:T(8,128)(2,1)} %bitcast.541), calls=%async_computation.3 | async-start | bytes 393216 | tf_op jit(solution)/shard_map/all_to_all | solution.py:402
  759.5 4.0 collective-permute-start.29
  763.5 3.7 collective-permute-start.30
  767.2 4.6 collective-permute-start.31
  771.8 3.7 collective-permute-start.32
  775.5 4.5 collective-permute-start.33
  (152 other events, 643.6 us)
Sparse Core Ops, SparseCore 0:
  24.7 80.5 all-gather.5
  108.7 120.5 all-gather.7
  393.3 47.7 all-gather.9
  446.6 169.6 reduce-scatter.2
  665.5 73.2 reduce-scatter.4
